TPU v7x, 32 devices: a whole 2x2x4 slice. The times are simulated.
32 devices in a mesh: dp: 8 (over y, x, core), expert: 4 (over z).
Axes of the slice: x: 2, y: 2, z: 4, core: 2. Of those that a mesh axis runs over, the one named last changes fastest.
Arguments:
- tokens: bfloat16 [4096, 1024], P(('dp', 'expert')), may hold values from -6 to 6
- first_gain: bfloat16 [1024], P(('dp', 'expert')), may hold values from 0.5 to 1.5
- w_qkv: bfloat16 [1024, 3072], P(('dp', 'expert')), may hold values from -0.1875 to 0.1875
- w_out: bfloat16 [1024, 1024], P(('dp', 'expert')), may hold values from -1 to 1
- second_gain: bfloat16 [1024], P(('dp', 'expert')), may hold values from 0.5 to 1.5
- w_mix: bfloat16 [1024, 2], P(('dp', 'expert')), may hold values from -0.1875 to 0.1875
- w_up: bfloat16 [1024, 4096], P(('dp', 'expert')), may hold values from -0.1875 to 0.1875
- w_down: bfloat16 [4096, 1024], P(('dp', 'expert')), may hold values from -0.1875 to 0.1875
- expert_up: bfloat16 [4, 1024, 4096], P('expert', 'dp'), may hold values from -0.1875 to 0.1875
- expert_down: bfloat16 [4, 4096, 1024], P('expert', 'dp'), may hold values from -0.1875 to 0.1875
- expert_ids: int32 [4096, 1], P(('dp', 'expert')), may hold values from 0 to 3; in each aligned block of 128 rows (0 to 127, 128 to 255, ...) at most 40 rows name the same one
- doc_lengths: int32 [8, 2], P('dp'), may hold values from 64 to 448, as said below
- out_grad: bfloat16 [4096, 1024], P(('dp', 'expert')), may hold values from -6 to 6
Outputs:
- output: bfloat16 [4096, 1024], P(('dp', 'expert'))
- tokens_grad: bfloat16 [4096, 1024], P(('dp', 'expert'))
- first_gain_grad: float32 [1024], P(('dp', 'expert'))
- w_qkv_grad: float32 [1024, 3072], P(('dp', 'expert'))
- w_out_grad: float32 [1024, 1024], P(('dp', 'expert'))
- second_gain_grad: float32 [1024], P(('dp', 'expert'))
- w_mix_grad: float32 [1024, 2], P(('dp', 'expert'))
- w_up_grad: float32 [1024, 4096], P(('dp', 'expert'))
- w_down_grad: float32 [4096, 1024], P(('dp', 'expert'))
- expert_up_grad: float32 [4, 1024, 4096], P('expert', 'dp')
- expert_down_grad: float32 [4, 4096, 1024], P('expert', 'dp')
Inputs may be any that keep to these rules, and one draw needn't show every extreme that they name: `expert_ids`: in each device's 128 rows no expert is chosen more than 40 times, a bound that some block reaches in some of them. `doc_lengths`: the two lengths of a group sum to 512; the longer is exactly 448 and stands first or second.
All inputs are finite; a program needn't handle non-finite values.
Results may differ from a plain program's by a relative error of at most 0.015.
Values may be sent and summed in bfloat16 or wider, within the bound.
No kernel may reach another device: no remote copies, remote signals or barrier semaphores. Data moves between devices by JAX's collectives and lax.ppermute only.
A program may use at most 256 MiB of HBM per device.

v0:
```python
import jax
import jax.numpy as jnp
from jax import lax
from jax.experimental import pallas as pl
from jax.experimental.pallas import tpu as pltpu
from jax.sharding import Mesh
from jax.sharding import PartitionSpec as P

HEAD_DIM = 64
EPSILON = 1e-05
SCORE_SCALE = 0.125
MASK_VALUE = -1e30
F32 = jnp.float32
BF16 = jnp.bfloat16
DP = ("chip", "core")
LANES = 128
PAD = 16
TANH_SCALE = 0.7978845608028654
TANH_CUBE = 0.044715
VMEM_LIMIT = 60 << 20
FLOPS_US = 1.15e9
LAST = 0


def dot(left, right):
    return jnp.dot(left, right, preferred_element_type=F32)


def dot_rt(left, right):
    return lax.dot_general(left, right, (((1,), (1,)), ((), ())), preferred_element_type=F32)


def dot_lt(left, right):
    return lax.dot_general(left, right, (((0,), (0,)), ((), ())), preferred_element_type=F32)


def norm_parts(values):
    row_mean = jnp.mean(values, axis=-1, keepdims=True)
    centred = values - row_mean
    spread = jnp.mean(centred * centred, axis=-1, keepdims=True)
    inverse = lax.rsqrt(spread + EPSILON)
    return (centred * inverse, inverse)


def norm_back(grad, normed, inverse, gain):
    scaled = grad * gain
    return inverse * (
        scaled
        - jnp.mean(scaled, axis=-1, keepdims=True)
        - normed * jnp.mean(scaled * normed, axis=-1, keepdims=True)
    )


def after(values, *earlier):
    return lax.optimization_barrier((values,) + earlier)[0]


def swap(values, axis):
    return lax.all_to_all(values, axis, split_axis=0, concat_axis=0, tiled=True)


def share(values, axis):
    copies = lax.axis_size(axis)
    return swap(jnp.broadcast_to(values[None], (copies,) + values.shape), axis)


def turn(values, step):
    count = lax.axis_size("expert")
    return lax.ppermute(values, "expert", [(i, (i + step) % count) for i in range(count)])


def turn_all(pieces):
    return [pieces[0]] + [turn(piece, k) for k, piece in enumerate(pieces) if k]


def other_core(values):
    return lax.ppermute(values, "core", [(0, 1), (1, 0)])


def by_core(core, first, second):
    return (jnp.where(core == 0, first, second), jnp.where(core == 0, second, first))


def flip(values, bit):
    chips = range(lax.axis_size("chip"))
    return lax.ppermute(values, "chip", [(i, i ^ bit) for i in chips])


def by_bit(bit, first, second):
    return by_core(lax.axis_index("chip") & bit, first, second)


def chip_bits():
    bits = []
    while 1 << len(bits) < lax.axis_size("chip"):
        bits.append(1 << len(bits))
    return bits


def gather_small(values, axes, copies):
    count, cols = values.shape
    step = min(count, max(16, ((1 << 20) - 1) // (2 * copies * cols) // 16 * 16))
    return [
        lax.all_gather(values[k : k + step], axes, axis=0, tiled=True).reshape(copies, -1, cols)
        for k in range(0, count, step)
    ]


def sum_core(values, core):
    own, sent = by_core(core, values[:, 0], values[:, 1])
    return own.astype(F32) + other_core(sent).astype(F32)


class Fold:
    def __init__(self, pair):
        bits = chip_bits()
        self.orders = [list(bits), list(bits[::-1])]
        self.left = [sorted(bits, reverse=True) for k in range(2)]
        self.pair = [v.reshape((2,) * len(bits) + v.shape[1:]) for v in pair]

    def send(self):
        self.keeps, self.gots = ([], [])
        for k in range(2):
            bit = self.orders[k].pop(0)
            at = self.left[k].index(bit)
            self.left[k].remove(bit)
            low, high = (lax.index_in_dim(self.pair[k], side, at, False) for side in (0, 1))
            keep, sent = by_bit(bit, low, high)
            self.keeps.append(keep)
            self.gots.append(flip(sent.astype(BF16), bit))

    def meet(self, *others):
        gots = lax.optimization_barrier((*self.gots, *others))
        self.pair = [
            keep.astype(F32) + got.astype(F32)
            for keep, got in zip(self.keeps, gots[:2], strict=True)
        ]
        return gots[2:]


def whole(shape):
    return pl.BlockSpec(shape, lambda *at: (0,) * len(shape), pipeline_mode=pl.Buffered(1))


def by_rows(tile, cols):
    return pl.BlockSpec((tile, cols), lambda t: (t, 0))


def shape_of(shape, kind):
    return jax.ShapeDtypeStruct(shape, kind)


def call(body, weight, out_shape, operands, in_specs, out_specs, grid=(1,), scratch=()):
    return pl.pallas_call(
        body,
        grid=grid,
        in_specs=in_specs,
        out_specs=out_specs,
        out_shape=out_shape,
        scratch_shapes=list(scratch),
        compiler_params=pltpu.CompilerParams(vmem_limit_bytes=VMEM_LIMIT),
        cost_estimate=pl.CostEstimate(
            flops=int(weight * FLOPS_US), bytes_accessed=0, transcendentals=0
        ),
    )(*operands)


def enter_body(x_ref, gain_ref, *refs):
    parts, (qkv_ref, attn_ref, w_ref) = (refs[:-3], refs[-3:])
    width, cols = w_ref.shape
    copies = parts[0].shape[0]
    matrix = jnp.concatenate([p[...] for p in parts], axis=1)[:, : width // copies]
    matrix = matrix.reshape(width, cols)
    w_ref[...] = matrix
    normed, unused = norm_parts(x_ref[...].astype(F32))
    attn_input = (normed * gain_ref[...]).astype(BF16)
    attn_ref[...] = attn_input
    qkv_ref[...] = dot(attn_input, matrix).astype(BF16)


def enter(inputs, gain, parts):
    group, width = inputs.shape
    cols = parts[0].shape[2]
    tile = min(512, group)
    return call(
        enter_body,
        0,
        [
            shape_of((group, cols), BF16),
            shape_of((group, width), BF16),
            shape_of((width, cols), BF16),
        ],
        [inputs, gain] + parts,
        [by_rows(tile, width), whole(gain.shape)] + [whole(p.shape) for p in parts],
        [by_rows(tile, cols), by_rows(tile, width), whole((width, cols))],
        grid=(group // tile,),
    )


def seen(split, query_axis, shape, first_query):
    query = first_query + lax.broadcasted_iota(jnp.int32, shape, query_axis)
    key = lax.broadcasted_iota(jnp.int32, shape, 1 - query_axis)
    return (query >= key) & ((query >= split) == (key >= split))


def attend_body(split_ref, q_ref, k_ref, v_ref, out_ref):
    tile, cols = q_ref.shape
    allowed = seen(split_ref[0], 0, (tile, k_ref.shape[0]), pl.program_id(1) * tile)
    for h in range(cols // HEAD_DIM):
        at = slice(h * HEAD_DIM, (h + 1) * HEAD_DIM)
        scores = dot_rt(q_ref[:, at], k_ref[:, at]) * SCORE_SCALE
        scores = jnp.where(allowed, scores, MASK_VALUE)
        weights = jnp.exp(scores - jnp.max(scores, axis=1, keepdims=True))
        probs = weights * (1.0 / jnp.sum(weights, axis=1, keepdims=True))
        out_ref[:, at] = dot(probs.astype(BF16), v_ref[:, at]).astype(BF16)


def attend_back_body(
    split_ref, q_ref, k_ref, v_ref, grad_ref, dq_ref, dk_ref, dv_ref, dk_sum, dv_sum
):
    tile, cols = q_ref.shape
    step = pl.program_id(1)
    allowed = seen(split_ref[0], 1, (k_ref.shape[0], tile), step * tile)
    for h in range(cols // HEAD_DIM):
        at = slice(h * HEAD_DIM, (h + 1) * HEAD_DIM)
        query, keys, vals, grad = (r[:, at] for r in (q_ref, k_ref, v_ref, grad_ref))
        scores = jnp.where(allowed, dot_rt(keys, query) * SCORE_SCALE, MASK_VALUE)
        weights = jnp.exp(scores - jnp.max(scores, axis=0, keepdims=True))
        probs = weights * (1.0 / jnp.sum(weights, axis=0, keepdims=True))
        dprobs = dot_rt(vals, grad)
        delta = jnp.sum(probs * dprobs, axis=0, keepdims=True)
        dscores = (probs * (dprobs - delta)).astype(BF16)
        dq_ref[:, at] = (dot_lt(dscores, keys) * SCORE_SCALE).astype(BF16)
        dk_new = dot(dscores, query) * SCORE_SCALE
        dv_new = dot(probs.astype(BF16), grad)

        @pl.when(step == 0)
        def first():
            dk_sum[:, at] = dk_new
            dv_sum[:, at] = dv_new

        @pl.when(step > 0)
        def later():
            dk_sum[:, at] += dk_new
            dv_sum[:, at] += dv_new

    @pl.when(step == pl.num_programs(1) - 1)
    def last():
        dk_ref[...] = dk_sum[...].astype(BF16)
        dv_ref[...] = dv_sum[...].astype(BF16)


def attention_parts(qkv, head_cols):
    group = qkv.shape[0]
    cols = min(LANES, head_cols)
    pairs = head_cols // cols
    tile = min(512, group)
    if head_cols % LANES == 0:
        operands, shift = ([qkv] * 3, pairs)
    else:
        operands = [qkv[:, k * head_cols : (k + 1) * head_cols] for k in range(3)]
        shift = 0
    specs = [
        pl.BlockSpec(memory_space=pltpu.SMEM),
        pl.BlockSpec((tile, cols), lambda p, t: (t, p)),
        pl.BlockSpec((group, cols), lambda p, t: (0, shift + p)),
        pl.BlockSpec((group, cols), lambda p, t: (0, 2 * shift + p)),
    ]
    by_tile = pl.BlockSpec((tile, cols), lambda p, t: (t, p))
    by_pair = pl.BlockSpec((group, cols), lambda p, t: (0, p))
    return (operands, specs, by_tile, by_pair, (pairs, group // tile), cols)


def attend(qkv, split, head_cols):
    group = qkv.shape[0]
    operands, specs, by_tile, unused, grid, cols = attention_parts(qkv, head_cols)
    return call(
        attend_body,
        0,
        [shape_of((group, head_cols), BF16)],
        [split] + operands,
        specs,
        [by_tile],
        grid=grid,
    )[0]


def attend_back(qkv, grad, split, head_cols):
    group = qkv.shape[0]
    operands, specs, by_tile, by_pair, grid, cols = attention_parts(qkv, head_cols)
    return call(
        attend_back_body,
        20,
        [shape_of((group, head_cols), BF16)] * 3,
        [split] + operands + [grad],
        specs + [by_tile],
        [by_tile, by_pair, by_pair],
        grid=grid,
        scratch=[pltpu.VMEM((group, cols), F32)] * 2,
    )


def middle_body(att_ref, x_ref, w_ref, gain_ref, mix_ref, middle_ref, ffn_ref, coeff_ref):
    n_exp, unused, head_cols = att_ref.shape
    middle = x_ref[...].astype(F32)
    for j in range(n_exp):
        middle = middle + dot(att_ref[j], w_ref[j * head_cols : (j + 1) * head_cols])
    middle_ref[...] = middle
    normed, unused = norm_parts(middle)
    ffn_input = (normed * gain_ref[...]).astype(BF16)
    ffn_ref[...] = ffn_input
    logits = dot_rt(ffn_input, mix_ref[...])
    first, second = (logits[:, 0:1], logits[:, 1:2])
    top = jnp.maximum(first, second)
    first, second = (jnp.exp(first - top), jnp.exp(second - top))
    coeff_ref[...] = jnp.concatenate([first, second], axis=1) / (first + second)


def to_middle(attended, inputs, matrix, gain, mix):
    n_exp, group, head_cols = attended.shape
    width = matrix.shape[0]
    tile = min(512, group)
    return call(
        middle_body,
        0,
        [shape_of((group, width), F32), shape_of((group, width), BF16), shape_of((group, 2), F32)],
        [attended, inputs, matrix, gain, mix],
        [
            pl.BlockSpec((n_exp, tile, head_cols), lambda t: (0, t, 0)),
            by_rows(tile, width),
            whole(matrix.shape),
            whole(gain.shape),
            whole(mix.shape),
        ],
        [by_rows(tile, width), by_rows(tile, width), by_rows(tile, 2)],
        grid=(group // tile,),
    )


def pick_body(slot_ref, ffn_ref, grad_ref, coeff_ref, out_ref):
    capacity = out_ref.shape[1]
    shape = (capacity, ffn_ref.shape[0])
    pick = (lax.broadcasted_iota(jnp.int32, shape, 0) == slot_ref[...]).astype(F32).astype(BF16)
    dexpert = (coeff_ref[:, 1:2] * grad_ref[...].astype(F32)).astype(BF16)
    out_ref[0] = dot(pick, ffn_ref[...]).astype(BF16)
    out_ref[1] = dot(pick, dexpert).astype(BF16)


def pick_rows(slot, ffn_input, grad, coeffs, capacity):
    group, width = ffn_input.shape
    operands = [slot.reshape(1, group), ffn_input, grad, coeffs]
    return call(
        pick_body,
        0,
        [shape_of((2, capacity, width), BF16)],
        operands,
        [whole(o.shape) for o in operands],
        [whole((2, capacity, width))],
    )[0]


def bend(pre):
    square = pre * pre
    bent = jnp.tanh(TANH_SCALE * pre * (1.0 + TANH_CUBE * square))
    half = 0.5 * (1.0 + bent)
    slope = half + 0.5 * pre * (1.0 - bent * bent) * TANH_SCALE * (1.0 + 3.0 * TANH_CUBE * square)
    return ((pre * half).astype(BF16), slope)


def add_step(total, new):
    @pl.when(pl.program_id(0) == 0)
    def first():
        total[...] = new

    @pl.when(pl.program_id(0) > 0)
    def later():
        total[...] += new


def hidden_back(rows_in, rows_grad, up, down, din_sum):
    act, slope = bend(dot(rows_in, up))
    dpre = (slope * dot_rt(rows_grad, down)).astype(BF16)
    add_step(din_sum, dot_rt(dpre, up))
    return (act, dpre)


def fill_rows(own_ref, got_ref, rows_in, rows_grad):
    capacity = own_ref.shape[1]

    @pl.when(pl.program_id(0) == 0)
    def begin():
        rows_in[:capacity] = own_ref[0]
        rows_in[capacity:] = got_ref[0]
        rows_grad[:capacity] = own_ref[1]
        rows_grad[capacity:] = got_ref[1]


def expert_body(
    own_ref,
    got_ref,
    up_ref,
    down_ref,
    keep_ref,
    send_ref,
    act_ref,
    dpre_ref,
    rows_in,
    rows_grad,
    outs,
    dins,
):
    width = own_ref.shape[2]
    capacity = own_ref.shape[1]
    fill_rows(own_ref, got_ref, rows_in, rows_grad)
    up = up_ref[...].reshape(width, -1)
    act, dpre_ref[...] = hidden_back(rows_in[...], rows_grad[...], up, down_ref[0], dins)
    add_step(outs, dot(act, down_ref[0]))
    act_ref[...] = act

    @pl.when(pl.program_id(0) == pl.num_programs(0) - 1)
    def last():
        for k, total in enumerate((outs, dins)):
            keep_ref[k] = total[:capacity]
            send_ref[k] = total[capacity:].astype(BF16)


def expert_grad_body(own_ref, got_ref, act_ref, dpre_ref, grads_ref, turned, rows_grad):
    n_chip, packed, width = grads_ref.shape
    cols = act_ref.shape[1]
    per = width // cols
    pair_rows = width // n_chip
    chunk = pl.program_id(0)
    capacity = own_ref.shape[1]

    @pl.when(chunk == 0)
    def begin():
        rows_in = jnp.concatenate([own_ref[0], got_ref[0]], axis=0)
        turned[...] = jnp.transpose(rows_in.astype(F32)).astype(BF16)
        rows_grad[:capacity] = own_ref[1]
        rows_grad[capacity:] = got_ref[1]

    dup = dot(turned[...], dpre_ref[...]).astype(BF16)
    ddown = dot_lt(act_ref[...], rows_grad[...]).astype(BF16)
    low = pl.multiple_of(chunk // per * pair_rows, pair_rows)
    left = pl.multiple_of(chunk % per * cols, cols)
    grads_ref[:, pl.ds(low, pair_rows), pl.ds(left, cols)] = dup.reshape(n_chip, pair_rows, cols)
    grads_ref[pl.ds(chunk, 1), packed - cols :, :] = ddown[None]


def expert_ffn(own, got, up, down, pair_rows):
    unused, capacity, width = own.shape
    n_chip, exp_cols, unused = down.shape
    per = width // exp_cols
    count = 2 * capacity
    hidden = n_chip * exp_cols
    by_cols = pl.BlockSpec((count, exp_cols), lambda c: (0, c))
    return call(
        expert_body,
        0,
        [
            shape_of(own.shape, F32),
            shape_of(own.shape, BF16),
            shape_of((count, hidden), BF16),
            shape_of((count, hidden), BF16),
        ],
        [own, got, up, down],
        [
            whole(own.shape),
            whole(own.shape),
            pl.BlockSpec((n_chip, pair_rows, exp_cols), lambda c: (0, c // per, c % per)),
            pl.BlockSpec((1, exp_cols, width), lambda c: (c, 0, 0)),
        ],
        [whole(own.shape), whole(own.shape), by_cols, by_cols],
        grid=(n_chip,),
        scratch=[pltpu.VMEM((count, width), BF16)] * 2 + [pltpu.VMEM((count, width), F32)] * 2,
    )


def expert_grad(own, got, act, dpre, n_chip):
    unused, capacity, width = own.shape
    count, hidden = act.shape
    cols = hidden // n_chip
    packed = (n_chip, hidden // n_chip + hidden // n_chip, width)
    by_cols = pl.BlockSpec((count, cols), lambda c: (0, c))
    return call(
        expert_grad_body,
        0,
        [shape_of(packed, BF16)],
        [own, got, act, dpre],
        [whole(own.shape), whole(own.shape), by_cols, by_cols],
        [whole(packed)],
        grid=(n_chip,),
        scratch=[pltpu.VMEM((width, count), BF16), pltpu.VMEM((count, width), BF16)],
    )[0]


def dense_body(ex_ref, x_ref, g_ref, coeff_ref, up_ref, down_ref, *refs):
    outs, (pay_ref, act_ref, dpre_ref, ddense_ref, dense, dins) = (refs[:-6], refs[-6:])
    n_exp, padded, width = pay_ref.shape
    rows = padded - PAD

    @pl.when(pl.program_id(0) == 0)
    def begin():
        ddense_ref[...] = (coeff_ref[:, 0:1] * g_ref[...].astype(F32)).astype(BF16)

    up = up_ref[...].reshape(width, -1)
    down = down_ref[...].reshape(-1, width)
    act, dpre_ref[...] = hidden_back(x_ref[...], ddense_ref[...], up, down, dins)
    act_ref[...] = act
    add_step(dense, dot(act, down))

    @pl.when(pl.program_id(0) == pl.num_programs(0) - 1)
    def last():
        for k, out_ref in enumerate(outs):
            to = lax.rem(ex_ref[0] + k, len(outs))
            at = pl.ds(pl.multiple_of(to * rows, rows), rows)
            out_ref[...] = (coeff_ref[at, 0:1] * dense[at]).astype(BF16)
        for j in range(n_exp):
            at = slice(j * rows, (j + 1) * rows)
            pay_ref[j, :rows] = dins[at].astype(BF16)
            sums = jnp.sum(g_ref[at].astype(F32) * dense[at], axis=1, keepdims=True)
            line = jnp.transpose(sums * jnp.ones((1, LANES), F32))[:PAD]
            high = line.astype(BF16).astype(F32)
            index = lax.broadcasted_iota(jnp.int32, (PAD, rows), 0)
            extra = jnp.where(index == 0, high, jnp.where(index == 1, line - high, 0.0))
            pay_ref[j, rows:] = jnp.concatenate(
                [extra, jnp.zeros((PAD, width - rows), F32)], axis=1
            ).astype(BF16)


def dense_grad_body(x_ref, g_ref, act_ref, dpre_ref, dup_ref, ddown_ref):
    dup_ref[...] = dot_lt(x_ref[...], dpre_ref[...]).astype(BF16)
    ddown_ref[...] = dot_lt(act_ref[...], g_ref[...]).astype(BF16)


def dense_ffn(ex, ffn_input, grad, coeffs, weights, specs, hidden, rows):
    group, width = ffn_input.shape
    step = 2 * LANES
    count = group // rows
    operands = [ffn_input, grad, coeffs]
    padded = (count, rows + PAD, width)
    by_cols = pl.BlockSpec((group, step), lambda c: (0, c))
    return call(
        dense_body,
        0,
        [shape_of((rows, width), BF16)] * count
        + [shape_of(padded, BF16)]
        + [shape_of((group, hidden), BF16)] * 2
        + [shape_of((group, width), BF16)],
        [ex] + operands + weights,
        [pl.BlockSpec(memory_space=pltpu.SMEM)] + [whole(o.shape) for o in operands] + specs,
        [whole((rows, width))] * count
        + [whole(padded), by_cols, by_cols, whole((group, width))],
        grid=(hidden // step,),
        scratch=[pltpu.VMEM((group, width), F32)] * 2,
    )


def dense_grad(ffn_input, ddense, act, dpre):
    group, width = ffn_input.shape
    hidden = act.shape[1]
    step = 2 * LANES
    by_cols = pl.BlockSpec((group, step), lambda c: (0, c))
    return call(
        dense_grad_body,
        0,
        [shape_of((width, hidden), BF16), shape_of((hidden, width), BF16)],
        [ffn_input, ddense, act, dpre],
        [whole(ffn_input.shape), whole(ddense.shape), by_cols, by_cols],
        [
            pl.BlockSpec((width, step), lambda c: (0, c)),
            pl.BlockSpec((step, width), lambda c: (c, 0)),
        ],
        grid=(hidden // step,),
    )


def middle_back_body(
    ex_ref, pay_ref, slot_ref, middle_ref, coeff_ref, g_ref, gain_ref, mix_ref, w_ref, *refs
):
    rets, (dmid_ref, low_ref, datt_ref, small_ref, base_ref) = (refs[:-5], refs[-5:])
    rows, width = middle_ref.shape
    n_exp = pay_ref.shape[0]
    head_cols = datt_ref.shape[2]
    total = pay_ref[0].astype(F32)
    for j in range(1, n_exp):
        total = total + pay_ref[j].astype(F32)
    capacity = rets[0].shape[1]
    exp_rows, exp_din = (jnp.zeros((rows, width), F32) for k in range(2))
    index = lax.broadcasted_iota(jnp.int32, (rows, capacity), 1)
    for k, ret_ref in enumerate(rets):
        source = lax.rem(ex_ref[0] + n_exp - k, n_exp)
        place = (index + source * capacity == slot_ref[...]).astype(F32).astype(BF16)
        exp_rows = exp_rows + dot(place, ret_ref[0])
        exp_din = exp_din + dot(place, ret_ref[1])
    dffn = total[:rows] + exp_din
    lines = jnp.concatenate([total[rows:, :rows], jnp.zeros((rows - PAD, rows), F32)], axis=0)
    lines = jnp.transpose(lines)
    grad = g_ref[...].astype(F32)
    dcoeff = [lines[:, 0:1] + lines[:, 1:2], jnp.sum(grad * exp_rows, axis=1, keepdims=True)]
    coeff = [coeff_ref[:, k : k + 1] for k in range(2)]
    base_ref[...] = middle_ref[...] + coeff[1] * exp_rows
    inner = coeff[0] * dcoeff[0] + coeff[1] * dcoeff[1]
    dlogit = [(c * (d - inner)).astype(BF16).astype(F32) for c, d in zip(coeff, dcoeff, strict=True)]
    mix = mix_ref[...].astype(F32)
    dffn = dffn + dlogit[0] * mix[0:1] + dlogit[1] * mix[1:2]
    normed, inverse = norm_parts(middle_ref[...])
    gain = gain_ref[...]
    dmiddle = grad + norm_back(dffn, normed, inverse, gain)
    dmid_ref[...] = dmiddle
    low = dmiddle.astype(BF16)
    low_ref[...] = low
    datt = dot_rt(low, w_ref[...]).astype(BF16)
    for j in range(n_exp):
        datt_ref[j] = datt[:, j * head_cols : (j + 1) * head_cols]
    lane = lax.broadcasted_iota(jnp.int32, (rows, LANES), 1)
    pair = jnp.where(lane == 0, dlogit[0], jnp.where(lane == 1, dlogit[1], 0.0)).astype(BF16)
    dmix = dot_lt(pair, (normed * gain).astype(BF16))
    dgain = jnp.sum(dffn * normed, axis=0, keepdims=True)
    nothing = jnp.zeros((1, width), F32)
    small_ref[...] = jnp.concatenate([nothing, dgain, dmix[:2], jnp.zeros((4, width), F32)], axis=0)


def middle_back(ex, arrived, returned, slot, middle, coeffs, grad, gain, mix, matrix, head_cols):
    rows, width = middle.shape
    n_exp = arrived.shape[0]
    operands = [arrived, slot, middle, coeffs, grad, gain, mix, matrix] + list(returned)
    shapes = [
        shape_of((rows, width), F32),
        shape_of((rows, width), BF16),
        shape_of((n_exp, rows, head_cols), BF16),
        shape_of((8, width), F32),
        shape_of((rows, width), F32),
    ]
    return call(
        middle_back_body,
        0,
        shapes,
        [ex] + operands,
        [pl.BlockSpec(memory_space=pltpu.SMEM)] + [whole(o.shape) for o in operands],
        [whole(o.shape) for o in shapes],
    )


def out_grad_body(att_ref, low_ref, grad_ref):
    n_exp, unused, head_cols = att_ref.shape
    for j in range(n_exp):
        grad_ref[j * head_cols : (j + 1) * head_cols] = dot_lt(att_ref[j], low_ref[...]).astype(BF16)


def attn_input_back_body(ex_ref, dq_ref, dk_ref, dv_ref, w_ref, x_ref, *refs):
    pays, (small_ref,) = (refs[:-1], refs[-1:])
    rows, width = pays[0].shape
    dgain = jnp.zeros((1, width), F32)
    for k, pay_ref in enumerate(pays):
        to = lax.rem(ex_ref[0] + k, len(pays))
        at = pl.ds(pl.multiple_of(to * rows, rows), rows)
        grads = jnp.concatenate([dq_ref[at], dk_ref[at], dv_ref[at]], axis=1)
        dattn = dot_rt(grads, w_ref[...])
        pay_ref[...] = dattn.astype(BF16)
        normed, unused = norm_parts(x_ref[at].astype(F32))
        dgain = dgain + jnp.sum(dattn * normed, axis=0, keepdims=True)
    small_ref[...] = jnp.concatenate([dgain, jnp.zeros((7, width), F32)], axis=0)


def attn_input_back(ex, dparts, matrix, inputs, rows):
    group, width = inputs.shape
    head_cols = dparts[0].shape[1]
    operands = list(dparts) + [matrix, inputs]
    shapes = [shape_of((rows, width), BF16)] * (group // rows) + [shape_of((8, width), F32)]
    return call(
        attn_input_back_body,
        0,
        shapes,
        [ex] + operands,
        [pl.BlockSpec(memory_space=pltpu.SMEM)] + [whole(o.shape) for o in operands],
        [whole(o.shape) for o in shapes],
    )


def qkv_grad_body(x_ref, dq_ref, dk_ref, dv_ref, grad_ref):
    rows_in = x_ref[...]
    grad_ref[...] = jnp.concatenate(
        [dot_lt(rows_in, r[...]).astype(BF16) for r in (dq_ref, dk_ref, dv_ref)], axis=1
    )


def leave_body(x_ref, gain_ref, dmid_ref, *refs):
    pays, out_ref = (refs[:-1], refs[-1])
    dattn = pays[0][...].astype(F32)
    for pay_ref in pays[1:]:
        dattn = dattn + pay_ref[...].astype(F32)
    normed, inverse = norm_parts(x_ref[...].astype(F32))
    out_ref[...] = (dmid_ref[...] + norm_back(dattn, normed, inverse, gain_ref[...])).astype(BF16)


def simple(body, weight, shape, operands):
    return call(
        body,
        weight,
        [shape],
        operands,
        [whole(o.shape) for o in operands],
        [whole(shape.shape)],
    )[0]


def shards(
    tokens,
    first_gain,
    w_qkv,
    w_out,
    second_gain,
    w_mix,
    w_up,
    w_down,
    expert_up,
    expert_down,
    expert_ids,
    doc_lengths,
    out_grad,
):
    rows, width = tokens.shape
    n_chip, n_core, n_exp = (lax.axis_size(a) for a in ("chip", "core", "expert"))
    n_dp = n_chip * n_core
    group = rows * n_exp
    head_cols = width // n_exp
    qkv_cols = 3 * head_cols
    w_rows = w_qkv.shape[0]
    block = n_exp * w_rows
    dense_rows = w_down.shape[0]
    dense_cols = n_dp * dense_rows
    exp_rows = expert_up.shape[1]
    exp_cols = expert_down.shape[1]
    ex = lax.axis_index("expert")
    ex_line = jnp.full((1,), ex, jnp.int32)
    core = lax.axis_index("core")
    share_cap = max(2, 5 * rows // (4 * n_exp))
    capacity = n_exp * share_cap
    bits = chip_bits()

    exp_split = (
        expert_up[0]
        .reshape(exp_rows, n_chip, n_core, exp_cols)
        .transpose(2, 0, 1, 3)
        .reshape(n_core, exp_rows, n_chip * exp_cols)
    )
    own_half, sent_half = by_core(core, exp_split[0], exp_split[1])
    chip_up = jnp.concatenate(by_core(core, own_half, other_core(sent_half)), axis=0)
    pair_rows = n_core * exp_rows
    n_block = n_chip * exp_cols // width
    up_rows = n_block * pair_rows
    chip_up = chip_up.reshape(pair_rows, n_block, width).transpose(1, 0, 2)
    down_all = lax.all_gather(expert_down[0], "chip", axis=0, tiled=True)
    down_all = down_all.reshape(n_chip, exp_cols, width)

    qkv_blocks = w_qkv.reshape(w_rows, 3, n_exp, head_cols).transpose(2, 0, 1, 3)
    small = jnp.stack([first_gain, second_gain, w_mix[:, 0], w_mix[:, 1]])
    small = jnp.concatenate(
        [
            jnp.pad(small, ((0, w_rows - 4), (0, LANES - w_rows))),
            jnp.pad(expert_ids[:, 0].astype(BF16)[None], ((0, w_rows - 1), (0, LANES - rows))),
        ],
        axis=1,
    )
    up_blocks = w_up.reshape(w_rows, n_dp, n_exp, dense_rows).transpose(2, 0, 1, 3)
    others = jnp.concatenate([w_out, small], axis=1)
    dealt = swap(
        jnp.concatenate(
            [
                qkv_blocks.reshape(n_exp, w_rows, qkv_cols),
                up_blocks.reshape(n_exp, w_rows, dense_cols),
                jnp.broadcast_to(others[None], (n_exp,) + others.shape),
            ],
            axis=2,
        ),
        "expert",
    )
    at = [qkv_cols, qkv_cols + dense_cols, qkv_cols + dense_cols + width]
    up_own = dealt[:, :, at[0] : at[1]].reshape(block, dense_cols)
    out_own = dealt[:, :, at[1] : at[2]].reshape(block, width)
    choice = after(dealt[:, 0, at[2] + LANES : at[2] + LANES + rows].astype(F32)).astype(jnp.int32)
    small = dealt[:, :4, at[2] : at[2] + w_rows].transpose(1, 0, 2).reshape(4, block)
    first_own = jnp.concatenate(
        [
            dealt[:, :, :qkv_cols].reshape(block, qkv_cols),
            jnp.pad(small, ((0, 4), (0, qkv_cols - block))),
        ]
    )
    group_tokens = share(after(tokens, dealt), "expert")
    first_parts = gather_small(first_own, DP, n_dp)
    small = first_parts[-1][:, -8:-4, :block].transpose(1, 0, 2).reshape(4, width)
    gain_one = small[0:1].astype(F32)
    gain_two = small[1:2].astype(F32)
    mix_rows = jnp.pad(small[2:4], ((0, PAD - 2), (0, 0)))

    group_tokens = after(group_tokens, first_parts, gain_one)
    inputs = group_tokens.reshape(group, width)
    step = 2 * LANES
    if dense_cols == width and dense_rows == block:
        dense_pack = after(jnp.concatenate([out_own, up_own, w_down], axis=0), inputs, down_all)
        dense_all = lax.all_gather(dense_pack, DP, axis=0, tiled=True)
        dense_all = dense_all.reshape(n_dp, 3, block, width)
        out_matrix = dense_all[:, 0].reshape(width, width)
        up_matrix = down_matrix = dense_all
        up_spec = pl.BlockSpec((n_dp, 1, block, step), lambda c: (0, 1, 0, c))
        down_spec = pl.BlockSpec((step // block, 1, block, width), lambda c: (c, 2, 0, 0))
    else:
        out_matrix, up_matrix, down_matrix = (
            lax.all_gather(w, DP, axis=0, tiled=True) for w in (out_own, up_own, w_down)
        )
        up_spec = pl.BlockSpec((width, step), lambda c: (0, c))
        down_spec = pl.BlockSpec((step, width), lambda c: (c, 0))
    chip_up = after(chip_up.reshape(up_rows, width), inputs)
    up_all = lax.all_gather(chip_up, "chip", axis=0, tiled=True)
    up_all = up_all.reshape(n_chip, up_rows, width)

    grad_all = share(after(out_grad, inputs), "expert").reshape(group, width)

    qkv, attn_input, qkv_matrix = enter(inputs, gain_one, first_parts)
    doc_split = doc_lengths[0, :1]
    attended_own = attend(qkv, doc_split, head_cols)
    attended_own, grad_all = lax.optimization_barrier((attended_own, grad_all))
    attended_all = share(attended_own, "expert")
    same = (choice[:, :, None] == choice[:, None, :]).astype(jnp.int32)
    earlier = jnp.arange(rows)[None, None, :] < jnp.arange(rows)[None, :, None]
    rank = jnp.sum(jnp.where(earlier, same, 0), axis=2)
    first_slot = jnp.arange(n_exp, dtype=jnp.int32)[:, None] * share_cap
    slot = jnp.where(choice == ex, first_slot + rank, -1).reshape(1, group)
    slot_own = lax.dynamic_slice_in_dim(choice * share_cap + rank, ex, 1, 0).reshape(rows, 1)
    slot, slot_own = lax.optimization_barrier((slot, slot_own))
    attended_all = after(attended_all, out_matrix, slot)
    middle, ffn_input, coeffs = to_middle(attended_all, inputs, out_matrix, gain_two, mix_rows)


    weights, specs = ([up_matrix, down_matrix], [up_spec, down_spec])
    *out_parts, payload, dense_act, dense_dpre, ddense = dense_ffn(
        ex_line, ffn_input, grad_all, coeffs, weights, specs, dense_cols, rows
    )
    arrived = swap(payload, "expert")
    own_rows = pick_rows(slot, ffn_input, grad_all, coeffs, capacity)
    own_rows = after(own_rows, payload)
    up_part, down_part = dense_grad(ffn_input, ddense, dense_act, dense_dpre)
    got_rows, up_part, down_part = lax.optimization_barrier(
        (other_core(own_rows), up_part, down_part)
    )
    exp_keep, exp_send, exp_act, exp_dpre = expert_ffn(
        own_rows, got_rows, up_all, down_all, pair_rows
    )
    exp_back = other_core(exp_send)
    returned = []
    for k in range(n_exp):
        low = lax.rem(ex + k, n_exp) * share_cap
        piece = [lax.dynamic_slice_in_dim(v, low, share_cap, 1) for v in (exp_keep, exp_back)]
        returned.append((piece[0] + piece[1].astype(F32)).astype(BF16))
    exp_grads = expert_grad(own_rows, got_rows, exp_act, exp_dpre, n_chip)
    arrived, exp_grads, *returned = lax.optimization_barrier((arrived, exp_grads, *returned))
    returned = turn_all(returned)
    exp_sum = lax.psum_scatter(
        exp_grads.reshape(-1, width), "chip", scatter_dimension=0, tiled=True
    )

    def mine(values, size=rows):
        return lax.dynamic_slice_in_dim(values, ex * size, size, 0)

    middle_own, coeffs_own = (mine(middle), mine(coeffs))
    att_own = lax.dynamic_slice_in_dim(attended_all, ex * rows, rows, 1)
    up_core = sum_core(up_part.reshape(n_chip, n_core, block, dense_cols), core)
    down_core = sum_core(down_part.reshape(n_chip, n_core, dense_rows, width), core)
    returned[0] = after(returned[0], middle_own, coeffs_own, att_own, up_core, down_core)
    dense_fold = Fold((up_core, down_core))
    dense_fold.send()
    dmiddle, dmid_low, datt, small_two, out_base = middle_back(
        ex_line,
        arrived,
        returned,
        slot_own,
        middle_own,
        coeffs_own,
        out_grad,
        gain_two,
        mix_rows,
        out_matrix,
        head_cols,
    )
    dattended = swap(datt, "expert")
    dattended = dattended.reshape(group, head_cols)
    (dattended,) = dense_fold.meet(dattended)
    out_sums = turn_all([after(piece, dattended) for piece in out_parts])

    dparts = attend_back(qkv, dattended, doc_split, head_cols)
    *dattn_parts, small_one = attn_input_back(ex_line, dparts, qkv_matrix, inputs, rows)
    while dense_fold.orders[0]:
        dense_fold.send()
        met = dense_fold.meet(*dattn_parts, *out_sums)
        dattn_parts, out_sums = (met[:n_exp], met[n_exp:])
    up_sum, down_sum = dense_fold.pair
    dattn = turn_all(dattn_parts)
    out_weight = simple(
        out_grad_body,
        0,
        shape_of((width, width), BF16),
        [after(att_own, dparts[0]), dmid_low],
    )
    out_core = sum_core(out_weight.reshape(n_chip, n_core, block, width), core)
    qkv_part = simple(
        qkv_grad_body,
        20,
        shape_of((width, qkv_cols), BF16),
        [after(attn_input, dattn_parts[0])] + list(dparts),
    )
    small_sum = (small_one + small_two).astype(BF16).reshape(8, n_dp, block).transpose(1, 0, 2)
    qkv_part = jnp.concatenate(
        [
            qkv_part.reshape(n_dp, block, qkv_cols),
            jnp.pad(small_sum, ((0, 0), (0, 0), (0, qkv_cols - block))),
        ],
        axis=1,
    )
    qkv_core = sum_core(qkv_part.reshape(n_chip, n_core, block + 8, qkv_cols), core)
    fold = Fold((out_core, qkv_core))
    fold.send()
    dattn = fold.meet(*dattn)
    while fold.orders[0]:
        fold.send()
        fold.meet()
    out_weight_sum, qkv_sum = fold.pair
    out_total = out_base
    for piece in out_sums:
        out_total = out_total + piece.astype(F32)
    small_sum = qkv_sum[block : block + 4, :block].reshape(4, n_exp, w_rows).transpose(1, 0, 2)
    small_sum = jnp.pad(small_sum, ((0, 0), (0, w_rows - 4), (0, LANES - w_rows)))
    tail = jnp.concatenate(
        [
            qkv_sum[:block].reshape(n_exp, w_rows, qkv_cols),
            out_weight_sum.reshape(n_exp, w_rows, width),
            small_sum,
            up_sum.reshape(n_exp, w_rows, dense_cols),
        ],
        axis=2,
    ).astype(BF16)
    tail_sent = after(tail, *dattn)
    tail = swap(tail_sent, "expert")
    tokens_grad = simple(
        leave_body, LAST, shape_of((rows, width), BF16), [tokens, gain_one, dmiddle] + list(dattn)
    )

    exp_sum = after(exp_sum, tail_sent)
    up_exp_sum = exp_sum[:up_rows].reshape(n_block, n_core, exp_rows, width)
    own_exp, sent_exp = by_core(core, up_exp_sum[:, 0], up_exp_sum[:, 1])
    halves = jnp.stack(by_core(core, own_exp, other_core(sent_exp)))
    exp_up_grad = halves.transpose(2, 0, 1, 3).reshape(exp_rows, n_core, n_chip, exp_cols)
    exp_up_grad = exp_up_grad.transpose(0, 2, 1, 3).reshape(1, exp_rows, n_dp * exp_cols)
    exp_up_grad = exp_up_grad.astype(F32)
    exp_down_grad = exp_sum[up_rows:].astype(F32)[None]
    tail = after(tail, exp_up_grad, exp_down_grad, tokens_grad, out_total, down_sum)
    up_grad = tail[:, :, qkv_cols + width + LANES :].reshape(n_exp, w_rows, n_dp, dense_rows)
    up_grad = up_grad.transpose(1, 2, 0, 3).reshape(w_rows, n_exp * dense_cols).astype(F32)
    qkv_grad = tail[:, :, :qkv_cols].reshape(n_exp, w_rows, 3, head_cols)
    small_sum = jnp.sum(tail[:, :4, qkv_cols + width : qkv_cols + width + w_rows].astype(F32), axis=0)
    return (
        out_total.astype(BF16),
        tokens_grad,
        small_sum[0],
        qkv_grad.transpose(1, 2, 0, 3).reshape(w_rows, 3 * width).astype(F32),
        jnp.sum(tail[:, :, qkv_cols : qkv_cols + width].astype(F32), axis=0),
        small_sum[1],
        small_sum[2:4].T,
        up_grad,
        down_sum,
        exp_up_grad,
        exp_down_grad,
    )


def solution(mesh):
    n_dp, n_exp = (mesh.shape["dp"], mesh.shape["expert"])
    fine = Mesh(mesh.devices.reshape(n_dp // 2, 2, n_exp), ("chip", "core", "expert"))
    every = ("chip", "core", "expert")
    rows = P(every, None)
    expert = P("expert", DP, None)
    return jax.shard_map(
        shards,
        mesh=fine,
        in_specs=(
            rows,
            P(every),
            rows,
            rows,
            P(every),
            rows,
            rows,
            rows,
            expert,
            expert,
            rows,
            P(DP, None),
            rows,
        ),
        out_specs=(
            rows,
            rows,
            P(every),
            rows,
            rows,
            P(every),
            rows,
            rows,
            rows,
            expert,
            expert,
        ),
        check_vma=False,
    )
```

profile of v0, /device:TPU:0, one launch (start us, length us, event | category | flops | bytes accessed | tf_op | source)
XLA Modules:
  0.0 363.4 jit_solution(703472192440347198)
XLA Ops:
  10.0 26.2 %all_to_all.35 = bf16[4,32,3072]{2,1,0:T(8,128)(2,1)S(1)} all-to-all(bf16[4,32,3072]{2,1,0:T(8,128)(2,1)S(1)} %pad_maximum_fusion.2), channel_id=1, replica_groups=mesh['chip'=4,'core'=2,'expert'=4] {'expert'}, dimensions={0} | all-to-all | bytes 1572864 | tf_op jit(solution)/shard_map/all_to_all | solution.py:59
  37.4 3.6 %all-to-all-start.1 = ((bf16[4,128,1024]{2,1,0:T(8,128)(2,1)}), bf16[4,128,1024]{2,1,0:T(8,128)(2,1)S(1)}, u32[]{:S(2)}, u32[]{:S(2)}) async-start(bf16[4,128,1024]{2,1,0:T(8,128)(2,1)} %broadcast_in_dim.33), calls=%async_computation.1 | async-start | bytes 2097152 | tf_op jit(solution)/shard_map/all_to_all | solution.py:59
  42.3 13.9 %all_gather.16 = bf16[448,768]{1,0:T(8,128)(2,1)S(1)} all-gather(bf16[56,768]{1,0:T(8,128)(2,1)S(1)} %fusion.21), channel_id=1, replica_groups=mesh['chip'=4,'core'=2,'expert'=4] {'chip','core'}, dimensions={0}, use_global_device_ids=true | all-gather | bytes 774144 | tf_op jit(solution)/shard_map/all_gather | solution.py:104
  56.2 16.5 %all_gather.15 = bf16[640,768]{1,0:T(8,128)(2,1)} all-gather(bf16[80,768]{1,0:T(8,128)(2,1)S(1)} %slice.231), channel_id=1, replica_groups=mesh['chip'=4,'core'=2,'expert'=4] {'chip','core'}, dimensions={0}, use_global_device_ids=true | all-gather | bytes 1105920 | tf_op jit(solution)/shard_map/all_gather | solution.py:104
  80.1 4.9 %all-to-all-start.2 = ((bf16[4,128,1024]{2,1,0:T(8,128)(2,1)}), bf16[4,128,1024]{2,1,0:T(8,128)(2,1)S(1)}, u32[]{:S(2)}, u32[]{:S(2)}) async-start(bf16[4,128,1024]{2,1,0:T(8,128)(2,1)} %broadcast_in_dim.58), calls=%async_computation.2 | async-start | bytes 2097152 | tf_op jit(solution)/shard_map/all_to_all | solution.py:59
  85.0 4.3 %shard_map.212 = (bf16[512,768]{1,0:T(8,128)(2,1)}, bf16[512,1024]{1,0:T(8,128)(2,1)}, bf16[1024,768]{1,0:T(8,128)(2,1)}) custom-call(bf16[512,1024]{1,0:T(8,128)(2,1)} %bitcast.275, f32[1,1024]{1,0:T(1,128)} %get-tuple-element.249.gain_ref, bf16[8,80,768]{2,1,0:T(8,128)(2,1)} %bitcast.299, bf16[8,56,768]{2,1,0:T(8,128)(2,1)} %bitcast.301), custom_call_target="tpu_custom_call" | custom-call | tf_op jit(solution)/shard_map/pallas_call | solution.py:154
  89.3 5.8 %shard_map.213 = bf16[512,256]{1,0:T(8,128)(2,1)} custom-call(s32[1]{0:T(128)} %bitcast.322, bf16[512,768]{1,0:T(8,128)(2,1)} %get-tuple-element.97.q_ref.k_ref.v_ref, bf16[512,768]{1,0:T(8,128)(2,1)} %get-tuple-element.97.q_ref.k_ref.v_ref, bf16[512,768]{1,0:T(8,128)(2,1)} %get-tuple-element.97.q_ref.k_ref.v_ref), custom_call_target="tpu_custom_call" | custom-call | tf_op jit(solution)/shard_map/pallas_call | solution.py:154
  95.1 16.1 %all-to-all-done.2 = bf16[4,128,1024]{2,1,0:T(8,128)(2,1)S(1)} async-done(((bf16[4,128,1024]{2,1,0:T(8,128)(2,1)}), bf16[4,128,1024]{2,1,0:T(8,128)(2,1)S(1)}, u32[]{:S(2)}, u32[]{:S(2)}) %all-to-all-start.2) | async-done | bytes 1048608 | tf_op jit(solution)/shard_map/all_to_all | solution.py:59
  113.4 4.0 %all-to-all-start.3 = ((bf16[4,512,256]{2,1,0:T(8,128)(2,1)}), bf16[4,512,256]{2,1,0:T(8,128)(2,1)S(1)}, u32[]{:S(2)}, u32[]{:S(2)}) async-start(bf16[4,512,256]{2,1,0:T(8,128)(2,1)} %broadcast_in_dim.59), calls=%async_computation.3 | async-start | bytes 2097152 | tf_op jit(solution)/shard_map/all_to_all | solution.py:59
  119.7 3.1 slice.237
  122.8 20.0 %all-to-all-done.3.att_ref = bf16[4,512,256]{2,1,0:T(8,128)(2,1)S(1)} async-done(((bf16[4,512,256]{2,1,0:T(8,128)(2,1)}), bf16[4,512,256]{2,1,0:T(8,128)(2,1)S(1)}, u32[]{:S(2)}, u32[]{:S(2)}) %all-to-all-start.3) | async-done | bytes 1048608 | tf_op jit(solution)/shard_map/all_to_all | solution.py:59
  143.8 5.7 %shard_map.214 = (f32[512,1024]{1,0:T(8,128)}, bf16[512,1024]{1,0:T(8,128)(2,1)}, f32[512,2]{1,0:T(8,128)}) custom-call(bf16[4,512,256]{2,1,0:T(8,128)(2,1)} %copy-done.9, bf16[512,1024]{1,0:T(8,128)(2,1)} %bitcast.276, bf16[1024,1024]{1,0:T(8,128)(2,1)} %bitcast.271, f32[1,1024]{1,0:T(1,128)} %get-tuple-element.248.gain_ref, bf16[16,1024]{1,0:T(8,128)(2,1)} %pad.28.mix_ref), custom_call_target="tpu_custom_call" | custom-call | tf_op jit(solution)/shard_map/pallas_call | solution.py:154
  149.5 13.0 %shard_map.215 = (bf16[128,1024]{1,0:T(8,128)(2,1)}, bf16[128,1024]{1,0:T(8,128)(2,1)}, bf16[128,1024]{1,0:T(8,128)(2,1)}, bf16[128,1024]{1,0:T(8,128)(2,1)}, bf...) custom-call(s32[1]{0:T(128)} %bitcast.ex_ref, ...), custom_call_target="tpu_custom_call" | custom-call | tf_op jit(solution)/shard_map/pallas_call | solution.py:154
  162.5 3.5 all-to-all-start.4
  166.3 3.0 shard_map.216.own_ref
  169.3 6.5 %shard_map.217 = (bf16[1024,1024]{1,0:T(8,128)(2,1)}, bf16[1024,1024]{1,0:T(8,128)(2,1)}) custom-call(bf16[512,1024]{1,0:T(8,128)(2,1)} %get-tuple-element.103.x_ref.ffn_ref, bf16[512,1024]{1,0:T(8,128)(2,1)} %get-tuple-element.108.g_ref, bf16[512,1024]{1,0:T(8,128)(2,1)} %get-tuple-element.109.act_ref, bf16[512,1024]{1,0:T(8,128)(2,1)} %get-tuple-element.110.dpre_ref), custom_call_target="tpu_custom_call" | custom-call | tf_op jit(solution)/shard_map/pallas_call | solution.py:154
  176.7 12.3 %shard_map.218 = (f32[2,160,1024]{2,1,0:T(8,128)}, bf16[2,160,1024]{2,1,0:T(8,128)(2,1)}, bf16[320,2048]{1,0:T(8,128)(2,1)}, bf16[320,2048]{1,0:T(8,128)(2,1)}) custom-call(bf16[2,160,1024]{2,1,0:T(8,128)(2,1)} %shard_map.216.own_ref, bf16[2,160,1024]{2,1,0:T(8,128)(2,1)} %copy-done.13, bf16[4,512,1024]{2,1,0:T(8,128)(2,1)} %bitcast.295, ...), custom_call_target="tpu_custom_call" | custom-call | tf_op jit(solution)/shard_map/pallas_call | solution.py:154
  189.5 10.3 %shard_map.219 = bf16[4,1024,1024]{2,1,0:T(8,128)(2,1)} custom-call(bf16[2,160,1024]{2,1,0:T(8,128)(2,1)} %shard_map.216.own_ref, bf16[2,160,1024]{2,1,0:T(8,128)(2,1)} %copy-done.13, bf16[320,2048]{1,0:T(8,128)(2,1)} %get-tuple-element.115.act_ref, bf16[320,2048]{1,0:T(8,128)(2,1)} %get-tuple-element.116.dpre_ref), custom_call_target="tpu_custom_call" | custom-call | tf_op jit(solution)/shard_map/pallas_call | solution.py:154
  225.1 6.0 %collective-permute-done.6.refs_2_ = bf16[2,40,1024]{2,1,0:T(8,128)(2,1)S(1)} collective-permute-done((bf16[2,40,1024]{2,1,0:T(8,128)(2,1)S(1)}, bf16[2,40,1024]{2,1,0:T(8,128)(2,1)S(1)}, u32[]{:S(2)}, u32[]{:S(2)}) %collective-permute-start.6) | collective-permute-done | bytes 163872 | tf_op jit(solution)/shard_map/ppermute | solution.py:69
  232.4 5.7 %shard_map.220 = (f32[128,1024]{1,0:T(8,128)}, bf16[128,1024]{1,0:T(8,128)(2,1)}, bf16[4,128,256]{2,1,0:T(8,128)(2,1)}, f32[8,1024]{1,0:T(8,128)}, f32[128,1024]{1,0:T(8,128)}) custom-call(s32[1]{0:T(128)} %bitcast.ex_ref, bf16[4,144,1024]{2,1,0:T(8,128)(2,1)} %copy-done.10, s32[128,1]{1,0:T(8,128)} %copy.201.slot_ref, ...), custom_call_target="tpu_custom_call" | custom-call | tf_op jit(solution)/shard_map/pallas_call | solution.py:154
  238.1 6.2 %all-to-all-start.5 = ((bf16[4,128,256]{2,1,0:T(8,128)(2,1)}), bf16[4,128,256]{2,1,0:T(8,128)(2,1)S(1)}, u32[]{:S(2)}, u32[]{:S(2)}) async-start(bf16[4,128,256]{2,1,0:T(8,128)(2,1)} %get-tuple-element.130), calls=%async_computation.5 | async-start | bytes 524288 | tf_op jit(solution)/shard_map/all_to_all | solution.py:59
  244.3 8.3 %all-to-all-done.5 = bf16[4,128,256]{2,1,0:T(8,128)(2,1)S(1)} async-done(((bf16[4,128,256]{2,1,0:T(8,128)(2,1)}), bf16[4,128,256]{2,1,0:T(8,128)(2,1)S(1)}, u32[]{:S(2)}, u32[]{:S(2)}) %all-to-all-start.5) | async-done | bytes 262176 | tf_op jit(solution)/shard_map/all_to_all | solution.py:59
  260.1 7.5 %shard_map.221 = (bf16[512,256]{1,0:T(8,128)(2,1)}, bf16[512,256]{1,0:T(8,128)(2,1)}, bf16[512,256]{1,0:T(8,128)(2,1)}) custom-call(s32[1]{0:T(128)} %bitcast.323, bf16[512,768]{1,0:T(8,128)(2,1)} %get-tuple-element.97.q_ref.k_ref.v_ref, bf16[512,768]{1,0:T(8,128)(2,1)} %get-tuple-element.97.q_ref.k_ref.v_ref, ...), custom_call_target="tpu_custom_call" | custom-call | flops 23000000512 | tf_op jit(solution)/shard_map/pallas_call | solution.py:154
  267.6 4.9 %shard_map.222 = (bf16[128,1024]{1,0:T(8,128)(2,1)}, bf16[128,1024]{1,0:T(8,128)(2,1)}, bf16[128,1024]{1,0:T(8,128)(2,1)}, bf16[128,1024]{1,0:T(8,128)(2,1)}, f32[8,1024]{1,0:T(8,128)}) custom-call(s32[1]{0:T(128)} %bitcast.ex_ref, bf16[512,256]{1,0:T(8,128)(2,1)} %get-tuple-element.134.dq_ref, bf16[512,256]{1,0:T(8,128)(2,1)} %get-tuple-element.135.dk_ref, ...), custom_call_target="tpu_custom_call" | custom-call | tf_op jit(solution)/shard_map/pallas_call | solution.py:154
  273.3 3.1 shard_map.223
  278.2 3.7 %shard_map.224 = bf16[1024,768]{1,0:T(8,128)(2,1)} custom-call(bf16[512,1024]{1,0:T(8,128)(2,1)} %get-tuple-element.159.x_ref, bf16[512,256]{1,0:T(8,128)(2,1)} %get-tuple-element.134.dq_ref, bf16[512,256]{1,0:T(8,128)(2,1)} %get-tuple-element.135.dk_ref, bf16[512,256]{1,0:T(8,128)(2,1)} %get-tuple-element.136.dv_ref), custom_call_target="tpu_custom_call" | custom-call | flops 23000000512 | tf_op jit(solution)/shard_map/pallas_call | solution.py:154
  294.9 5.8 %collective-permute-done.19.refs_1_ = bf16[128,1024]{1,0:T(8,128)(2,1)S(1)} collective-permute-done((bf16[128,1024]{1,0:T(8,128)(2,1)S(1)}, bf16[128,1024]{1,0:T(8,128)(2,1)S(1)}, u32[]{:S(2)}, u32[]{:S(2)}) %collective-permute-start.19) | collective-permute-done | bytes 262176 | tf_op jit(solution)/shard_map/ppermute | solution.py:69
  300.7 10.1 %collective-permute-done.20.refs_2_ = bf16[128,1024]{1,0:T(8,128)(2,1)S(1)} collective-permute-done((bf16[128,1024]{1,0:T(8,128)(2,1)S(1)}, bf16[128,1024]{1,0:T(8,128)(2,1)S(1)}, u32[]{:S(2)}, u32[]{:S(2)}) %collective-permute-start.20) | collective-permute-done | bytes 262176 | tf_op jit(solution)/shard_map/ppermute | solution.py:69
  316.2 4.3 %collective-permute-done.23 = bf16[136,768]{1,0:T(8,128)(2,1)S(1)} collective-permute-done((bf16[136,768]{1,0:T(8,128)(2,1)S(1)}, bf16[136,768]{1,0:T(8,128)(2,1)S(1)}, u32[]{:S(2)}, u32[]{:S(2)}) %collective-permute-start.23) | collective-permute-done | bytes 208928 | tf_op jit(solution)/shard_map/ppermute | solution.py:86
  323.3 7.1 %all-to-all-start.6 = ((bf16[4,32,2944]{2,1,0:T(8,128)(2,1)}), bf16[4,32,2944]{2,1,0:T(8,128)(2,1)S(1)}, u32[]{:S(2)}, u32[]{:S(2)}) async-start(bf16[4,32,2944]{2,1,0:T(8,128)(2,1)} %fusion.7), calls=%async_computation.6 | async-start | bytes 1507328 | tf_op jit(solution)/shard_map/all_to_all | solution.py:59
  330.4 3.2 bitcast_convert_fusion
  344.0 5.3 %all-to-all-done.6 = bf16[4,32,2944]{2,1,0:T(8,128)(2,1)S(1)} async-done(((bf16[4,32,2944]{2,1,0:T(8,128)(2,1)}), bf16[4,32,2944]{2,1,0:T(8,128)(2,1)S(1)}, u32[]{:S(2)}, u32[]{:S(2)}) %all-to-all-start.6) | async-done | bytes 753696 | tf_op jit(solution)/shard_map/all_to_all | solution.py:59
  (249 shorter events, 94.6 us)
Async XLA Ops:
  7.2 66.1 %all-gather.9.cloned.1.call-start = ((), (), s32[]{:S(2)}) async-start(), calls=%async_computation.11 | async-start | bytes 5242880 | tf_op jit(solution)/shard_map/all_gather | solution.py:754
  37.4 35.8 %all-to-all-start.1 = ((bf16[4,128,1024]{2,1,0:T(8,128)(2,1)}), bf16[4,128,1024]{2,1,0:T(8,128)(2,1)S(1)}, u32[]{:S(2)}, u32[]{:S(2)}) async-start(bf16[4,128,1024]{2,1,0:T(8,128)(2,1)} %broadcast_in_dim.33), calls=%async_computation.1 | async-start | bytes 2097152 | tf_op jit(solution)/shard_map/all_to_all | solution.py:59
  41.1 78.6 %all-gather.5.cloned.1.call-start = ((), (), s32[]{:S(2)}) async-start(), calls=%async_computation.8 | async-start | bytes 7077888 | tf_op jit(solution)/shard_map/all_gather | solution.py:802
  73.3 102.5 %all-gather.7.cloned.1.call-start = ((), (), s32[]{:S(2)}) async-start(), calls=%async_computation.9 | async-start | bytes 5242880 | tf_op jit(solution)/shard_map/all_gather | solution.py:815
  80.1 31.2 %all-to-all-start.2 = ((bf16[4,128,1024]{2,1,0:T(8,128)(2,1)}), bf16[4,128,1024]{2,1,0:T(8,128)(2,1)S(1)}, u32[]{:S(2)}, u32[]{:S(2)}) async-start(bf16[4,128,1024]{2,1,0:T(8,128)(2,1)} %broadcast_in_dim.58), calls=%async_computation.2 | async-start | bytes 2097152 | tf_op jit(solution)/shard_map/all_to_all | solution.py:59
  113.4 29.4 %all-to-all-start.3 = ((bf16[4,512,256]{2,1,0:T(8,128)(2,1)}), bf16[4,512,256]{2,1,0:T(8,128)(2,1)S(1)}, u32[]{:S(2)}, u32[]{:S(2)}) async-start(bf16[4,512,256]{2,1,0:T(8,128)(2,1)} %broadcast_in_dim.59), calls=%async_computation.3 | async-start | bytes 2097152 | tf_op jit(solution)/shard_map/all_to_all | solution.py:59
  162.5 38.2 %all-to-all-start.4 = ((bf16[4,144,1024]{2,1,0:T(8,128)(2,1)}), bf16[4,144,1024]{2,1,0:T(8,128)(2,1)S(1)}, u32[]{:S(2)}, u32[]{:S(2)}) async-start(bf16[4,144,1024]{2,1,0:T(8,128)(2,1)} %get-tuple-element.106), calls=%async_computation.4 | async-start | bytes 2359296 | tf_op jit(solution)/shard_map/all_to_all | solution.py:59
  166.1 164.3 %reduce-scatter.2.cloned.1.call-start = ((), (), s32[]{:S(2)}) async-start(), calls=%async_computation.10 | async-start | bytes 10485760 | tf_op jit(solution)/shard_map/reduce_scatter | solution.py:859
  169.3 6.5 %collective-permute-start = (bf16[2,160,1024]{2,1,0:T(8,128)(2,1)}, bf16[2,160,1024]{2,1,0:T(8,128)(2,1)S(1)}, u32[]{:S(2)}, u32[]{:S(2)}) collective-permute-start(bf16[2,160,1024]{2,1,0:T(8,128)(2,1)} %shard_map.216.own_ref), channel_id=1, source_target_pairs={{0,4},{4,0},{1,5},{5,1},{2,6},{6,2},{3,7},{7,3},{8,12},{12,8},{9,1... | collective-permute-start | bytes 1966088 | tf_op jit(solution)/shard_map/ppermute | solution.py:77
  189.0 10.8 %collective-permute-start.2 = (bf16[2,160,1024]{2,1,0:T(8,128)(2,1)}, bf16[2,160,1024]{2,1,0:T(8,128)(2,1)S(1)}, u32[]{:S(2)}, u32[]{:S(2)}) collective-permute-start(bf16[2,160,1024]{2,1,0:T(8,128)(2,1)} %get-tuple-element.118), channel_id=1, source_target_pairs={{0,4},{4,0},{1,5},{5,1},{2,6},{6,2},{3,7},{7,3},{8,12},{12,8},{9,1... | collective-permute-start | bytes 1966088 | tf_op jit(solution)/shard_map/ppermute | solution.py:77
  204.1 7.6 %collective-permute-start.3 = (bf16[4,128,1024]{2,1,0:T(8,128)(2,1)S(1)}, bf16[4,128,1024]{2,1,0:T(8,128)(2,1)}, u32[]{:S(2)}, u32[]{:S(2)}) collective-permute-start(bf16[4,128,1024]{2,1,0:T(8,128)(2,1)S(1)} %select_bitcast_fusion.2), channel_id=1, source_target_pairs={{0,4},{4,0},{1,5},{5,1},{2,6},{6,2},{3,7},{7,3},{8,12},{12,8},{9,1... | collective-permute-start | bytes 3145736 | tf_op jit(solution)/shard_map/ppermute | solution.py:77
  210.1 34.1 %collective-permute-start.9 = (bf16[2,128,1024]{2,1,0:T(8,128)(2,1)}, bf16[2,128,1024]{2,1,0:T(8,128)(2,1)}, u32[]{:S(2)}, u32[]{:S(2)}) collective-permute-start(bf16[2,128,1024]{2,1,0:T(8,128)(2,1)} %select_convert_fusion), channel_id=1, source_target_pairs={{0,16},{8,24},{16,0},{24,8},{1,17},{9,25},{17,1},{25,9},{2,18},{10... | collective-permute-start | bytes 1572872 | tf_op jit(solution)/shard_map/ppermute | solution.py:86
  214.9 29.4 %collective-permute-start.8 = (bf16[2,128,1024]{2,1,0:T(8,128)(2,1)S(1)}, bf16[2,128,1024]{2,1,0:T(8,128)(2,1)S(1)}, u32[]{:S(2)}, u32[]{:S(2)}) collective-permute-start(bf16[2,128,1024]{2,1,0:T(8,128)(2,1)S(1)} %fusion.9), channel_id=1, source_target_pairs={{0,8},{8,0},{16,24},{24,16},{1,9},{9,1},{17,25},{25,17},{2,10},{10... | collective-permute-start | bytes 1572872 | tf_op jit(solution)/shard_map/ppermute | solution.py:86
  216.0 9.1 %collective-permute-start.5 = (bf16[2,40,1024]{2,1,0:T(8,128)(2,1)S(1)}, bf16[2,40,1024]{2,1,0:T(8,128)(2,1)S(1)}, u32[]{:S(2)}, u32[]{:S(2)}) collective-permute-start(bf16[2,40,1024]{2,1,0:T(8,128)(2,1)S(1)} %copy-done.33), channel_id=1, source_target_pairs={{0,1},{1,2},{2,3},{3,0},{4,5},{5,6},{6,7},{7,4},{8,9},{9,10},{10,1... | collective-permute-start | bytes 491528 | tf_op jit(solution)/shard_map/ppermute | solution.py:69
  217.9 13.2 %collective-permute-start.6 = (bf16[2,40,1024]{2,1,0:T(8,128)(2,1)S(1)}, bf16[2,40,1024]{2,1,0:T(8,128)(2,1)S(1)}, u32[]{:S(2)}, u32[]{:S(2)}) collective-permute-start(bf16[2,40,1024]{2,1,0:T(8,128)(2,1)S(1)} %get-tuple-element.127), channel_id=1, source_target_pairs={{0,2},{1,3},{2,0},{3,1},{4,6},{5,7},{6,4},{7,5},{8,10},{9,11},{10,... | collective-permute-start | bytes 491528 | tf_op jit(solution)/shard_map/ppermute | solution.py:69
  220.3 10.8 %collective-permute-start.7 = (bf16[2,40,1024]{2,1,0:T(8,128)(2,1)S(1)}, bf16[2,40,1024]{2,1,0:T(8,128)(2,1)S(1)}, u32[]{:S(2)}, u32[]{:S(2)}) collective-permute-start(bf16[2,40,1024]{2,1,0:T(8,128)(2,1)S(1)} %get-tuple-element.128), channel_id=1, source_target_pairs={{0,3},{1,0},{2,1},{3,2},{4,7},{5,4},{6,5},{7,6},{8,11},{9,8},{10,9... | collective-permute-start | bytes 491528 | tf_op jit(solution)/shard_map/ppermute | solution.py:69
  238.1 14.4 %all-to-all-start.5 = ((bf16[4,128,256]{2,1,0:T(8,128)(2,1)}), bf16[4,128,256]{2,1,0:T(8,128)(2,1)S(1)}, u32[]{:S(2)}, u32[]{:S(2)}) async-start(bf16[4,128,256]{2,1,0:T(8,128)(2,1)} %get-tuple-element.130), calls=%async_computation.5 | async-start | bytes 524288 | tf_op jit(solution)/shard_map/all_to_all | solution.py:59
  252.5 25.5 %collective-permute-start.14 = (bf16[128,1024]{1,0:T(8,128)(2,1)}, bf16[128,1024]{1,0:T(8,128)(2,1)S(1)}, u32[]{:S(2)}, u32[]{:S(2)}) collective-permute-start(bf16[128,1024]{1,0:T(8,128)(2,1)} %get-tuple-element.149), channel_id=1, source_target_pairs={{0,3},{1,0},{2,1},{3,2},{4,7},{5,4},{6,5},{7,6},{8,11},{9,8},{10,9... | collective-permute-start | bytes 786440 | tf_op jit(solution)/shard_map/ppermute | solution.py:69
  253.8 24.4 %collective-permute-start.13 = (bf16[128,1024]{1,0:T(8,128)(2,1)}, bf16[128,1024]{1,0:T(8,128)(2,1)S(1)}, u32[]{:S(2)}, u32[]{:S(2)}) collective-permute-start(bf16[128,1024]{1,0:T(8,128)(2,1)} %get-tuple-element.147), channel_id=1, source_target_pairs={{0,2},{1,3},{2,0},{3,1},{4,6},{5,7},{6,4},{7,5},{8,10},{9,11},{10,... | collective-permute-start | bytes 786440 | tf_op jit(solution)/shard_map/ppermute | solution.py:69
  254.1 24.1 %collective-permute-start.12 = (bf16[128,1024]{1,0:T(8,128)(2,1)}, bf16[128,1024]{1,0:T(8,128)(2,1)}, u32[]{:S(2)}, u32[]{:S(2)}) collective-permute-start(bf16[128,1024]{1,0:T(8,128)(2,1)} %get-tuple-element.145), channel_id=1, source_target_pairs={{0,1},{1,2},{2,3},{3,0},{4,5},{5,6},{6,7},{7,4},{8,9},{9,10},{10,1... | collective-permute-start | bytes 786440 | tf_op jit(solution)/shard_map/ppermute | solution.py:69
  257.5 20.7 %collective-permute-start.11 = (bf16[128,1024]{1,0:T(8,128)(2,1)}, bf16[128,1024]{1,0:T(8,128)(2,1)}, u32[]{:S(2)}, u32[]{:S(2)}) collective-permute-start(bf16[128,1024]{1,0:T(8,128)(2,1)} %fusion.16), channel_id=1, source_target_pairs={{0,8},{8,0},{16,24},{24,16},{1,9},{9,1},{17,25},{25,17},{2,10},{10... | collective-permute-start | bytes 786440 | tf_op jit(solution)/shard_map/ppermute | solution.py:86
  259.6 18.6 %collective-permute-start.10 = (bf16[128,1024]{1,0:T(8,128)(2,1)}, bf16[128,1024]{1,0:T(8,128)(2,1)}, u32[]{:S(2)}, u32[]{:S(2)}) collective-permute-start(bf16[128,1024]{1,0:T(8,128)(2,1)} %fusion.15), channel_id=1, source_target_pairs={{0,16},{8,24},{16,0},{24,8},{1,17},{9,25},{17,1},{25,9},{2,18},{10... | collective-permute-start | bytes 786440 | tf_op jit(solution)/shard_map/ppermute | solution.py:86
  278.1 6.1 %collective-permute-start.15 = (bf16[4,128,1024]{2,1,0:T(8,128)(2,1)S(1)}, bf16[4,128,1024]{2,1,0:T(8,128)(2,1)}, u32[]{:S(2)}, u32[]{:S(2)}) collective-permute-start(bf16[4,128,1024]{2,1,0:T(8,128)(2,1)S(1)} %select_bitcast_fusion), channel_id=1, source_target_pairs={{0,4},{4,0},{1,5},{5,1},{2,6},{6,2},{3,7},{7,3},{8,12},{12,8},{9,1... | collective-permute-start | bytes 3145736 | tf_op jit(solution)/shard_map/ppermute | solution.py:77
  286.2 25.8 %collective-permute-start.16 = (bf16[2,128,1024]{2,1,0:T(8,128)(2,1)S(1)}, bf16[2,128,1024]{2,1,0:T(8,128)(2,1)S(1)}, u32[]{:S(2)}, u32[]{:S(2)}) collective-permute-start(bf16[2,128,1024]{2,1,0:T(8,128)(2,1)S(1)} %fusion.10), channel_id=1, source_target_pairs={{0,8},{8,0},{16,24},{24,16},{1,9},{9,1},{17,25},{25,17},{2,10},{10... | collective-permute-start | bytes 1572872 | tf_op jit(solution)/shard_map/ppermute | solution.py:86
  288.2 22.7 %collective-permute-start.18 = (bf16[2,136,768]{2,1,0:T(8,128)(2,1)S(1)}, bf16[2,136,768]{2,1,0:T(8,128)(2,1)S(1)}, u32[]{:S(2)}, u32[]{:S(2)}) collective-permute-start(bf16[2,136,768]{2,1,0:T(8,128)(2,1)S(1)} %select_convert_fusion.2), channel_id=1, source_target_pairs={{0,16},{8,24},{16,0},{24,8},{1,17},{9,25},{17,1},{25,9},{2,18},{10... | collective-permute-start | bytes 1253384 | tf_op jit(solution)/shard_map/ppermute | solution.py:86
  289.6 11.1 %collective-permute-start.19 = (bf16[128,1024]{1,0:T(8,128)(2,1)S(1)}, bf16[128,1024]{1,0:T(8,128)(2,1)S(1)}, u32[]{:S(2)}, u32[]{:S(2)}) collective-permute-start(bf16[128,1024]{1,0:T(8,128)(2,1)S(1)} %copy-done.44), channel_id=1, source_target_pairs={{0,1},{1,2},{2,3},{3,0},{4,5},{5,6},{6,7},{7,4},{8,9},{9,10},{10,1... | collective-permute-start | bytes 786440 | tf_op jit(solution)/shard_map/ppermute | solution.py:69
  292.1 18.7 %collective-permute-start.20 = (bf16[128,1024]{1,0:T(8,128)(2,1)S(1)}, bf16[128,1024]{1,0:T(8,128)(2,1)S(1)}, u32[]{:S(2)}, u32[]{:S(2)}) collective-permute-start(bf16[128,1024]{1,0:T(8,128)(2,1)S(1)} %copy-done.43), channel_id=1, source_target_pairs={{0,2},{1,3},{2,0},{3,1},{4,6},{5,7},{6,4},{7,5},{8,10},{9,11},{10,... | collective-permute-start | bytes 786440 | tf_op jit(solution)/shard_map/ppermute | solution.py:69
  293.0 17.8 %collective-permute-start.21 = (bf16[128,1024]{1,0:T(8,128)(2,1)S(1)}, bf16[128,1024]{1,0:T(8,128)(2,1)S(1)}, u32[]{:S(2)}, u32[]{:S(2)}) collective-permute-start(bf16[128,1024]{1,0:T(8,128)(2,1)S(1)} %copy-done.42), channel_id=1, source_target_pairs={{0,3},{1,0},{2,1},{3,2},{4,7},{5,4},{6,5},{7,6},{8,11},{9,8},{10,9... | collective-permute-start | bytes 786440 | tf_op jit(solution)/shard_map/ppermute | solution.py:69
  312.3 8.1 %collective-permute-start.22 = (bf16[128,1024]{1,0:T(8,128)(2,1)S(1)}, bf16[128,1024]{1,0:T(8,128)(2,1)S(1)}, u32[]{:S(2)}, u32[]{:S(2)}) collective-permute-start(bf16[128,1024]{1,0:T(8,128)(2,1)S(1)} %fusion.17), channel_id=1, source_target_pairs={{0,16},{8,24},{16,0},{24,8},{1,17},{9,25},{17,1},{25,9},{2,18},{10... | collective-permute-start | bytes 786440 | tf_op jit(solution)/shard_map/ppermute | solution.py:86
  314.1 6.4 %collective-permute-start.23 = (bf16[136,768]{1,0:T(8,128)(2,1)S(1)}, bf16[136,768]{1,0:T(8,128)(2,1)S(1)}, u32[]{:S(2)}, u32[]{:S(2)}) collective-permute-start(bf16[136,768]{1,0:T(8,128)(2,1)S(1)} %fusion.18), channel_id=1, source_target_pairs={{0,8},{8,0},{16,24},{24,16},{1,9},{9,1},{17,25},{25,17},{2,10},{10... | collective-permute-start | bytes 626696 | tf_op jit(solution)/shard_map/ppermute | solution.py:86
  323.3 25.9 %all-to-all-start.6 = ((bf16[4,32,2944]{2,1,0:T(8,128)(2,1)}), bf16[4,32,2944]{2,1,0:T(8,128)(2,1)S(1)}, u32[]{:S(2)}, u32[]{:S(2)}) async-start(bf16[4,32,2944]{2,1,0:T(8,128)(2,1)} %fusion.7), calls=%async_computation.6 | async-start | bytes 1507328 | tf_op jit(solution)/shard_map/all_to_all | solution.py:59
  333.7 6.5 %collective-permute-start.24 = (bf16[2,128,1024]{2,1,0:T(8,128)(2,1)S(1)}, bf16[2,128,1024]{2,1,0:T(8,128)(2,1)S(1)}, u32[]{:S(2)}, u32[]{:S(2)}) collective-permute-start(bf16[2,128,1024]{2,1,0:T(8,128)(2,1)S(1)} %fusion.8), channel_id=1, source_target_pairs={{0,4},{4,0},{1,5},{5,1},{2,6},{6,2},{3,7},{7,3},{8,12},{12,8},{9,1... | collective-permute-start | bytes 1572872 | tf_op jit(solution)/shard_map/ppermute | solution.py:77
  (49 other events, 193.8 us)
Sparse Core Ops, SparseCore 0:
  9.9 62.1 all-gather.8
  73.9 45.5 all-gather.4
  121.4 52.6 all-gather.6
  201.9 115.3 reduce-scatter.1
where the time goes:
time: 370 us; the launch traced here: 363 us
  Pallas kernels  88.5 us (24%)
  waiting for transfers between devices  79.4 us (21%)
  blocking collectives  56.6 us (15%)
  starting transfers between devices  55.2 us (15%)
  local copies, waits for them, and re-layouts  37.5 us (10%)
  other arithmetic  31.4 us (8%)
  between operations  14.9 us (4%)
    pallas_call x14, Pallas kernels, call(): pl.pallas_call(body, grid=grid, in_specs=in_specs, out_specs=out_specs, o...  88.5 us
    all_to_all x6, waiting for transfers between devices, swap(): return lax.all_to_all(values, axis, split_axis=0, concat_axis=0, tiled=True)  49.6 us
    all_gather x2, blocking collectives, gather_small(): lax.all_gather(values[k:k + step], axes, axis=0, tiled=True)  30.3 us
    all_to_all x6, starting transfers between devices, swap(): return lax.all_to_all(values, axis, split_axis=0, concat_axis=0, tiled=True)  29.4 us
    all_to_all x1, blocking collectives, swap(): return lax.all_to_all(values, axis, split_axis=0, concat_axis=0, tiled=True)  26.2 us
    ppermute x9, waiting for transfers between devices, turn(): lax.ppermute(values, 'expert', [(i, (i + step) % count) for i in range(co...  21.9 us
    ppermute x9, starting transfers between devices, turn(): lax.ppermute(values, 'expert', [(i, (i + step) % count) for i in range(co...  13.8 us
    unnamed x96, local copies, waits for them, and re-layouts  12.1 us
  transfers between devices with their start and end apart: 35, of which 10 were waited for; matrix products, arithmetic and copies ran while one was open for 15% of the time, Pallas kernels for 24%

commit v1 on v0

--- a/solution.py
+++ b/solution.py
@@ -212,7 +212,9 @@
         scores = jnp.where(allowed, scores, MASK_VALUE)
         weights = jnp.exp(scores - jnp.max(scores, axis=1, keepdims=True))
         probs = weights * (1.0 / jnp.sum(weights, axis=1, keepdims=True))
-        out_ref[:, at] = dot(probs.astype(BF16), v_ref[:, at]).astype(BF16)
+        result = dot(probs.astype(BF16), v_ref[:, at]).astype(BF16)
+        for j in range(out_ref.shape[0]):
+            out_ref[j, :, at] = result
 
 
 def attend_back_body(
@@ -271,16 +273,17 @@
     return (operands, specs, by_tile, by_pair, (pairs, group // tile), cols)
 
 
-def attend(qkv, split, head_cols):
+def attend(qkv, split, head_cols, copies):
     group = qkv.shape[0]
-    operands, specs, by_tile, unused, grid, cols = attention_parts(qkv, head_cols)
+    tile = min(512, group)
+    operands, specs, unused, unused, grid, cols = attention_parts(qkv, head_cols)
     return call(
         attend_body,
         0,
-        [shape_of((group, head_cols), BF16)],
+        [shape_of((copies, group, head_cols), BF16)],
         [split] + operands,
         specs,
-        [by_tile],
+        [pl.BlockSpec((copies, tile, cols), lambda p, t: (0, t, p))],
         grid=grid,
     )[0]
 
@@ -424,27 +427,17 @@
             send_ref[k] = total[capacity:].astype(BF16)
 
 
-def expert_grad_body(own_ref, got_ref, act_ref, dpre_ref, grads_ref, turned, rows_grad):
-    n_chip, packed, width = grads_ref.shape
-    cols = act_ref.shape[1]
-    per = width // cols
-    pair_rows = width // n_chip
-    chunk = pl.program_id(0)
-    capacity = own_ref.shape[1]
-
-    @pl.when(chunk == 0)
-    def begin():
-        rows_in = jnp.concatenate([own_ref[0], got_ref[0]], axis=0)
-        turned[...] = jnp.transpose(rows_in.astype(F32)).astype(BF16)
-        rows_grad[:capacity] = own_ref[1]
-        rows_grad[capacity:] = got_ref[1]
-
-    dup = dot(turned[...], dpre_ref[...]).astype(BF16)
-    ddown = dot_lt(act_ref[...], rows_grad[...]).astype(BF16)
-    low = pl.multiple_of(chunk // per * pair_rows, pair_rows)
-    left = pl.multiple_of(chunk % per * cols, cols)
-    grads_ref[:, pl.ds(low, pair_rows), pl.ds(left, cols)] = dup.reshape(n_chip, pair_rows, cols)
-    grads_ref[pl.ds(chunk, 1), packed - cols :, :] = ddown[None]
+def expert_grad_body(own_x, got_x, own_g, got_g, act_ref, dpre_ref, grads_ref):
+    width = grads_ref.shape[2]
+    rows_in = jnp.concatenate([own_x[0], got_x[0]], axis=0)
+    rows_grad = jnp.concatenate([own_g[0], got_g[0]], axis=0)
+    dup = dot_lt(rows_in, dpre_ref[...]).astype(BF16)
+    pair_rows, hidden = dup.shape
+    up_rows = hidden // width * pair_rows
+    for k in range(hidden // width):
+        at = slice(k * pair_rows, (k + 1) * pair_rows)
+        grads_ref[0, at] = dup[:, k * width : (k + 1) * width]
+    grads_ref[0, up_rows:] = dot_lt(act_ref[...], rows_grad).astype(BF16)
 
 
 def expert_ffn(own, got, up, down, pair_rows):
@@ -479,18 +472,25 @@
 def expert_grad(own, got, act, dpre, n_chip):
     unused, capacity, width = own.shape
     count, hidden = act.shape
-    cols = hidden // n_chip
-    packed = (n_chip, hidden // n_chip + hidden // n_chip, width)
-    by_cols = pl.BlockSpec((count, cols), lambda c: (0, c))
+    cols, pair_rows = (hidden // n_chip, width // n_chip)
+    rows = hidden // width * pair_rows + cols
+    by_width = pl.BlockSpec((1, capacity, pair_rows), lambda d: (0, 0, d))
+    second = pl.BlockSpec((1, capacity, width), lambda d: (1, 0, 0))
     return call(
         expert_grad_body,
         0,
-        [shape_of(packed, BF16)],
-        [own, got, act, dpre],
-        [whole(own.shape), whole(own.shape), by_cols, by_cols],
-        [whole(packed)],
+        [shape_of((n_chip, rows, width), BF16)],
+        [own, got, own, got, act, dpre],
+        [
+            by_width,
+            by_width,
+            second,
+            second,
+            pl.BlockSpec((count, cols), lambda d: (0, d)),
+            whole(dpre.shape),
+        ],
+        [pl.BlockSpec((1, rows, width), lambda d: (d, 0, 0))],
         grid=(n_chip,),
-        scratch=[pltpu.VMEM((width, count), BF16), pltpu.VMEM((count, width), BF16)],
     )[0]
 
 
@@ -553,6 +553,41 @@
         + [whole(padded), by_cols, by_cols, whole((group, width))],
         grid=(hidden // step,),
         scratch=[pltpu.VMEM((group, width), F32)] * 2,
+    )
+
+
+def dense_pack_body(core_ref, x_ref, g_ref, act_ref, dpre_ref, keep_ref, send_ref):
+    n_chip, unused, block, unused = keep_ref.shape
+    step = act_ref.shape[1]
+    chunk = pl.program_id(0)
+    left = pl.ds(pl.multiple_of(chunk * step, step), step)
+    first_core = core_ref[0] == 0
+    dup = dot_lt(x_ref[...], dpre_ref[...]).astype(BF16).reshape(n_chip, 2, block, step)
+    ddown = dot_lt(act_ref[...], g_ref[...]).astype(BF16)
+    keep_ref[:, 0, :, left] = jnp.where(first_core, dup[:, 0], dup[:, 1])
+    send_ref[:, 0, :, left] = jnp.where(first_core, dup[:, 1], dup[:, 0])
+    at = pl.ds(chunk, 1)
+    keep_ref[at, 1] = jnp.where(first_core, ddown[:block], ddown[block:])[None]
+    send_ref[at, 1] = jnp.where(first_core, ddown[block:], ddown[:block])[None]
+
+
+def dense_split(core, ffn_input, ddense, act, dpre, shape):
+    group, step = (ffn_input.shape[0], 2 * LANES)
+    by_cols = pl.BlockSpec((group, step), lambda c: (0, c))
+    return call(
+        dense_pack_body,
+        0,
+        [shape_of(shape, BF16)] * 2,
+        [core, ffn_input, ddense, act, dpre],
+        [
+            pl.BlockSpec(memory_space=pltpu.SMEM),
+            whole(ffn_input.shape),
+            whole(ddense.shape),
+            by_cols,
+            by_cols,
+        ],
+        [whole(shape)] * 2,
+        grid=(act.shape[1] // step,),
     )
 
 
@@ -642,47 +677,76 @@
     )
 
 
-def out_grad_body(att_ref, low_ref, grad_ref):
-    n_exp, unused, head_cols = att_ref.shape
-    for j in range(n_exp):
-        grad_ref[j * head_cols : (j + 1) * head_cols] = dot_lt(att_ref[j], low_ref[...]).astype(BF16)
-
-
-def attn_input_back_body(ex_ref, dq_ref, dk_ref, dv_ref, w_ref, x_ref, *refs):
-    pays, (small_ref,) = (refs[:-1], refs[-1:])
-    rows, width = pays[0].shape
-    dgain = jnp.zeros((1, width), F32)
+def split_cores(core_ref, grads, keep_ref, send_ref):
+    n_chip, block = keep_ref.shape[:2]
+    grads = grads.reshape(n_chip, 2, block, grads.shape[-1])
+    first_core = core_ref[0] == 0
+    keep_ref[...] = jnp.where(first_core, grads[:, 0], grads[:, 1])
+    send_ref[...] = jnp.where(first_core, grads[:, 1], grads[:, 0])
+
+
+def out_grad_body(core_ref, att_ref, low_ref, keep_ref, send_ref):
+    grads = [dot_lt(att_ref[j], low_ref[...]).astype(BF16) for j in range(att_ref.shape[0])]
+    split_cores(core_ref, jnp.concatenate(grads, axis=0), keep_ref, send_ref)
+
+
+def attn_input_back_body(ex_ref, dq_ref, dk_ref, dv_ref, w_ref, *pays):
+    rows = pays[0].shape[0]
     for k, pay_ref in enumerate(pays):
         to = lax.rem(ex_ref[0] + k, len(pays))
         at = pl.ds(pl.multiple_of(to * rows, rows), rows)
         grads = jnp.concatenate([dq_ref[at], dk_ref[at], dv_ref[at]], axis=1)
-        dattn = dot_rt(grads, w_ref[...])
-        pay_ref[...] = dattn.astype(BF16)
-        normed, unused = norm_parts(x_ref[at].astype(F32))
-        dgain = dgain + jnp.sum(dattn * normed, axis=0, keepdims=True)
-    small_ref[...] = jnp.concatenate([dgain, jnp.zeros((7, width), F32)], axis=0)
-
-
-def attn_input_back(ex, dparts, matrix, inputs, rows):
-    group, width = inputs.shape
-    head_cols = dparts[0].shape[1]
-    operands = list(dparts) + [matrix, inputs]
-    shapes = [shape_of((rows, width), BF16)] * (group // rows) + [shape_of((8, width), F32)]
-    return call(
-        attn_input_back_body,
-        0,
+        pay_ref[...] = dot_rt(grads, w_ref[...]).astype(BF16)
+
+
+def qkv_grad_body(
+    core_ref, x_ref, w_ref, gain_ref, small_ref, dq_ref, dk_ref, dv_ref, keep_ref, send_ref
+):
+    n_chip, padded, cols = keep_ref.shape
+    block = padded - PAD
+    rows_in = x_ref[...]
+    grads = jnp.concatenate([dot_lt(rows_in, r[...]) for r in (dq_ref, dk_ref, dv_ref)], axis=1)
+    width = grads.shape[0]
+    dgain = jnp.sum(grads * w_ref[...].astype(F32), axis=1, keepdims=True)
+    dgain = jnp.transpose(dgain * jnp.ones((1, LANES), F32))[:8] / gain_ref[...]
+    index = lax.broadcasted_iota(jnp.int32, (8, width), 0)
+    small = jnp.where(index == 0, dgain, small_ref[...])
+    small = jnp.concatenate([small, jnp.zeros((PAD - 8, width), F32)], axis=0)
+    first_core = core_ref[0] == 0
+    for chip in range(n_chip):
+        pair = []
+        for core in range(2):
+            low = (2 * chip + core) * block
+            edge = jnp.concatenate(
+                [small[:, low : low + block], jnp.zeros((PAD, cols - block), F32)], axis=1
+            )
+            pair.append(jnp.concatenate([grads[low : low + block], edge], axis=0).astype(BF16))
+        keep_ref[chip] = jnp.where(first_core, pair[0], pair[1])
+        send_ref[chip] = jnp.where(first_core, pair[1], pair[0])
+
+
+def scalar_call(body, shapes, scalar, operands, weight=0):
+    return call(
+        body,
+        weight,
         shapes,
-        [ex] + operands,
+        [scalar] + operands,
         [pl.BlockSpec(memory_space=pltpu.SMEM)] + [whole(o.shape) for o in operands],
         [whole(o.shape) for o in shapes],
     )
 
 
-def qkv_grad_body(x_ref, dq_ref, dk_ref, dv_ref, grad_ref):
-    rows_in = x_ref[...]
-    grad_ref[...] = jnp.concatenate(
-        [dot_lt(rows_in, r[...]).astype(BF16) for r in (dq_ref, dk_ref, dv_ref)], axis=1
-    )
+def expert_end_body(core_ref, own_ref, got_ref, down_ref, up_out, down_out):
+    cols = down_ref.shape[0]
+    per = own_ref.shape[2] // cols
+    first_core = core_ref[0] == 0
+    for k in range(own_ref.shape[0] * per):
+        at = slice(k % per * cols, (k % per + 1) * cols)
+        mine, theirs = (r[k // per, :, at].astype(F32) for r in (own_ref, got_ref))
+        low = 2 * k * cols
+        up_out[:, low : low + cols] = jnp.where(first_core, mine, theirs)
+        up_out[:, low + cols : low + 2 * cols] = jnp.where(first_core, theirs, mine)
+    down_out[...] = down_ref[...].astype(F32)
 
 
 def leave_body(x_ref, gain_ref, dmid_ref, *refs):
@@ -735,6 +799,7 @@
     ex = lax.axis_index("expert")
     ex_line = jnp.full((1,), ex, jnp.int32)
     core = lax.axis_index("core")
+    core_line = jnp.full((1,), core, jnp.int32)
     share_cap = max(2, 5 * rows // (4 * n_exp))
     capacity = n_exp * share_cap
     bits = chip_bits()
@@ -779,6 +844,9 @@
     at = [qkv_cols, qkv_cols + dense_cols, qkv_cols + dense_cols + width]
     up_own = dealt[:, :, at[0] : at[1]].reshape(block, dense_cols)
     out_own = dealt[:, :, at[1] : at[2]].reshape(block, width)
+    chip_up = chip_up.reshape(up_rows, width)
+    grad_copies = jnp.broadcast_to(out_grad[None], (n_exp,) + out_grad.shape)
+    dealt, chip_up, grad_copies = lax.optimization_barrier((dealt, chip_up, grad_copies))
     choice = after(dealt[:, 0, at[2] + LANES : at[2] + LANES + rows].astype(F32)).astype(jnp.int32)
     small = dealt[:, :4, at[2] : at[2] + w_rows].transpose(1, 0, 2).reshape(4, block)
     first_own = jnp.concatenate(
@@ -811,17 +879,17 @@
         )
         up_spec = pl.BlockSpec((width, step), lambda c: (0, c))
         down_spec = pl.BlockSpec((step, width), lambda c: (c, 0))
-    chip_up = after(chip_up.reshape(up_rows, width), inputs)
+    chip_up = after(chip_up, inputs)
     up_all = lax.all_gather(chip_up, "chip", axis=0, tiled=True)
     up_all = up_all.reshape(n_chip, up_rows, width)
 
-    grad_all = share(after(out_grad, inputs), "expert").reshape(group, width)
+    grad_all = swap(after(grad_copies, inputs), "expert").reshape(group, width)
 
     qkv, attn_input, qkv_matrix = enter(inputs, gain_one, first_parts)
     doc_split = doc_lengths[0, :1]
-    attended_own = attend(qkv, doc_split, head_cols)
+    attended_own = attend(qkv, doc_split, head_cols, n_exp)
     attended_own, grad_all = lax.optimization_barrier((attended_own, grad_all))
-    attended_all = share(attended_own, "expert")
+    attended_all = swap(attended_own, "expert")
     same = (choice[:, :, None] == choice[:, None, :]).astype(jnp.int32)
     earlier = jnp.arange(rows)[None, None, :] < jnp.arange(rows)[None, :, None]
     rank = jnp.sum(jnp.where(earlier, same, 0), axis=2)
@@ -838,12 +906,25 @@
         ex_line, ffn_input, grad_all, coeffs, weights, specs, dense_cols, rows
     )
     arrived = swap(payload, "expert")
-    own_rows = pick_rows(slot, ffn_input, grad_all, coeffs, capacity)
-    own_rows = after(own_rows, payload)
-    up_part, down_part = dense_grad(ffn_input, ddense, dense_act, dense_dpre)
-    got_rows, up_part, down_part = lax.optimization_barrier(
-        (other_core(own_rows), up_part, down_part)
-    )
+    own_rows = pick_rows(after(slot, payload), ffn_input, grad_all, coeffs, capacity)
+    joined = dense_cols == width and dense_rows == block and step == 2 * block
+    if joined:
+        shape = (n_chip, 2, block, width)
+        grads = dense_split(core_line, ffn_input, ddense, dense_act, dense_dpre, shape)
+    else:
+        grads = dense_grad(ffn_input, ddense, dense_act, dense_dpre)
+    got_rows, *grads = lax.optimization_barrier((other_core(own_rows), *grads))
+    if joined:
+        dense_core = (grads[0].astype(F32) + other_core(grads[1]).astype(F32)).astype(BF16)
+        got_rows, dense_core = lax.optimization_barrier((got_rows, dense_core))
+        dense_sum = lax.psum_scatter(
+            dense_core.reshape(-1, width), "chip", scatter_dimension=0, tiled=True
+        )
+        up_sum, down_sum = (dense_sum[:block], dense_sum[block:])
+    else:
+        up_sum, down_sum = (
+            lax.psum_scatter(g, DP, scatter_dimension=0, tiled=True) for g in grads
+        )
     exp_keep, exp_send, exp_act, exp_dpre = expert_ffn(
         own_rows, got_rows, up_all, down_all, pair_rows
     )
@@ -853,7 +934,9 @@
         low = lax.rem(ex + k, n_exp) * share_cap
         piece = [lax.dynamic_slice_in_dim(v, low, share_cap, 1) for v in (exp_keep, exp_back)]
         returned.append((piece[0] + piece[1].astype(F32)).astype(BF16))
-    exp_grads = expert_grad(own_rows, got_rows, exp_act, exp_dpre, n_chip)
+    exp_grads = expert_grad(
+        own_rows, got_rows, exp_act, exp_dpre, n_chip
+    )
     arrived, exp_grads, *returned = lax.optimization_barrier((arrived, exp_grads, *returned))
     returned = turn_all(returned)
     exp_sum = lax.psum_scatter(
@@ -865,11 +948,7 @@
 
     middle_own, coeffs_own = (mine(middle), mine(coeffs))
     att_own = lax.dynamic_slice_in_dim(attended_all, ex * rows, rows, 1)
-    up_core = sum_core(up_part.reshape(n_chip, n_core, block, dense_cols), core)
-    down_core = sum_core(down_part.reshape(n_chip, n_core, dense_rows, width), core)
-    returned[0] = after(returned[0], middle_own, coeffs_own, att_own, up_core, down_core)
-    dense_fold = Fold((up_core, down_core))
-    dense_fold.send()
+    returned[0] = after(returned[0], middle_own, coeffs_own, att_own)
     dmiddle, dmid_low, datt, small_two, out_base = middle_back(
         ex_line,
         arrived,
@@ -884,40 +963,37 @@
         head_cols,
     )
     dattended = swap(datt, "expert")
+    out_keep, out_send = scalar_call(
+        out_grad_body,
+        [shape_of((n_chip, block, width), BF16)] * 2,
+        core_line,
+        [att_own, dmid_low],
+    )
+    dattended, out_keep, out_send = lax.optimization_barrier((dattended, out_keep, out_send))
     dattended = dattended.reshape(group, head_cols)
-    (dattended,) = dense_fold.meet(dattended)
     out_sums = turn_all([after(piece, dattended) for piece in out_parts])
 
     dparts = attend_back(qkv, dattended, doc_split, head_cols)
-    *dattn_parts, small_one = attn_input_back(ex_line, dparts, qkv_matrix, inputs, rows)
-    while dense_fold.orders[0]:
-        dense_fold.send()
-        met = dense_fold.meet(*dattn_parts, *out_sums)
-        dattn_parts, out_sums = (met[:n_exp], met[n_exp:])
-    up_sum, down_sum = dense_fold.pair
+    qkv_shape = shape_of((n_chip, block + PAD, qkv_cols), BF16)
+    qkv_keep, qkv_send = scalar_call(
+        qkv_grad_body,
+        [qkv_shape] * 2,
+        core_line,
+        [attn_input, qkv_matrix, gain_one, small_two] + list(dparts),
+    )
+    dparts = [after(dparts[0], qkv_keep), dparts[1], dparts[2]]
+    dattn_parts = scalar_call(
+        attn_input_back_body,
+        [shape_of((rows, width), BF16)] * n_exp,
+        ex_line,
+        dparts + [qkv_matrix],
+    )
+    met = lax.optimization_barrier((*dattn_parts, *out_sums))
+    dattn_parts, out_sums = (met[:n_exp], met[n_exp:])
     dattn = turn_all(dattn_parts)
-    out_weight = simple(
-        out_grad_body,
-        0,
-        shape_of((width, width), BF16),
-        [after(att_own, dparts[0]), dmid_low],
-    )
-    out_core = sum_core(out_weight.reshape(n_chip, n_core, block, width), core)
-    qkv_part = simple(
-        qkv_grad_body,
-        20,
-        shape_of((width, qkv_cols), BF16),
-        [after(attn_input, dattn_parts[0])] + list(dparts),
-    )
-    small_sum = (small_one + small_two).astype(BF16).reshape(8, n_dp, block).transpose(1, 0, 2)
-    qkv_part = jnp.concatenate(
-        [
-            qkv_part.reshape(n_dp, block, qkv_cols),
-            jnp.pad(small_sum, ((0, 0), (0, 0), (0, qkv_cols - block))),
-        ],
-        axis=1,
-    )
-    qkv_core = sum_core(qkv_part.reshape(n_chip, n_core, block + 8, qkv_cols), core)
+    qkv_send = after(qkv_send, dattn_parts[0])
+    qkv_core = qkv_keep.astype(F32) + other_core(qkv_send).astype(F32)
+    out_core = out_keep.astype(F32) + other_core(out_send).astype(F32)
     fold = Fold((out_core, qkv_core))
     fold.send()
     dattn = fold.meet(*dattn)
@@ -935,7 +1011,7 @@
             qkv_sum[:block].reshape(n_exp, w_rows, qkv_cols),
             out_weight_sum.reshape(n_exp, w_rows, width),
             small_sum,
-            up_sum.reshape(n_exp, w_rows, dense_cols),
+            up_sum.astype(F32).reshape(n_exp, w_rows, dense_cols),
         ],
         axis=2,
     ).astype(BF16)
@@ -947,12 +1023,14 @@
 
     exp_sum = after(exp_sum, tail_sent)
     up_exp_sum = exp_sum[:up_rows].reshape(n_block, n_core, exp_rows, width)
-    own_exp, sent_exp = by_core(core, up_exp_sum[:, 0], up_exp_sum[:, 1])
-    halves = jnp.stack(by_core(core, own_exp, other_core(sent_exp)))
-    exp_up_grad = halves.transpose(2, 0, 1, 3).reshape(exp_rows, n_core, n_chip, exp_cols)
-    exp_up_grad = exp_up_grad.transpose(0, 2, 1, 3).reshape(1, exp_rows, n_dp * exp_cols)
-    exp_up_grad = exp_up_grad.astype(F32)
-    exp_down_grad = exp_sum[up_rows:].astype(F32)[None]
+    own_exp = lax.dynamic_index_in_dim(up_exp_sum, core, 1, False)
+    sent_exp = lax.dynamic_index_in_dim(up_exp_sum, 1 - core, 1, False)
+    exp_up_grad, exp_down_grad = scalar_call(
+        expert_end_body,
+        [shape_of((exp_rows, n_dp * exp_cols), F32), shape_of((exp_cols, width), F32)],
+        core_line,
+        [own_exp, other_core(sent_exp), exp_sum[up_rows:]],
+    )
     tail = after(tail, exp_up_grad, exp_down_grad, tokens_grad, out_total, down_sum)
     up_grad = tail[:, :, qkv_cols + width + LANES :].reshape(n_exp, w_rows, n_dp, dense_rows)
     up_grad = up_grad.transpose(1, 2, 0, 3).reshape(w_rows, n_exp * dense_cols).astype(F32)
@@ -967,9 +1045,9 @@
         small_sum[1],
         small_sum[2:4].T,
         up_grad,
-        down_sum,
-        exp_up_grad,
-        exp_down_grad,
+        down_sum.astype(F32),
+        exp_up_grad[None],
+        exp_down_grad[None],
     )
 
 

time: 370 us -> 349 us (0.943); the launches traced: 363 us -> 347 us
  waiting for transfers between devices: 79.4 us -> 118 us
  blocking collectives: 56.6 us -> 27.7 us
  other arithmetic: 31.4 us -> 14.5 us
  local copies, waits for them, and re-layouts: 37.5 us -> 29.5 us
  starting transfers between devices: 55.2 us -> 51.1 us
    all_to_all x1 -> x0, blocking collectives: 26.2 us -> none  [swap(): return lax.all_to_all(values, axis, split_axis=0, concat_axis=0, tiled=True)]
    all_to_all x6 -> x7, waiting for transfers between devices: 49.6 us -> 64.8 us  [swap(): return lax.all_to_all(values, axis, split_axis=0, concat_axis=0, tiled=True)]
    all_gather x1, waiting for transfers between devices: 0.01 us -> 7.94 us  [shards(): dense_all = lax.all_gather(dense_pack, DP, axis=0, tiled=True)]
    ppermute x8 -> x4, waiting for transfers between devices: 5.52 us -> 12.2 us  [flip(): return lax.ppermute(values, 'chip', [(i, i ^ bit) for i in chips])]
    add x4 -> x2, other arithmetic: 6.52 us -> 0.62 us  [the longest x1 0.4 us: shards(): out_core = out_keep.astype(F32) + other_core(out_send).astype(F32)]
    convert_element_type x1 -> x2, other arithmetic: 0.14 us -> 5.81 us  [the longest x1 3.91 us: shards(): (grads[0].astype(F32) + other_core(grads[1]).astype(F32)).astype(BF16)]
    ppermute x9, waiting for transfers between devices: 21.9 us -> 27 us  [turn(): lax.ppermute(values, 'expert', [(i, (i + step) % count) for i in range(co...]
    ppermute x8 -> x4, starting transfers between devices: 9.79 us -> 5.04 us  [flip(): return lax.ppermute(values, 'chip', [(i, i ^ bit) for i in chips])]
  transfers between devices with their start and end apart: 35 -> 32, of which waited for: 10 -> 16; matrix products, arithmetic and copies ran while one was open for 15% -> 9% of each run, Pallas kernels for 24% -> 27%
where the time goes in v1:
time: 349 us; the launch traced here: 347 us
  waiting for transfers between devices  118 us (34%)
  Pallas kernels  92.1 us (26%)
  starting transfers between devices  51.1 us (15%)
  local copies, waits for them, and re-layouts  29.5 us (8%)
  blocking collectives  27.7 us (8%)
  other arithmetic  14.5 us (4%)
  between operations  14.4 us (4%)
    pallas_call x15, Pallas kernels, call(): pl.pallas_call(body, grid=grid, in_specs=in_specs, out_specs=out_specs, o...  92.1 us
    all_to_all x7, waiting for transfers between devices, swap(): return lax.all_to_all(values, axis, split_axis=0, concat_axis=0, tiled=True)  64.8 us
    all_to_all x7, starting transfers between devices, swap(): return lax.all_to_all(values, axis, split_axis=0, concat_axis=0, tiled=True)  31.6 us
    all_gather x2, blocking collectives, gather_small(): lax.all_gather(values[k:k + step], axes, axis=0, tiled=True)  27.7 us
    ppermute x9, waiting for transfers between devices, turn(): lax.ppermute(values, 'expert', [(i, (i + step) % count) for i in range(co...  27 us
    ppermute x9, starting transfers between devices, turn(): lax.ppermute(values, 'expert', [(i, (i + step) % count) for i in range(co...  12.4 us
    ppermute x4, waiting for transfers between devices, flip(): return lax.ppermute(values, 'chip', [(i, i ^ bit) for i in chips])  12.2 us
    all_gather x1, waiting for transfers between devices, shards(): dense_all = lax.all_gather(dense_pack, DP, axis=0, tiled=True)  7.94 us
  transfers between devices with their start and end apart: 32, of which 16 were waited for; matrix products, arithmetic and copies ran while one was open for 9% of the time, Pallas kernels for 27%

profile of v1, /device:TPU:0, one launch (start us, length us, event | category | flops | bytes accessed | tf_op | source)
XLA Modules:
  0.0 347.4 jit_solution(11343366922332380792)
XLA Ops:
  11.7 6.2 %all-to-all-start = ((bf16[4,32,3072]{2,1,0:T(8,128)(2,1)}), bf16[4,32,3072]{2,1,0:T(8,128)(2,1)S(1)}, u32[]{:S(2)}, u32[]{:S(2)}) async-start(bf16[4,32,3072]{2,1,0:T(8,128)(2,1)} %pad_maximum_fusion.1), calls=%async_computation | async-start | bytes 1572864 | tf_op jit(solution)/shard_map/all_to_all | solution.py:59
  19.5 18.8 %all-to-all-done = bf16[4,32,3072]{2,1,0:T(8,128)(2,1)S(1)} async-done(((bf16[4,32,3072]{2,1,0:T(8,128)(2,1)}), bf16[4,32,3072]{2,1,0:T(8,128)(2,1)S(1)}, u32[]{:S(2)}, u32[]{:S(2)}) %all-to-all-start) | async-done | bytes 786464 | tf_op jit(solution)/shard_map/all_to_all | solution.py:59
  45.4 13.9 %all_gather.16 = bf16[448,768]{1,0:T(8,128)(2,1)S(1)} all-gather(bf16[56,768]{1,0:T(8,128)(2,1)S(1)} %fusion.12), channel_id=1, replica_groups=mesh['chip'=4,'core'=2,'expert'=4] {'chip','core'}, dimensions={0}, use_global_device_ids=true | all-gather | bytes 774144 | tf_op jit(solution)/shard_map/all_gather | solution.py:104
  59.3 13.8 %all_gather.15 = bf16[640,768]{1,0:T(8,128)(2,1)} all-gather(bf16[80,768]{1,0:T(8,128)(2,1)S(1)} %slice.166), channel_id=1, replica_groups=mesh['chip'=4,'core'=2,'expert'=4] {'chip','core'}, dimensions={0}, use_global_device_ids=true | all-gather | bytes 1105920 | tf_op jit(solution)/shard_map/all_gather | solution.py:104
  74.7 4.6 %all-to-all-start.2 = ((bf16[4,128,1024]{2,1,0:T(8,128)(2,1)}), bf16[4,128,1024]{2,1,0:T(8,128)(2,1)S(1)}, u32[]{:S(2)}, u32[]{:S(2)}) async-start(bf16[4,128,1024]{2,1,0:T(8,128)(2,1)} %broadcast_in_dim.54), calls=%async_computation.2 | async-start | bytes 2097152 | tf_op jit(solution)/shard_map/all_to_all | solution.py:59
  79.3 4.5 %shard_map.212 = (bf16[512,768]{1,0:T(8,128)(2,1)}, bf16[512,1024]{1,0:T(8,128)(2,1)}, bf16[1024,768]{1,0:T(8,128)(2,1)}) custom-call(bf16[512,1024]{1,0:T(8,128)(2,1)} %bitcast.135, f32[1,1024]{1,0:T(1,128)} %get-tuple-element.212.gain_ref, bf16[8,80,768]{2,1,0:T(8,128)(2,1)} %bitcast.146, bf16[8,56,768]{2,1,0:T(8,128)(2,1)} %bitcast.148), custom_call_target="tpu_custom_call" | custom-call | tf_op jit(solution)/shard_map/pallas_call | solution.py:154
  83.9 6.1 %shard_map.213 = bf16[4,512,256]{2,1,0:T(8,128)(2,1)} custom-call(s32[1]{0:T(128)} %bitcast.166, bf16[512,768]{1,0:T(8,128)(2,1)} %get-tuple-element.106.q_ref.k_ref.v_ref, bf16[512,768]{1,0:T(8,128)(2,1)} %get-tuple-element.106.q_ref.k_ref.v_ref, bf16[512,768]{1,0:T(8,128)(2,1)} %get-tuple-element.106.q_ref.k_ref.v_ref), custom_call_target="tpu_custom_call" | custom-call | tf_op jit(solution)/shard_map/pallas_call | solution.py:154
  89.9 15.6 %all-to-all-done.2 = bf16[4,128,1024]{2,1,0:T(8,128)(2,1)S(1)} async-done(((bf16[4,128,1024]{2,1,0:T(8,128)(2,1)}), bf16[4,128,1024]{2,1,0:T(8,128)(2,1)S(1)}, u32[]{:S(2)}, u32[]{:S(2)}) %all-to-all-start.2) | async-done | bytes 1048608 | tf_op jit(solution)/shard_map/all_to_all | solution.py:59
  111.5 7.9 %all-gather.5.cloned.1.call-done = bf16[3072,1024]{1,0:T(8,128)(2,1)} async-done(((bf16[384,1024]{1,0:T(8,128)(2,1)}), bf16[3072,1024]{1,0:T(8,128)(2,1)}) %all-gather.5.cloned.1.call-update) | async-done | bytes 6291472 | tf_op jit(solution)/shard_map/all_gather | solution.py:870
  122.5 11.9 %all-to-all-done.3.att_ref = bf16[4,512,256]{2,1,0:T(8,128)(2,1)S(1)} async-done(((bf16[4,512,256]{2,1,0:T(8,128)(2,1)}), bf16[4,512,256]{2,1,0:T(8,128)(2,1)S(1)}, u32[]{:S(2)}, u32[]{:S(2)}) %all-to-all-start.3) | async-done | bytes 1048608 | tf_op jit(solution)/shard_map/all_to_all | solution.py:59
  135.4 5.7 %shard_map.214 = (f32[512,1024]{1,0:T(8,128)}, bf16[512,1024]{1,0:T(8,128)(2,1)}, f32[512,2]{1,0:T(8,128)}) custom-call(bf16[4,512,256]{2,1,0:T(8,128)(2,1)} %copy-done.3, bf16[512,1024]{1,0:T(8,128)(2,1)} %bitcast.136, bf16[1024,1024]{1,0:T(8,128)(2,1)} %bitcast.131, f32[1,1024]{1,0:T(1,128)} %get-tuple-element.211.gain_ref, bf16[16,1024]{1,0:T(8,128)(2,1)} %pad.24.mix_ref), custom_call_target="tpu_custom_call" | custom-call | tf_op jit(solution)/shard_map/pallas_call | solution.py:154
  141.1 12.9 %shard_map.215 = (bf16[128,1024]{1,0:T(8,128)(2,1)}, bf16[128,1024]{1,0:T(8,128)(2,1)}, bf16[128,1024]{1,0:T(8,128)(2,1)}, bf16[128,1024]{1,0:T(8,128)(2,1)}, bf...) custom-call(s32[1]{0:T(128)} %bitcast.ex_ref, ...), custom_call_target="tpu_custom_call" | custom-call | tf_op jit(solution)/shard_map/pallas_call | solution.py:154
  157.0 7.2 %shard_map.217 = (bf16[4,2,128,1024]{3,2,1,0:T(8,128)(2,1)}, bf16[4,2,128,1024]{3,2,1,0:T(8,128)(2,1)}) custom-call(s32[1]{0:T(128)} %bitcast.35.core_ref, bf16[512,1024]{1,0:T(8,128)(2,1)} %get-tuple-element.113.x_ref.ffn_ref, bf16[512,1024]{1,0:T(8,128)(2,1)} %get-tuple-element.118.g_ref, bf16[512,1024]{1,0:T(8,128)(2,1)} %get-tuple-element.119.act_ref, ...), custom_call_target="tpu_custom_call" | custom-call | tf_op jit(solution)/shard_map/pallas_call | solution.py:154
  164.7 4.0 %collective-permute-done.2 = bf16[4,2,128,1024]{3,2,1,0:T(8,128)(2,1)S(1)} collective-permute-done((bf16[4,2,128,1024]{3,2,1,0:T(8,128)(2,1)}, bf16[4,2,128,1024]{3,2,1,0:T(8,128)(2,1)S(1)}, u32[]{:S(2)}, u32[]{:S(2)}) %collective-permute-start.2) | collective-permute-done | bytes 2097184 | tf_op jit(solution)/shard_map/ppermute | solution.py:77
  168.7 3.9 %add_convert_fusion = bf16[4,2,128,1024]{3,2,1,0:T(8,128)(2,1)} fusion(bf16[4,2,128,1024]{3,2,1,0:T(8,128)(2,1)S(1)} %collective-permute-done.2, bf16[4,2,128,1024]{3,2,1,0:T(8,128)(2,1)} %get-tuple-element.124), kind=kLoop, calls=%fused_computation | loop fusion | flops 4194304 | bytes 6291456 | tf_op jit(solution)/shard_map/convert_element_type | solution.py:918
  176.5 12.4 %shard_map.218 = (f32[2,160,1024]{2,1,0:T(8,128)}, bf16[2,160,1024]{2,1,0:T(8,128)(2,1)}, bf16[320,2048]{1,0:T(8,128)(2,1)}, bf16[320,2048]{1,0:T(8,128)(2,1)}) custom-call(bf16[2,160,1024]{2,1,0:T(8,128)(2,1)} %shard_map.216.own_ref.own_x.own_g, bf16[2,160,1024]{2,1,0:T(8,128)(2,1)} %copy-done.2, bf16[4,512,1024]{2,1,0:T(8,128)(2,1)} %bitcast.141, ...), custom_call_target="tpu_custom_call" | custom-call | tf_op jit(solution)/shard_map/pallas_call | solution.py:154
  189.2 8.7 %shard_map.219 = bf16[4,1024,1024]{2,1,0:T(8,128)(2,1)} custom-call(bf16[2,160,1024]{2,1,0:T(8,128)(2,1)} %shard_map.216.own_ref.own_x.own_g, bf16[2,160,1024]{2,1,0:T(8,128)(2,1)} %copy-done.2, bf16[2,160,1024]{2,1,0:T(8,128)(2,1)} %shard_map.216.own_ref.own_x.own_g, bf16[2,160,1024]{2,1,0:T(8,128)(2,1)} %copy-done.2, ...), custom_call_target="tpu_custom_call" | custom-call | tf_op jit(solution)/shard_map/pallas_call | solution.py:154
  198.9 6.6 %all-to-all-done.4.pay_ref = bf16[4,144,1024]{2,1,0:T(8,128)(2,1)S(1)} async-done(((bf16[4,144,1024]{2,1,0:T(8,128)(2,1)}), bf16[4,144,1024]{2,1,0:T(8,128)(2,1)S(1)}, u32[]{:S(2)}, u32[]{:S(2)}) %all-to-all-start.4) | async-done | bytes 1179680 | tf_op jit(solution)/shard_map/all_to_all | solution.py:59
  218.0 5.6 %collective-permute-done.5.refs_2_ = bf16[2,40,1024]{2,1,0:T(8,128)(2,1)S(1)} collective-permute-done((bf16[2,40,1024]{2,1,0:T(8,128)(2,1)S(1)}, bf16[2,40,1024]{2,1,0:T(8,128)(2,1)S(1)}, u32[]{:S(2)}, u32[]{:S(2)}) %collective-permute-start.5) | collective-permute-done | bytes 163872 | tf_op jit(solution)/shard_map/ppermute | solution.py:69
  225.0 5.4 %shard_map.220 = (f32[128,1024]{1,0:T(8,128)}, bf16[128,1024]{1,0:T(8,128)(2,1)}, bf16[4,128,256]{2,1,0:T(8,128)(2,1)}, f32[8,1024]{1,0:T(8,128)}, f32[128,1024]{1,0:T(8,128)}) custom-call(s32[1]{0:T(128)} %bitcast.ex_ref, bf16[4,144,1024]{2,1,0:T(8,128)(2,1)} %copy-done.4, s32[128,1]{1,0:T(8,128)} %copy.93.slot_ref, ...), custom_call_target="tpu_custom_call" | custom-call | tf_op jit(solution)/shard_map/pallas_call | solution.py:154
  230.4 3.7 %all-to-all-start.5 = ((bf16[4,128,256]{2,1,0:T(8,128)(2,1)}), bf16[4,128,256]{2,1,0:T(8,128)(2,1)S(1)}, u32[]{:S(2)}, u32[]{:S(2)}) async-start(bf16[4,128,256]{2,1,0:T(8,128)(2,1)} %get-tuple-element.142), calls=%async_computation.5 | async-start | bytes 524288 | tf_op jit(solution)/shard_map/all_to_all | solution.py:59
  237.2 5.1 %all-to-all-done.5 = bf16[4,128,256]{2,1,0:T(8,128)(2,1)S(1)} async-done(((bf16[4,128,256]{2,1,0:T(8,128)(2,1)}), bf16[4,128,256]{2,1,0:T(8,128)(2,1)S(1)}, u32[]{:S(2)}, u32[]{:S(2)}) %all-to-all-start.5) | async-done | bytes 262176 | tf_op jit(solution)/shard_map/all_to_all | solution.py:59
  244.9 7.5 %shard_map.222 = (bf16[512,256]{1,0:T(8,128)(2,1)}, bf16[512,256]{1,0:T(8,128)(2,1)}, bf16[512,256]{1,0:T(8,128)(2,1)}) custom-call(s32[1]{0:T(128)} %bitcast.167, bf16[512,768]{1,0:T(8,128)(2,1)} %get-tuple-element.106.q_ref.k_ref.v_ref, bf16[512,768]{1,0:T(8,128)(2,1)} %get-tuple-element.106.q_ref.k_ref.v_ref, ...), custom_call_target="tpu_custom_call" | custom-call | flops 23000000512 | tf_op jit(solution)/shard_map/pallas_call | solution.py:154
  252.4 4.7 %shard_map.223 = (bf16[4,144,768]{2,1,0:T(8,128)(2,1)}, bf16[4,144,768]{2,1,0:T(8,128)(2,1)}) custom-call(s32[1]{0:T(128)} %bitcast.35.core_ref, bf16[512,1024]{1,0:T(8,128)(2,1)} %get-tuple-element.148.x_ref, bf16[1024,768]{1,0:T(8,128)(2,1)} %get-tuple-element.149.w_ref, f32[1,1024]{1,0:T(1,128)} %get-tuple-element.212.gain_ref, ...), custom_call_target="tpu_custom_call" | custom-call | tf_op jit(solution)/shard_map/pallas_call | solution.py:154
  257.1 4.6 %shard_map.224 = (bf16[128,1024]{1,0:T(8,128)(2,1)}, bf16[128,1024]{1,0:T(8,128)(2,1)}, bf16[128,1024]{1,0:T(8,128)(2,1)}, bf16[128,1024]{1,0:T(8,128)(2,1)}) custom-call(s32[1]{0:T(128)} %bitcast.ex_ref, bf16[512,256]{1,0:T(8,128)(2,1)} %get-tuple-element.154.dq_ref, bf16[512,256]{1,0:T(8,128)(2,1)} %get-tuple-element.151.dk_ref, ...), custom_call_target="tpu_custom_call" | custom-call | tf_op jit(solution)/shard_map/pallas_call | solution.py:154
  261.7 4.4 %collective-permute-done.8 = bf16[128,1024]{1,0:T(8,128)(2,1)S(1)} collective-permute-done((bf16[128,1024]{1,0:T(8,128)(2,1)S(1)}, bf16[128,1024]{1,0:T(8,128)(2,1)S(1)}, u32[]{:S(2)}, u32[]{:S(2)}) %collective-permute-start.8) | collective-permute-done | bytes 262176 | tf_op jit(solution)/shard_map/ppermute | solution.py:69
  277.4 5.0 %collective-permute-done.14.refs_1_ = bf16[128,1024]{1,0:T(8,128)(2,1)S(1)} collective-permute-done((bf16[128,1024]{1,0:T(8,128)(2,1)S(1)}, bf16[128,1024]{1,0:T(8,128)(2,1)S(1)}, u32[]{:S(2)}, u32[]{:S(2)}) %collective-permute-start.14) | collective-permute-done | bytes 262176 | tf_op jit(solution)/shard_map/ppermute | solution.py:69
  282.4 10.1 %collective-permute-done.15.refs_2_ = bf16[128,1024]{1,0:T(8,128)(2,1)S(1)} collective-permute-done((bf16[128,1024]{1,0:T(8,128)(2,1)S(1)}, bf16[128,1024]{1,0:T(8,128)(2,1)S(1)}, u32[]{:S(2)}, u32[]{:S(2)}) %collective-permute-start.15) | collective-permute-done | bytes 262176 | tf_op jit(solution)/shard_map/ppermute | solution.py:69
  295.6 11.2 %collective-permute-done.18 = bf16[144,768]{1,0:T(8,128)(2,1)S(1)} collective-permute-done((bf16[144,768]{1,0:T(8,128)(2,1)S(1)}, bf16[144,768]{1,0:T(8,128)(2,1)S(1)}, u32[]{:S(2)}, u32[]{:S(2)}) %collective-permute-start.18) | collective-permute-done | bytes 221216 | tf_op jit(solution)/shard_map/ppermute | solution.py:86
  311.0 6.3 %all-to-all-start.6 = ((bf16[4,32,2944]{2,1,0:T(8,128)(2,1)}), bf16[4,32,2944]{2,1,0:T(8,128)(2,1)S(1)}, u32[]{:S(2)}, u32[]{:S(2)}) async-start(bf16[4,32,2944]{2,1,0:T(8,128)(2,1)} %fusion.4), calls=%async_computation.7 | async-start | bytes 1507328 | tf_op jit(solution)/shard_map/all_to_all | solution.py:59
  325.7 3.8 %shard_map.226 = (f32[128,4096]{1,0:T(8,128)}, f32[512,1024]{1,0:T(8,128)}) custom-call(s32[1]{0:T(128)} %bitcast.35.core_ref, bf16[2,128,1024]{2,1,0:T(8,128)(2,1)} %get-tuple-element.202.own_ref, bf16[2,128,1024]{2,1,0:T(8,128)(2,1)} %copy-done.13, bf16[512,1024]{1,0:T(8,128)(2,1)} %get-tuple-element.195.down_ref), custom_call_target="tpu_custom_call" | custom-call | tf_op jit(solution)/shard_map/pallas_call | solution.py:154
  329.5 6.7 %all-to-all-done.6 = bf16[4,32,2944]{2,1,0:T(8,128)(2,1)S(1)} async-done(((bf16[4,32,2944]{2,1,0:T(8,128)(2,1)}), bf16[4,32,2944]{2,1,0:T(8,128)(2,1)S(1)}, u32[]{:S(2)}, u32[]{:S(2)}) %all-to-all-start.6) | async-done | bytes 753696 | tf_op jit(solution)/shard_map/all_to_all | solution.py:59
  (207 shorter events, 84.1 us)
Async XLA Ops:
  7.2 66.5 %all-gather.9.cloned.1.call-start = ((), (), s32[]{:S(2)}) async-start(), calls=%async_computation.13 | async-start | bytes 5242880 | tf_op jit(solution)/shard_map/all_gather | solution.py:819
  9.2 8.7 %collective-permute-start = (bf16[128,2048]{0,1:T(8,128)(2,1)S(1)}, bf16[128,2048]{0,1:T(8,128)(2,1)S(1)}, u32[]{:S(2)}, u32[]{:S(2)}) collective-permute-start(bf16[128,2048]{0,1:T(8,128)(2,1)S(1)} %bitcast.162), channel_id=1, source_target_pairs={{0,4},{4,0},{1,5},{5,1},{2,6},{6,2},{3,7},{7,3},{8,12},{12,8},{9,1... | collective-permute-start | bytes 1572872 | tf_op jit(solution)/shard_map/ppermute | solution.py:77
  11.7 26.6 %all-to-all-start = ((bf16[4,32,3072]{2,1,0:T(8,128)(2,1)}), bf16[4,32,3072]{2,1,0:T(8,128)(2,1)S(1)}, u32[]{:S(2)}, u32[]{:S(2)}) async-start(bf16[4,32,3072]{2,1,0:T(8,128)(2,1)} %pad_maximum_fusion.1), calls=%async_computation | async-start | bytes 1572864 | tf_op jit(solution)/shard_map/all_to_all | solution.py:59
  40.5 33.2 %all-to-all-start.1 = ((bf16[4,128,1024]{2,1,0:T(8,128)(2,1)}), bf16[4,128,1024]{2,1,0:T(8,128)(2,1)S(1)}, u32[]{:S(2)}, u32[]{:S(2)}) async-start(bf16[4,128,1024]{2,1,0:T(8,128)(2,1)} %broadcast_in_dim.55), calls=%async_computation.1 | async-start | bytes 2097152 | tf_op jit(solution)/shard_map/all_to_all | solution.py:59
  44.2 75.3 %all-gather.5.cloned.1.call-start = ((), (), s32[]{:S(2)}) async-start(), calls=%async_computation.9 | async-start | bytes 7077888 | tf_op jit(solution)/shard_map/all_gather | solution.py:870
  73.7 102.8 %all-gather.7.cloned.1.call-start = ((), (), s32[]{:S(2)}) async-start(), calls=%async_computation.10 | async-start | bytes 5242880 | tf_op jit(solution)/shard_map/all_gather | solution.py:883
  74.7 30.9 %all-to-all-start.2 = ((bf16[4,128,1024]{2,1,0:T(8,128)(2,1)}), bf16[4,128,1024]{2,1,0:T(8,128)(2,1)S(1)}, u32[]{:S(2)}, u32[]{:S(2)}) async-start(bf16[4,128,1024]{2,1,0:T(8,128)(2,1)} %broadcast_in_dim.54), calls=%async_computation.2 | async-start | bytes 2097152 | tf_op jit(solution)/shard_map/all_to_all | solution.py:59
  105.6 28.9 %all-to-all-start.3 = ((bf16[4,512,256]{2,1,0:T(8,128)(2,1)}), bf16[4,512,256]{2,1,0:T(8,128)(2,1)S(1)}, u32[]{:S(2)}, u32[]{:S(2)}) async-start(bf16[4,512,256]{2,1,0:T(8,128)(2,1)} %shard_map.213), calls=%async_computation.3 | async-start | bytes 2097152 | tf_op jit(solution)/shard_map/all_to_all | solution.py:59
  109.1 199.1 %reduce-scatter.3.cloned.1.call-start = ((), (), s32[]{:S(2)}) async-start(), calls=%async_computation.11 | async-start | bytes 2621440 | tf_op jit(solution)/shard_map/reduce_scatter | solution.py:920
  157.0 7.2 %collective-permute-start.1 = (bf16[2,160,1024]{2,1,0:T(8,128)(2,1)}, bf16[2,160,1024]{2,1,0:T(8,128)(2,1)S(1)}, u32[]{:S(2)}, u32[]{:S(2)}) collective-permute-start(bf16[2,160,1024]{2,1,0:T(8,128)(2,1)} %shard_map.216.own_ref.own_x.own_g), channel_id=1, source_target_pairs={{0,4},{4,0},{1,5},{5,1},{2,6},{6,2},{3,7},{7,3},{8,12},{12,8},{9,1... | collective-permute-start | bytes 1966088 | tf_op jit(solution)/shard_map/ppermute | solution.py:77
  164.2 4.6 %collective-permute-start.2 = (bf16[4,2,128,1024]{3,2,1,0:T(8,128)(2,1)}, bf16[4,2,128,1024]{3,2,1,0:T(8,128)(2,1)S(1)}, u32[]{:S(2)}, u32[]{:S(2)}) collective-permute-start(bf16[4,2,128,1024]{3,2,1,0:T(8,128)(2,1)} %get-tuple-element.125), channel_id=1, source_target_pairs={{0,4},{4,0},{1,5},{5,1},{2,6},{6,2},{3,7},{7,3},{8,12},{12,8},{9,1... | collective-permute-start | bytes 6291464 | tf_op jit(solution)/shard_map/ppermute | solution.py:77
  172.7 32.9 %all-to-all-start.4 = ((bf16[4,144,1024]{2,1,0:T(8,128)(2,1)}), bf16[4,144,1024]{2,1,0:T(8,128)(2,1)S(1)}, u32[]{:S(2)}, u32[]{:S(2)}) async-start(bf16[4,144,1024]{2,1,0:T(8,128)(2,1)} %get-tuple-element.116), calls=%async_computation.4 | async-start | bytes 2359296 | tf_op jit(solution)/shard_map/all_to_all | solution.py:59
  176.2 141.1 %reduce-scatter.5.cloned.1.call-start = ((), (), s32[]{:S(2)}) async-start(), calls=%async_computation.12 | async-start | bytes 10485760 | tf_op jit(solution)/shard_map/reduce_scatter | solution.py:942
  188.9 9.1 %collective-permute-start.3 = (bf16[2,160,1024]{2,1,0:T(8,128)(2,1)}, bf16[2,160,1024]{2,1,0:T(8,128)(2,1)S(1)}, u32[]{:S(2)}, u32[]{:S(2)}) collective-permute-start(bf16[2,160,1024]{2,1,0:T(8,128)(2,1)} %get-tuple-element.132), channel_id=1, source_target_pairs={{0,4},{4,0},{1,5},{5,1},{2,6},{6,2},{3,7},{7,3},{8,12},{12,8},{9,1... | collective-permute-start | bytes 1966088 | tf_op jit(solution)/shard_map/ppermute | solution.py:77
  209.0 9.0 %collective-permute-start.4 = (bf16[2,40,1024]{2,1,0:T(8,128)(2,1)S(1)}, bf16[2,40,1024]{2,1,0:T(8,128)(2,1)S(1)}, u32[]{:S(2)}, u32[]{:S(2)}) collective-permute-start(bf16[2,40,1024]{2,1,0:T(8,128)(2,1)S(1)} %copy-done.24), channel_id=1, source_target_pairs={{0,1},{1,2},{2,3},{3,0},{4,5},{5,6},{6,7},{7,4},{8,9},{9,10},{10,1... | collective-permute-start | bytes 491528 | tf_op jit(solution)/shard_map/ppermute | solution.py:69
  209.0 14.7 %collective-permute-start.5 = (bf16[2,40,1024]{2,1,0:T(8,128)(2,1)S(1)}, bf16[2,40,1024]{2,1,0:T(8,128)(2,1)S(1)}, u32[]{:S(2)}, u32[]{:S(2)}) collective-permute-start(bf16[2,40,1024]{2,1,0:T(8,128)(2,1)S(1)} %get-tuple-element.139), channel_id=1, source_target_pairs={{0,2},{1,3},{2,0},{3,1},{4,6},{5,7},{6,4},{7,5},{8,10},{9,11},{10,... | collective-permute-start | bytes 491528 | tf_op jit(solution)/shard_map/ppermute | solution.py:69
  211.0 12.7 %collective-permute-start.6 = (bf16[2,40,1024]{2,1,0:T(8,128)(2,1)S(1)}, bf16[2,40,1024]{2,1,0:T(8,128)(2,1)S(1)}, u32[]{:S(2)}, u32[]{:S(2)}) collective-permute-start(bf16[2,40,1024]{2,1,0:T(8,128)(2,1)S(1)} %get-tuple-element.140), channel_id=1, source_target_pairs={{0,3},{1,0},{2,1},{3,2},{4,7},{5,4},{6,5},{7,6},{8,11},{9,8},{10,9... | collective-permute-start | bytes 491528 | tf_op jit(solution)/shard_map/ppermute | solution.py:69
  230.4 11.9 %all-to-all-start.5 = ((bf16[4,128,256]{2,1,0:T(8,128)(2,1)}), bf16[4,128,256]{2,1,0:T(8,128)(2,1)S(1)}, u32[]{:S(2)}, u32[]{:S(2)}) async-start(bf16[4,128,256]{2,1,0:T(8,128)(2,1)} %get-tuple-element.142), calls=%async_computation.5 | async-start | bytes 524288 | tf_op jit(solution)/shard_map/all_to_all | solution.py:59
  242.4 19.3 %collective-permute-start.9 = (bf16[128,1024]{1,0:T(8,128)(2,1)}, bf16[128,1024]{1,0:T(8,128)(2,1)S(1)}, u32[]{:S(2)}, u32[]{:S(2)}) collective-permute-start(bf16[128,1024]{1,0:T(8,128)(2,1)} %get-tuple-element.166), channel_id=1, source_target_pairs={{0,3},{1,0},{2,1},{3,2},{4,7},{5,4},{6,5},{7,6},{8,11},{9,8},{10,9... | collective-permute-start | bytes 786440 | tf_op jit(solution)/shard_map/ppermute | solution.py:69
  244.2 21.9 %collective-permute-start.8 = (bf16[128,1024]{1,0:T(8,128)(2,1)S(1)}, bf16[128,1024]{1,0:T(8,128)(2,1)S(1)}, u32[]{:S(2)}, u32[]{:S(2)}) collective-permute-start(bf16[128,1024]{1,0:T(8,128)(2,1)S(1)} %copy-done.33), channel_id=1, source_target_pairs={{0,2},{1,3},{2,0},{3,1},{4,6},{5,7},{6,4},{7,5},{8,10},{9,11},{10,... | collective-permute-start | bytes 786440 | tf_op jit(solution)/shard_map/ppermute | solution.py:69
  244.2 21.9 %collective-permute-start.7 = (bf16[128,1024]{1,0:T(8,128)(2,1)S(1)}, bf16[128,1024]{1,0:T(8,128)(2,1)S(1)}, u32[]{:S(2)}, u32[]{:S(2)}) collective-permute-start(bf16[128,1024]{1,0:T(8,128)(2,1)S(1)} %copy-done.32), channel_id=1, source_target_pairs={{0,1},{1,2},{2,3},{3,0},{4,5},{5,6},{6,7},{7,4},{8,9},{9,10},{10,1... | collective-permute-start | bytes 786440 | tf_op jit(solution)/shard_map/ppermute | solution.py:69
  244.9 21.9 %collective-permute-start.10 = (bf16[4,128,1024]{2,1,0:T(8,128)(2,1)}, bf16[4,128,1024]{2,1,0:T(8,128)(2,1)S(1)}, u32[]{:S(2)}, u32[]{:S(2)}) collective-permute-start(bf16[4,128,1024]{2,1,0:T(8,128)(2,1)} %get-tuple-element.173), channel_id=1, source_target_pairs={{0,4},{4,0},{1,5},{5,1},{2,6},{6,2},{3,7},{7,3},{8,12},{12,8},{9,1... | collective-permute-start | bytes 3145736 | tf_op jit(solution)/shard_map/ppermute | solution.py:77
  266.8 2.6 collective-permute-start.12
  267.4 25.2 %collective-permute-start.11 = (bf16[2,128,1024]{2,1,0:T(8,128)(2,1)S(1)}, bf16[2,128,1024]{2,1,0:T(8,128)(2,1)S(1)}, u32[]{:S(2)}, u32[]{:S(2)}) collective-permute-start(bf16[2,128,1024]{2,1,0:T(8,128)(2,1)S(1)} %fusion.5), channel_id=1, source_target_pairs={{0,8},{8,0},{16,24},{24,16},{1,9},{9,1},{17,25},{25,17},{2,10},{10... | collective-permute-start | bytes 1572872 | tf_op jit(solution)/shard_map/ppermute | solution.py:86
  269.8 22.8 %collective-permute-start.13 = (bf16[2,144,768]{2,1,0:T(8,128)(2,1)S(1)}, bf16[2,144,768]{2,1,0:T(8,128)(2,1)S(1)}, u32[]{:S(2)}, u32[]{:S(2)}) collective-permute-start(bf16[2,144,768]{2,1,0:T(8,128)(2,1)S(1)} %select_convert_fusion), channel_id=1, source_target_pairs={{0,16},{8,24},{16,0},{24,8},{1,17},{9,25},{17,1},{25,9},{2,18},{10... | collective-permute-start | bytes 1327112 | tf_op jit(solution)/shard_map/ppermute | solution.py:86
  271.3 11.1 %collective-permute-start.14 = (bf16[128,1024]{1,0:T(8,128)(2,1)S(1)}, bf16[128,1024]{1,0:T(8,128)(2,1)S(1)}, u32[]{:S(2)}, u32[]{:S(2)}) collective-permute-start(bf16[128,1024]{1,0:T(8,128)(2,1)S(1)} %copy-done.36), channel_id=1, source_target_pairs={{0,1},{1,2},{2,3},{3,0},{4,5},{5,6},{6,7},{7,4},{8,9},{9,10},{10,1... | collective-permute-start | bytes 786440 | tf_op jit(solution)/shard_map/ppermute | solution.py:69
  272.6 20.0 %collective-permute-start.15 = (bf16[128,1024]{1,0:T(8,128)(2,1)S(1)}, bf16[128,1024]{1,0:T(8,128)(2,1)S(1)}, u32[]{:S(2)}, u32[]{:S(2)}) collective-permute-start(bf16[128,1024]{1,0:T(8,128)(2,1)S(1)} %copy-done.35), channel_id=1, source_target_pairs={{0,2},{1,3},{2,0},{3,1},{4,6},{5,7},{6,4},{7,5},{8,10},{9,11},{10,... | collective-permute-start | bytes 786440 | tf_op jit(solution)/shard_map/ppermute | solution.py:69
  274.6 18.0 %collective-permute-start.16 = (bf16[128,1024]{1,0:T(8,128)(2,1)S(1)}, bf16[128,1024]{1,0:T(8,128)(2,1)S(1)}, u32[]{:S(2)}, u32[]{:S(2)}) collective-permute-start(bf16[128,1024]{1,0:T(8,128)(2,1)S(1)} %copy-done.34), channel_id=1, source_target_pairs={{0,3},{1,0},{2,1},{3,2},{4,7},{5,4},{6,5},{7,6},{8,11},{9,8},{10,9... | collective-permute-start | bytes 786440 | tf_op jit(solution)/shard_map/ppermute | solution.py:69
  293.4 14.5 %collective-permute-start.17 = (bf16[128,1024]{1,0:T(8,128)(2,1)S(1)}, bf16[128,1024]{1,0:T(8,128)(2,1)S(1)}, u32[]{:S(2)}, u32[]{:S(2)}) collective-permute-start(bf16[128,1024]{1,0:T(8,128)(2,1)S(1)} %fusion.8), channel_id=1, source_target_pairs={{0,16},{8,24},{16,0},{24,8},{1,17},{9,25},{17,1},{25,9},{2,18},{10... | collective-permute-start | bytes 786440 | tf_op jit(solution)/shard_map/ppermute | solution.py:86
  294.2 12.6 %collective-permute-start.18 = (bf16[144,768]{1,0:T(8,128)(2,1)S(1)}, bf16[144,768]{1,0:T(8,128)(2,1)S(1)}, u32[]{:S(2)}, u32[]{:S(2)}) collective-permute-start(bf16[144,768]{1,0:T(8,128)(2,1)S(1)} %fusion.9), channel_id=1, source_target_pairs={{0,8},{8,0},{16,24},{24,16},{1,9},{9,1},{17,25},{25,17},{2,10},{10... | collective-permute-start | bytes 663560 | tf_op jit(solution)/shard_map/ppermute | solution.py:86
  311.0 25.1 %all-to-all-start.6 = ((bf16[4,32,2944]{2,1,0:T(8,128)(2,1)}), bf16[4,32,2944]{2,1,0:T(8,128)(2,1)S(1)}, u32[]{:S(2)}, u32[]{:S(2)}) async-start(bf16[4,32,2944]{2,1,0:T(8,128)(2,1)} %fusion.4), calls=%async_computation.7 | async-start | bytes 1507328 | tf_op jit(solution)/shard_map/all_to_all | solution.py:59
  320.9 4.0 %collective-permute-start.19 = (bf16[2,128,1024]{2,1,0:T(8,128)(2,1)S(1)}, bf16[2,128,1024]{2,1,0:T(8,128)(2,1)S(1)}, u32[]{:S(2)}, u32[]{:S(2)}) collective-permute-start(bf16[2,128,1024]{2,1,0:T(8,128)(2,1)S(1)} %get-tuple-element.201), channel_id=1, source_target_pairs={{0,4},{4,0},{1,5},{5,1},{2,6},{6,2},{3,7},{7,3},{8,12},{12,8},{9,1... | collective-permute-start | bytes 1572872 | tf_op jit(solution)/shard_map/ppermute | solution.py:77
  (38 other events, 209.4 us)
Sparse Core Ops, SparseCore 0:
  9.9 60.0 all-gather.8
  73.9 45.5 all-gather.4
  121.3 52.6 all-gather.6
  176.9 35.1 reduce-scatter.2
  215.3 96.2 reduce-scatter.4

commit v2 on v1

--- a/solution.py
+++ b/solution.py
@@ -114,13 +114,14 @@
 class Fold:
     def __init__(self, pair):
         bits = chip_bits()
-        self.orders = [list(bits), list(bits[::-1])]
-        self.left = [sorted(bits, reverse=True) for k in range(2)]
+        count = len(pair)
+        self.orders = [list(bits[:: 1 - 2 * (k % 2)]) for k in range(count)]
+        self.left = [sorted(bits, reverse=True) for k in range(count)]
         self.pair = [v.reshape((2,) * len(bits) + v.shape[1:]) for v in pair]
 
     def send(self):
         self.keeps, self.gots = ([], [])
-        for k in range(2):
+        for k in range(len(self.pair)):
             bit = self.orders[k].pop(0)
             at = self.left[k].index(bit)
             self.left[k].remove(bit)
@@ -133,9 +134,9 @@
         gots = lax.optimization_barrier((*self.gots, *others))
         self.pair = [
             keep.astype(F32) + got.astype(F32)
-            for keep, got in zip(self.keeps, gots[:2], strict=True)
+            for keep, got in zip(self.keeps, gots[: len(self.keeps)], strict=True)
         ]
-        return gots[2:]
+        return gots[len(self.keeps) :]
 
 
 def whole(shape):
@@ -338,28 +339,6 @@
         [by_rows(tile, width), by_rows(tile, width), by_rows(tile, 2)],
         grid=(group // tile,),
     )
-
-
-def pick_body(slot_ref, ffn_ref, grad_ref, coeff_ref, out_ref):
-    capacity = out_ref.shape[1]
-    shape = (capacity, ffn_ref.shape[0])
-    pick = (lax.broadcasted_iota(jnp.int32, shape, 0) == slot_ref[...]).astype(F32).astype(BF16)
-    dexpert = (coeff_ref[:, 1:2] * grad_ref[...].astype(F32)).astype(BF16)
-    out_ref[0] = dot(pick, ffn_ref[...]).astype(BF16)
-    out_ref[1] = dot(pick, dexpert).astype(BF16)
-
-
-def pick_rows(slot, ffn_input, grad, coeffs, capacity):
-    group, width = ffn_input.shape
-    operands = [slot.reshape(1, group), ffn_input, grad, coeffs]
-    return call(
-        pick_body,
-        0,
-        [shape_of((2, capacity, width), BF16)],
-        operands,
-        [whole(o.shape) for o in operands],
-        [whole((2, capacity, width))],
-    )[0]
 
 
 def bend(pre):
@@ -494,14 +473,20 @@
     )[0]
 
 
-def dense_body(ex_ref, x_ref, g_ref, coeff_ref, up_ref, down_ref, *refs):
-    outs, (pay_ref, act_ref, dpre_ref, ddense_ref, dense, dins) = (refs[:-6], refs[-6:])
+def dense_body(ex_ref, x_ref, g_ref, coeff_ref, slot_ref, up_ref, down_ref, *refs):
+    outs, (pay_ref, act_ref, dpre_ref, ddense_ref, own_ref, dense, dins) = (refs[:-7], refs[-7:])
     n_exp, padded, width = pay_ref.shape
     rows = padded - PAD
 
     @pl.when(pl.program_id(0) == 0)
     def begin():
-        ddense_ref[...] = (coeff_ref[:, 0:1] * g_ref[...].astype(F32)).astype(BF16)
+        grad = g_ref[...].astype(F32)
+        ddense_ref[...] = (coeff_ref[:, 0:1] * grad).astype(BF16)
+        shape = (own_ref.shape[1], x_ref.shape[0])
+        pick = (lax.broadcasted_iota(jnp.int32, shape, 0) == slot_ref[...]).astype(F32)
+        pick = pick.astype(BF16)
+        own_ref[0] = dot(pick, x_ref[...]).astype(BF16)
+        own_ref[1] = dot(pick, (coeff_ref[:, 1:2] * grad).astype(BF16)).astype(BF16)
 
     up = up_ref[...].reshape(width, -1)
     down = down_ref[...].reshape(-1, width)
@@ -533,11 +518,12 @@
     ddown_ref[...] = dot_lt(act_ref[...], g_ref[...]).astype(BF16)
 
 
-def dense_ffn(ex, ffn_input, grad, coeffs, weights, specs, hidden, rows):
+def dense_ffn(ex, ffn_input, grad, coeffs, slot, capacity, weights, specs, hidden, rows):
     group, width = ffn_input.shape
     step = 2 * LANES
     count = group // rows
-    operands = [ffn_input, grad, coeffs]
+    operands = [ffn_input, grad, coeffs, slot]
+    own = (2, capacity, width)
     padded = (count, rows + PAD, width)
     by_cols = pl.BlockSpec((group, step), lambda c: (0, c))
     return call(
@@ -546,11 +532,11 @@
         [shape_of((rows, width), BF16)] * count
         + [shape_of(padded, BF16)]
         + [shape_of((group, hidden), BF16)] * 2
-        + [shape_of((group, width), BF16)],
+        + [shape_of((group, width), BF16), shape_of(own, BF16)],
         [ex] + operands + weights,
         [pl.BlockSpec(memory_space=pltpu.SMEM)] + [whole(o.shape) for o in operands] + specs,
         [whole((rows, width))] * count
-        + [whole(padded), by_cols, by_cols, whole((group, width))],
+        + [whole(padded), by_cols, by_cols, whole((group, width)), whole(own)],
         grid=(hidden // step,),
         scratch=[pltpu.VMEM((group, width), F32)] * 2,
     )
@@ -902,11 +888,10 @@
 
 
     weights, specs = ([up_matrix, down_matrix], [up_spec, down_spec])
-    *out_parts, payload, dense_act, dense_dpre, ddense = dense_ffn(
-        ex_line, ffn_input, grad_all, coeffs, weights, specs, dense_cols, rows
+    *out_parts, payload, dense_act, dense_dpre, ddense, own_rows = dense_ffn(
+        ex_line, ffn_input, grad_all, coeffs, slot, capacity, weights, specs, dense_cols, rows
     )
     arrived = swap(payload, "expert")
-    own_rows = pick_rows(after(slot, payload), ffn_input, grad_all, coeffs, capacity)
     joined = dense_cols == width and dense_rows == block and step == 2 * block
     if joined:
         shape = (n_chip, 2, block, width)
@@ -972,6 +957,9 @@
     dattended, out_keep, out_send = lax.optimization_barrier((dattended, out_keep, out_send))
     dattended = dattended.reshape(group, head_cols)
     out_sums = turn_all([after(piece, dattended) for piece in out_parts])
+    out_core = out_keep.astype(F32) + other_core(out_send).astype(F32)
+    out_fold = Fold((out_core,))
+    out_fold.send()
 
     dparts = attend_back(qkv, dattended, doc_split, head_cols)
     qkv_shape = shape_of((n_chip, block + PAD, qkv_cols), BF16)
@@ -988,19 +976,25 @@
         ex_line,
         dparts + [qkv_matrix],
     )
-    met = lax.optimization_barrier((*dattn_parts, *out_sums))
+    met = out_fold.meet(*dattn_parts, *out_sums)
     dattn_parts, out_sums = (met[:n_exp], met[n_exp:])
     dattn = turn_all(dattn_parts)
     qkv_send = after(qkv_send, dattn_parts[0])
     qkv_core = qkv_keep.astype(F32) + other_core(qkv_send).astype(F32)
-    out_core = out_keep.astype(F32) + other_core(out_send).astype(F32)
-    fold = Fold((out_core, qkv_core))
+    half = qkv_cols // 2
+    halves = (qkv_core,)
+    if half % LANES == 0:
+        halves = (qkv_core[..., :half], qkv_core[..., half:])
+    fold = Fold(halves)
     fold.send()
+    while out_fold.orders[0]:
+        out_fold.send()
+        dattn = out_fold.meet(*dattn)
     dattn = fold.meet(*dattn)
     while fold.orders[0]:
         fold.send()
         fold.meet()
-    out_weight_sum, qkv_sum = fold.pair
+    out_weight_sum, qkv_sum = (out_fold.pair[0], jnp.concatenate(fold.pair, axis=-1))
     out_total = out_base
     for piece in out_sums:
         out_total = out_total + piece.astype(F32)

time: 349 us -> 346 us (level)
  waiting for transfers between devices: 118 us -> 114 us
    ppermute x9, waiting for transfers between devices: 27 us -> 23.2 us  [turn(): lax.ppermute(values, 'expert', [(i, (i + step) % count) for i in range(co...]
    ppermute x4 -> x6, starting transfers between devices: 5.04 us -> 7.74 us  [flip(): return lax.ppermute(values, 'chip', [(i, i ^ bit) for i in chips])]
    pallas_call x15 -> x14, Pallas kernels: 92.1 us -> 89.5 us  [call(): pl.pallas_call(body, grid=grid, in_specs=in_specs, out_specs=out_specs, o...]
    ppermute x4 -> x6, waiting for transfers between devices: 12.2 us -> 12.6 us  [flip(): return lax.ppermute(values, 'chip', [(i, i ^ bit) for i in chips])]
    unnamed x78 -> x68, local copies, waits for them, and re-layouts: 7.35 us -> 7.1 us
  transfers between devices with their start and end apart: 32 -> 34, of which waited for: 16 -> 19; matrix products, arithmetic and copies ran while one was open for 9% -> 10% of each run, Pallas kernels for 27% -> 26%
where the time goes in v2:
time: 346 us; the launch traced here: 345 us
  waiting for transfers between devices  114 us (33%)
  Pallas kernels  89.5 us (26%)
  starting transfers between devices  53.4 us (15%)
  local copies, waits for them, and re-layouts  29.3 us (8%)
  blocking collectives  27.7 us (8%)
  other arithmetic  17 us (5%)
  between operations  14.4 us (4%)
    pallas_call x14, Pallas kernels, call(): pl.pallas_call(body, grid=grid, in_specs=in_specs, out_specs=out_specs, o...  89.5 us
    all_to_all x7, waiting for transfers between devices, swap(): return lax.all_to_all(values, axis, split_axis=0, concat_axis=0, tiled=True)  63.4 us
    all_to_all x7, starting transfers between devices, swap(): return lax.all_to_all(values, axis, split_axis=0, concat_axis=0, tiled=True)  32.8 us
    all_gather x2, blocking collectives, gather_small(): lax.all_gather(values[k:k + step], axes, axis=0, tiled=True)  27.7 us
    ppermute x9, waiting for transfers between devices, turn(): lax.ppermute(values, 'expert', [(i, (i + step) % count) for i in range(co...  23.2 us
    ppermute x6, waiting for transfers between devices, flip(): return lax.ppermute(values, 'chip', [(i, i ^ bit) for i in chips])  12.6 us
    ppermute x9, starting transfers between devices, turn(): lax.ppermute(values, 'expert', [(i, (i + step) % count) for i in range(co...  10.7 us
    ppermute x6, starting transfers between devices, flip(): return lax.ppermute(values, 'chip', [(i, i ^ bit) for i in chips])  7.74 us
  transfers between devices with their start and end apart: 34, of which 19 were waited for; matrix products, arithmetic and copies ran while one was open for 10% of the time, Pallas kernels for 26%

profile of v2, /device:TPU:0, one launch (start us, length us, event | category | flops | bytes accessed | tf_op | source)
XLA Modules:
  0.0 344.9 jit_solution(9447581943786614182)
XLA Ops:
  11.7 6.2 %all-to-all-start = ((bf16[4,32,3072]{2,1,0:T(8,128)(2,1)}), bf16[4,32,3072]{2,1,0:T(8,128)(2,1)S(1)}, u32[]{:S(2)}, u32[]{:S(2)}) async-start(bf16[4,32,3072]{2,1,0:T(8,128)(2,1)} %pad_maximum_fusion.1), calls=%async_computation | async-start | bytes 1572864 | tf_op jit(solution)/shard_map/all_to_all | solution.py:59
  19.5 18.8 %all-to-all-done = bf16[4,32,3072]{2,1,0:T(8,128)(2,1)S(1)} async-done(((bf16[4,32,3072]{2,1,0:T(8,128)(2,1)}), bf16[4,32,3072]{2,1,0:T(8,128)(2,1)S(1)}, u32[]{:S(2)}, u32[]{:S(2)}) %all-to-all-start) | async-done | bytes 786464 | tf_op jit(solution)/shard_map/all_to_all | solution.py:59
  40.6 3.6 %all-to-all-start.1 = ((bf16[4,128,1024]{2,1,0:T(8,128)(2,1)}), bf16[4,128,1024]{2,1,0:T(8,128)(2,1)S(1)}, u32[]{:S(2)}, u32[]{:S(2)}) async-start(bf16[4,128,1024]{2,1,0:T(8,128)(2,1)} %broadcast_in_dim.55), calls=%async_computation.1 | async-start | bytes 2097152 | tf_op jit(solution)/shard_map/all_to_all | solution.py:59
  45.4 13.9 %all_gather.16 = bf16[448,768]{1,0:T(8,128)(2,1)S(1)} all-gather(bf16[56,768]{1,0:T(8,128)(2,1)S(1)} %fusion.15), channel_id=1, replica_groups=mesh['chip'=4,'core'=2,'expert'=4] {'chip','core'}, dimensions={0}, use_global_device_ids=true | all-gather | bytes 774144 | tf_op jit(solution)/shard_map/all_gather | solution.py:104
  59.3 13.8 %all_gather.15 = bf16[640,768]{1,0:T(8,128)(2,1)} all-gather(bf16[80,768]{1,0:T(8,128)(2,1)S(1)} %slice.189), channel_id=1, replica_groups=mesh['chip'=4,'core'=2,'expert'=4] {'chip','core'}, dimensions={0}, use_global_device_ids=true | all-gather | bytes 1105920 | tf_op jit(solution)/shard_map/all_gather | solution.py:104
  74.7 4.6 %all-to-all-start.2 = ((bf16[4,128,1024]{2,1,0:T(8,128)(2,1)}), bf16[4,128,1024]{2,1,0:T(8,128)(2,1)S(1)}, u32[]{:S(2)}, u32[]{:S(2)}) async-start(bf16[4,128,1024]{2,1,0:T(8,128)(2,1)} %broadcast_in_dim.54), calls=%async_computation.2 | async-start | bytes 2097152 | tf_op jit(solution)/shard_map/all_to_all | solution.py:59
  79.3 4.5 %shard_map.212 = (bf16[512,768]{1,0:T(8,128)(2,1)}, bf16[512,1024]{1,0:T(8,128)(2,1)}, bf16[1024,768]{1,0:T(8,128)(2,1)}) custom-call(bf16[512,1024]{1,0:T(8,128)(2,1)} %bitcast.162, f32[1,1024]{1,0:T(1,128)} %get-tuple-element.224.gain_ref, bf16[8,80,768]{2,1,0:T(8,128)(2,1)} %bitcast.174, bf16[8,56,768]{2,1,0:T(8,128)(2,1)} %bitcast.176), custom_call_target="tpu_custom_call" | custom-call | tf_op jit(solution)/shard_map/pallas_call | solution.py:155
  83.8 6.1 %shard_map.213 = bf16[4,512,256]{2,1,0:T(8,128)(2,1)} custom-call(s32[1]{0:T(128)} %bitcast.194, bf16[512,768]{1,0:T(8,128)(2,1)} %get-tuple-element.112.q_ref.k_ref.v_ref, bf16[512,768]{1,0:T(8,128)(2,1)} %get-tuple-element.112.q_ref.k_ref.v_ref, bf16[512,768]{1,0:T(8,128)(2,1)} %get-tuple-element.112.q_ref.k_ref.v_ref), custom_call_target="tpu_custom_call" | custom-call | tf_op jit(solution)/shard_map/pallas_call | solution.py:155
  89.9 15.7 %all-to-all-done.2 = bf16[4,128,1024]{2,1,0:T(8,128)(2,1)S(1)} async-done(((bf16[4,128,1024]{2,1,0:T(8,128)(2,1)}), bf16[4,128,1024]{2,1,0:T(8,128)(2,1)S(1)}, u32[]{:S(2)}, u32[]{:S(2)}) %all-to-all-start.2) | async-done | bytes 1048608 | tf_op jit(solution)/shard_map/all_to_all | solution.py:59
  112.5 6.9 %all-gather.5.cloned.1.call-done = bf16[3072,1024]{1,0:T(8,128)(2,1)} async-done(((bf16[384,1024]{1,0:T(8,128)(2,1)}), bf16[3072,1024]{1,0:T(8,128)(2,1)}) %all-gather.5.cloned.1.call-update) | async-done | bytes 6291472 | tf_op jit(solution)/shard_map/all_gather | solution.py:856
  122.6 12.9 %all-to-all-done.3.att_ref = bf16[4,512,256]{2,1,0:T(8,128)(2,1)S(1)} async-done(((bf16[4,512,256]{2,1,0:T(8,128)(2,1)}), bf16[4,512,256]{2,1,0:T(8,128)(2,1)S(1)}, u32[]{:S(2)}, u32[]{:S(2)}) %all-to-all-start.3) | async-done | bytes 1048608 | tf_op jit(solution)/shard_map/all_to_all | solution.py:59
  136.4 5.7 %shard_map.214 = (f32[512,1024]{1,0:T(8,128)}, bf16[512,1024]{1,0:T(8,128)(2,1)}, f32[512,2]{1,0:T(8,128)}) custom-call(bf16[4,512,256]{2,1,0:T(8,128)(2,1)} %copy-done.2, bf16[512,1024]{1,0:T(8,128)(2,1)} %bitcast.163, bf16[1024,1024]{1,0:T(8,128)(2,1)} %bitcast.158, f32[1,1024]{1,0:T(1,128)} %get-tuple-element.223.gain_ref, bf16[16,1024]{1,0:T(8,128)(2,1)} %pad.24.mix_ref), custom_call_target="tpu_custom_call" | custom-call | tf_op jit(solution)/shard_map/pallas_call | solution.py:155
  142.1 13.5 %shard_map.215 = (bf16[128,1024]{1,0:T(8,128)(2,1)}, bf16[128,1024]{1,0:T(8,128)(2,1)}, bf16[128,1024]{1,0:T(8,128)(2,1)}, bf16[128,1024]{1,0:T(8,128)(2,1)}, bf...) custom-call(s32[1]{0:T(128)} %bitcast.ex_ref, ...), custom_call_target="tpu_custom_call" | custom-call | tf_op jit(solution)/shard_map/pallas_call | solution.py:155
  155.7 7.2 %shard_map.216 = (bf16[4,2,128,1024]{3,2,1,0:T(8,128)(2,1)}, bf16[4,2,128,1024]{3,2,1,0:T(8,128)(2,1)}) custom-call(s32[1]{0:T(128)} %bitcast.35.core_ref, bf16[512,1024]{1,0:T(8,128)(2,1)} %get-tuple-element.119.x_ref, bf16[512,1024]{1,0:T(8,128)(2,1)} %get-tuple-element.124.g_ref, bf16[512,1024]{1,0:T(8,128)(2,1)} %get-tuple-element.125.act_ref, ...), custom_call_target="tpu_custom_call" | custom-call | tf_op jit(solution)/shard_map/pallas_call | solution.py:155
  163.4 4.0 %collective-permute-done.2 = bf16[4,2,128,1024]{3,2,1,0:T(8,128)(2,1)S(1)} collective-permute-done((bf16[4,2,128,1024]{3,2,1,0:T(8,128)(2,1)}, bf16[4,2,128,1024]{3,2,1,0:T(8,128)(2,1)S(1)}, u32[]{:S(2)}, u32[]{:S(2)}) %collective-permute-start.2) | collective-permute-done | bytes 2097184 | tf_op jit(solution)/shard_map/ppermute | solution.py:77
  167.4 3.9 %add_convert_fusion = bf16[4,2,128,1024]{3,2,1,0:T(8,128)(2,1)} fusion(bf16[4,2,128,1024]{3,2,1,0:T(8,128)(2,1)S(1)} %collective-permute-done.2, bf16[4,2,128,1024]{3,2,1,0:T(8,128)(2,1)} %get-tuple-element.130), kind=kLoop, calls=%fused_computation | loop fusion | flops 4194304 | bytes 6291456 | tf_op jit(solution)/shard_map/convert_element_type | solution.py:903
  175.1 12.4 %shard_map.217 = (f32[2,160,1024]{2,1,0:T(8,128)}, bf16[2,160,1024]{2,1,0:T(8,128)(2,1)}, bf16[320,2048]{1,0:T(8,128)(2,1)}, bf16[320,2048]{1,0:T(8,128)(2,1)}) custom-call(bf16[2,160,1024]{2,1,0:T(8,128)(2,1)} %get-tuple-element.123.own_ref.own_x.own_g, bf16[2,160,1024]{2,1,0:T(8,128)(2,1)} %copy-done.1, bf16[4,512,1024]{2,1,0:T(8,128)(2,1)} %bitcast.168, ...), custom_call_target="tpu_custom_call" | custom-call | tf_op jit(solution)/shard_map/pallas_call | solution.py:155
  187.9 8.7 %shard_map.218 = bf16[4,1024,1024]{2,1,0:T(8,128)(2,1)} custom-call(bf16[2,160,1024]{2,1,0:T(8,128)(2,1)} %get-tuple-element.123.own_ref.own_x.own_g, bf16[2,160,1024]{2,1,0:T(8,128)(2,1)} %copy-done.1, bf16[2,160,1024]{2,1,0:T(8,128)(2,1)} %get-tuple-element.123.own_ref.own_x.own_g, bf16[2,160,1024]{2,1,0:T(8,128)(2,1)} %copy-done.1, ...), custom_call_target="tpu_custom_call" | custom-call | tf_op jit(solution)/shard_map/pallas_call | solution.py:155
  197.6 6.6 %all-to-all-done.4.pay_ref = bf16[4,144,1024]{2,1,0:T(8,128)(2,1)S(1)} async-done(((bf16[4,144,1024]{2,1,0:T(8,128)(2,1)}), bf16[4,144,1024]{2,1,0:T(8,128)(2,1)S(1)}, u32[]{:S(2)}, u32[]{:S(2)}) %all-to-all-start.4) | async-done | bytes 1179680 | tf_op jit(solution)/shard_map/all_to_all | solution.py:59
  216.7 5.6 %collective-permute-done.5.refs_2_ = bf16[2,40,1024]{2,1,0:T(8,128)(2,1)S(1)} collective-permute-done((bf16[2,40,1024]{2,1,0:T(8,128)(2,1)S(1)}, bf16[2,40,1024]{2,1,0:T(8,128)(2,1)S(1)}, u32[]{:S(2)}, u32[]{:S(2)}) %collective-permute-start.5) | collective-permute-done | bytes 163872 | tf_op jit(solution)/shard_map/ppermute | solution.py:69
  223.7 5.4 %shard_map.219 = (f32[128,1024]{1,0:T(8,128)}, bf16[128,1024]{1,0:T(8,128)(2,1)}, bf16[4,128,256]{2,1,0:T(8,128)(2,1)}, f32[8,1024]{1,0:T(8,128)}, f32[128,1024]{1,0:T(8,128)}) custom-call(s32[1]{0:T(128)} %bitcast.ex_ref, bf16[4,144,1024]{2,1,0:T(8,128)(2,1)} %copy-done.3, s32[128,1]{1,0:T(8,128)} %copy.101.slot_ref, ...), custom_call_target="tpu_custom_call" | custom-call | tf_op jit(solution)/shard_map/pallas_call | solution.py:155
  229.1 3.7 %all-to-all-start.5 = ((bf16[4,128,256]{2,1,0:T(8,128)(2,1)}), bf16[4,128,256]{2,1,0:T(8,128)(2,1)S(1)}, u32[]{:S(2)}, u32[]{:S(2)}) async-start(bf16[4,128,256]{2,1,0:T(8,128)(2,1)} %get-tuple-element.148), calls=%async_computation.5 | async-start | bytes 524288 | tf_op jit(solution)/shard_map/all_to_all | solution.py:59
  235.9 5.5 %all-to-all-done.5 = bf16[4,128,256]{2,1,0:T(8,128)(2,1)S(1)} async-done(((bf16[4,128,256]{2,1,0:T(8,128)(2,1)}), bf16[4,128,256]{2,1,0:T(8,128)(2,1)S(1)}, u32[]{:S(2)}, u32[]{:S(2)}) %all-to-all-start.5) | async-done | bytes 262176 | tf_op jit(solution)/shard_map/all_to_all | solution.py:59
  247.6 7.5 %shard_map.221 = (bf16[512,256]{1,0:T(8,128)(2,1)}, bf16[512,256]{1,0:T(8,128)(2,1)}, bf16[512,256]{1,0:T(8,128)(2,1)}) custom-call(s32[1]{0:T(128)} %bitcast.195, bf16[512,768]{1,0:T(8,128)(2,1)} %get-tuple-element.112.q_ref.k_ref.v_ref, bf16[512,768]{1,0:T(8,128)(2,1)} %get-tuple-element.112.q_ref.k_ref.v_ref, ...), custom_call_target="tpu_custom_call" | custom-call | flops 23000000512 | tf_op jit(solution)/shard_map/pallas_call | solution.py:155
  255.1 4.6 %shard_map.222 = (bf16[4,144,768]{2,1,0:T(8,128)(2,1)}, bf16[4,144,768]{2,1,0:T(8,128)(2,1)}) custom-call(s32[1]{0:T(128)} %bitcast.35.core_ref, bf16[512,1024]{1,0:T(8,128)(2,1)} %get-tuple-element.156.x_ref, bf16[1024,768]{1,0:T(8,128)(2,1)} %get-tuple-element.157.w_ref, f32[1,1024]{1,0:T(1,128)} %get-tuple-element.224.gain_ref, ...), custom_call_target="tpu_custom_call" | custom-call | tf_op jit(solution)/shard_map/pallas_call | solution.py:155
  259.6 4.5 %shard_map.223 = (bf16[128,1024]{1,0:T(8,128)(2,1)}, bf16[128,1024]{1,0:T(8,128)(2,1)}, bf16[128,1024]{1,0:T(8,128)(2,1)}, bf16[128,1024]{1,0:T(8,128)(2,1)}) custom-call(s32[1]{0:T(128)} %bitcast.ex_ref, bf16[512,256]{1,0:T(8,128)(2,1)} %get-tuple-element.162.dq_ref, bf16[512,256]{1,0:T(8,128)(2,1)} %get-tuple-element.159.dk_ref, ...), custom_call_target="tpu_custom_call" | custom-call | tf_op jit(solution)/shard_map/pallas_call | solution.py:155
  266.9 4.9 %collective-permute-done.8 = bf16[2,128,1024]{2,1,0:T(8,128)(2,1)S(1)} collective-permute-done((bf16[2,128,1024]{2,1,0:T(8,128)(2,1)S(1)}, bf16[2,128,1024]{2,1,0:T(8,128)(2,1)S(1)}, u32[]{:S(2)}, u32[]{:S(2)}) %collective-permute-start.8) | collective-permute-done | bytes 524320 | tf_op jit(solution)/shard_map/ppermute | solution.py:86
  284.8 10.5 %collective-permute-done.17.refs_2_ = bf16[128,1024]{1,0:T(8,128)(2,1)S(1)} collective-permute-done((bf16[128,1024]{1,0:T(8,128)(2,1)S(1)}, bf16[128,1024]{1,0:T(8,128)(2,1)S(1)}, u32[]{:S(2)}, u32[]{:S(2)}) %collective-permute-start.17) | collective-permute-done | bytes 262176 | tf_op jit(solution)/shard_map/ppermute | solution.py:69
  297.8 5.6 %collective-permute-done.20 = bf16[144,384]{1,0:T(8,128)(2,1)S(1)} collective-permute-done((bf16[144,384]{1,0:T(8,128)(2,1)S(1)}, bf16[144,384]{1,0:T(8,128)(2,1)S(1)}, u32[]{:S(2)}, u32[]{:S(2)}) %collective-permute-start.20) | collective-permute-done | bytes 110624 | tf_op jit(solution)/shard_map/ppermute | solution.py:86
  307.6 7.5 %all-to-all-start.6 = ((bf16[4,32,2944]{2,1,0:T(8,128)(2,1)}), bf16[4,32,2944]{2,1,0:T(8,128)(2,1)S(1)}, u32[]{:S(2)}, u32[]{:S(2)}) async-start(bf16[4,32,2944]{2,1,0:T(8,128)(2,1)} %fusion.4), calls=%async_computation.7 | async-start | bytes 1507328 | tf_op jit(solution)/shard_map/all_to_all | solution.py:59
  325.9 3.8 %shard_map.225 = (f32[128,4096]{1,0:T(8,128)}, f32[512,1024]{1,0:T(8,128)}) custom-call(s32[1]{0:T(128)} %bitcast.35.core_ref, bf16[2,128,1024]{2,1,0:T(8,128)(2,1)} %get-tuple-element.214.own_ref, bf16[2,128,1024]{2,1,0:T(8,128)(2,1)} %copy-done.12, bf16[512,1024]{1,0:T(8,128)(2,1)} %get-tuple-element.207.down_ref), custom_call_target="tpu_custom_call" | custom-call | tf_op jit(solution)/shard_map/pallas_call | solution.py:155
  329.7 3.9 %all-to-all-done.6 = bf16[4,32,2944]{2,1,0:T(8,128)(2,1)S(1)} async-done(((bf16[4,32,2944]{2,1,0:T(8,128)(2,1)}), bf16[4,32,2944]{2,1,0:T(8,128)(2,1)S(1)}, u32[]{:S(2)}, u32[]{:S(2)}) %all-to-all-start.6) | async-done | bytes 753696 | tf_op jit(solution)/shard_map/all_to_all | solution.py:59
  (204 shorter events, 88.3 us)
Async XLA Ops:
  7.2 66.5 %all-gather.9.cloned.1.call-start = ((), (), s32[]{:S(2)}) async-start(), calls=%async_computation.13 | async-start | bytes 5242880 | tf_op jit(solution)/shard_map/all_gather | solution.py:805
  9.2 8.7 %collective-permute-start = (bf16[128,2048]{0,1:T(8,128)(2,1)S(1)}, bf16[128,2048]{0,1:T(8,128)(2,1)S(1)}, u32[]{:S(2)}, u32[]{:S(2)}) collective-permute-start(bf16[128,2048]{0,1:T(8,128)(2,1)S(1)} %bitcast.190), channel_id=1, source_target_pairs={{0,4},{4,0},{1,5},{5,1},{2,6},{6,2},{3,7},{7,3},{8,12},{12,8},{9,1... | collective-permute-start | bytes 1572872 | tf_op jit(solution)/shard_map/ppermute | solution.py:77
  11.7 26.6 %all-to-all-start = ((bf16[4,32,3072]{2,1,0:T(8,128)(2,1)}), bf16[4,32,3072]{2,1,0:T(8,128)(2,1)S(1)}, u32[]{:S(2)}, u32[]{:S(2)}) async-start(bf16[4,32,3072]{2,1,0:T(8,128)(2,1)} %pad_maximum_fusion.1), calls=%async_computation | async-start | bytes 1572864 | tf_op jit(solution)/shard_map/all_to_all | solution.py:59
  40.6 33.1 %all-to-all-start.1 = ((bf16[4,128,1024]{2,1,0:T(8,128)(2,1)}), bf16[4,128,1024]{2,1,0:T(8,128)(2,1)S(1)}, u32[]{:S(2)}, u32[]{:S(2)}) async-start(bf16[4,128,1024]{2,1,0:T(8,128)(2,1)} %broadcast_in_dim.55), calls=%async_computation.1 | async-start | bytes 2097152 | tf_op jit(solution)/shard_map/all_to_all | solution.py:59
  44.2 75.3 %all-gather.5.cloned.1.call-start = ((), (), s32[]{:S(2)}) async-start(), calls=%async_computation.9 | async-start | bytes 7077888 | tf_op jit(solution)/shard_map/all_gather | solution.py:856
  73.8 101.4 %all-gather.7.cloned.1.call-start = ((), (), s32[]{:S(2)}) async-start(), calls=%async_computation.10 | async-start | bytes 5242880 | tf_op jit(solution)/shard_map/all_gather | solution.py:869
  74.7 30.9 %all-to-all-start.2 = ((bf16[4,128,1024]{2,1,0:T(8,128)(2,1)}), bf16[4,128,1024]{2,1,0:T(8,128)(2,1)S(1)}, u32[]{:S(2)}, u32[]{:S(2)}) async-start(bf16[4,128,1024]{2,1,0:T(8,128)(2,1)} %broadcast_in_dim.54), calls=%async_computation.2 | async-start | bytes 2097152 | tf_op jit(solution)/shard_map/all_to_all | solution.py:59
  106.6 28.9 %all-to-all-start.3 = ((bf16[4,512,256]{2,1,0:T(8,128)(2,1)}), bf16[4,512,256]{2,1,0:T(8,128)(2,1)S(1)}, u32[]{:S(2)}, u32[]{:S(2)}) async-start(bf16[4,512,256]{2,1,0:T(8,128)(2,1)} %shard_map.213), calls=%async_computation.3 | async-start | bytes 2097152 | tf_op jit(solution)/shard_map/all_to_all | solution.py:59
  110.1 194.6 %reduce-scatter.3.cloned.1.call-start = ((), (), s32[]{:S(2)}) async-start(), calls=%async_computation.11 | async-start | bytes 2621440 | tf_op jit(solution)/shard_map/reduce_scatter | solution.py:905
  155.6 7.3 %collective-permute-start.1 = (bf16[2,160,1024]{2,1,0:T(8,128)(2,1)}, bf16[2,160,1024]{2,1,0:T(8,128)(2,1)S(1)}, u32[]{:S(2)}, u32[]{:S(2)}) collective-permute-start(bf16[2,160,1024]{2,1,0:T(8,128)(2,1)} %get-tuple-element.123.own_ref.own_x.own_g), channel_id=1, source_target_pairs={{0,4},{4,0},{1,5},{5,1},{2,6},{6,2},{3,7},{7,3},{8,12},{12,8},{9,1... | collective-permute-start | bytes 1966088 | tf_op jit(solution)/shard_map/ppermute | solution.py:77
  171.3 32.9 %all-to-all-start.4 = ((bf16[4,144,1024]{2,1,0:T(8,128)(2,1)}), bf16[4,144,1024]{2,1,0:T(8,128)(2,1)S(1)}, u32[]{:S(2)}, u32[]{:S(2)}) async-start(bf16[4,144,1024]{2,1,0:T(8,128)(2,1)} %get-tuple-element.122), calls=%async_computation.4 | async-start | bytes 2359296 | tf_op jit(solution)/shard_map/all_to_all | solution.py:59
  174.9 141.7 %reduce-scatter.5.cloned.1.call-start = ((), (), s32[]{:S(2)}) async-start(), calls=%async_computation.12 | async-start | bytes 10485760 | tf_op jit(solution)/shard_map/reduce_scatter | solution.py:927
  187.5 9.1 %collective-permute-start.3 = (bf16[2,160,1024]{2,1,0:T(8,128)(2,1)}, bf16[2,160,1024]{2,1,0:T(8,128)(2,1)S(1)}, u32[]{:S(2)}, u32[]{:S(2)}) collective-permute-start(bf16[2,160,1024]{2,1,0:T(8,128)(2,1)} %get-tuple-element.138), channel_id=1, source_target_pairs={{0,4},{4,0},{1,5},{5,1},{2,6},{6,2},{3,7},{7,3},{8,12},{12,8},{9,1... | collective-permute-start | bytes 1966088 | tf_op jit(solution)/shard_map/ppermute | solution.py:77
  207.7 9.0 %collective-permute-start.4 = (bf16[2,40,1024]{2,1,0:T(8,128)(2,1)S(1)}, bf16[2,40,1024]{2,1,0:T(8,128)(2,1)S(1)}, u32[]{:S(2)}, u32[]{:S(2)}) collective-permute-start(bf16[2,40,1024]{2,1,0:T(8,128)(2,1)S(1)} %copy-done.21), channel_id=1, source_target_pairs={{0,1},{1,2},{2,3},{3,0},{4,5},{5,6},{6,7},{7,4},{8,9},{9,10},{10,1... | collective-permute-start | bytes 491528 | tf_op jit(solution)/shard_map/ppermute | solution.py:69
  207.7 14.7 %collective-permute-start.5 = (bf16[2,40,1024]{2,1,0:T(8,128)(2,1)S(1)}, bf16[2,40,1024]{2,1,0:T(8,128)(2,1)S(1)}, u32[]{:S(2)}, u32[]{:S(2)}) collective-permute-start(bf16[2,40,1024]{2,1,0:T(8,128)(2,1)S(1)} %get-tuple-element.145), channel_id=1, source_target_pairs={{0,2},{1,3},{2,0},{3,1},{4,6},{5,7},{6,4},{7,5},{8,10},{9,11},{10,... | collective-permute-start | bytes 491528 | tf_op jit(solution)/shard_map/ppermute | solution.py:69
  209.7 12.7 %collective-permute-start.6 = (bf16[2,40,1024]{2,1,0:T(8,128)(2,1)S(1)}, bf16[2,40,1024]{2,1,0:T(8,128)(2,1)S(1)}, u32[]{:S(2)}, u32[]{:S(2)}) collective-permute-start(bf16[2,40,1024]{2,1,0:T(8,128)(2,1)S(1)} %get-tuple-element.146), channel_id=1, source_target_pairs={{0,3},{1,0},{2,1},{3,2},{4,7},{5,4},{6,5},{7,6},{8,11},{9,8},{10,9... | collective-permute-start | bytes 491528 | tf_op jit(solution)/shard_map/ppermute | solution.py:69
  229.1 12.3 %all-to-all-start.5 = ((bf16[4,128,256]{2,1,0:T(8,128)(2,1)}), bf16[4,128,256]{2,1,0:T(8,128)(2,1)S(1)}, u32[]{:S(2)}, u32[]{:S(2)}) async-start(bf16[4,128,256]{2,1,0:T(8,128)(2,1)} %get-tuple-element.148), calls=%async_computation.5 | async-start | bytes 524288 | tf_op jit(solution)/shard_map/all_to_all | solution.py:59
  241.4 22.8 %collective-permute-start.11 = (bf16[128,1024]{1,0:T(8,128)(2,1)}, bf16[128,1024]{1,0:T(8,128)(2,1)}, u32[]{:S(2)}, u32[]{:S(2)}) collective-permute-start(bf16[128,1024]{1,0:T(8,128)(2,1)} %get-tuple-element.174), channel_id=1, source_target_pairs={{0,3},{1,0},{2,1},{3,2},{4,7},{5,4},{6,5},{7,6},{8,11},{9,8},{10,9... | collective-permute-start | bytes 786440 | tf_op jit(solution)/shard_map/ppermute | solution.py:69
  242.9 24.0 %collective-permute-start.10 = (bf16[128,1024]{1,0:T(8,128)(2,1)}, bf16[128,1024]{1,0:T(8,128)(2,1)}, u32[]{:S(2)}, u32[]{:S(2)}) collective-permute-start(bf16[128,1024]{1,0:T(8,128)(2,1)} %get-tuple-element.172), channel_id=1, source_target_pairs={{0,2},{1,3},{2,0},{3,1},{4,6},{5,7},{6,4},{7,5},{8,10},{9,11},{10,... | collective-permute-start | bytes 786440 | tf_op jit(solution)/shard_map/ppermute | solution.py:69
  243.1 23.9 %collective-permute-start.9 = (bf16[128,1024]{1,0:T(8,128)(2,1)}, bf16[128,1024]{1,0:T(8,128)(2,1)}, u32[]{:S(2)}, u32[]{:S(2)}) collective-permute-start(bf16[128,1024]{1,0:T(8,128)(2,1)} %get-tuple-element.170), channel_id=1, source_target_pairs={{0,1},{1,2},{2,3},{3,0},{4,5},{5,6},{6,7},{7,4},{8,9},{9,10},{10,1... | collective-permute-start | bytes 786440 | tf_op jit(solution)/shard_map/ppermute | solution.py:69
  246.0 25.8 %collective-permute-start.8 = (bf16[2,128,1024]{2,1,0:T(8,128)(2,1)S(1)}, bf16[2,128,1024]{2,1,0:T(8,128)(2,1)S(1)}, u32[]{:S(2)}, u32[]{:S(2)}) collective-permute-start(bf16[2,128,1024]{2,1,0:T(8,128)(2,1)S(1)} %fusion.5), channel_id=1, source_target_pairs={{0,8},{8,0},{16,24},{24,16},{1,9},{9,1},{17,25},{25,17},{2,10},{10... | collective-permute-start | bytes 1572872 | tf_op jit(solution)/shard_map/ppermute | solution.py:86
  271.8 6.7 %collective-permute-start.12 = (bf16[4,144,768]{2,1,0:T(8,128)(2,1)}, bf16[4,144,768]{2,1,0:T(8,128)(2,1)S(1)}, u32[]{:S(2)}, u32[]{:S(2)}) collective-permute-start(bf16[4,144,768]{2,1,0:T(8,128)(2,1)} %get-tuple-element.182), channel_id=1, source_target_pairs={{0,4},{4,0},{1,5},{5,1},{2,6},{6,2},{3,7},{7,3},{8,12},{12,8},{9,1... | collective-permute-start | bytes 2654216 | tf_op jit(solution)/shard_map/ppermute | solution.py:77
  272.2 8.8 %collective-permute-start.15 = (bf16[128,1024]{1,0:T(8,128)(2,1)S(1)}, bf16[128,1024]{1,0:T(8,128)(2,1)S(1)}, u32[]{:S(2)}, u32[]{:S(2)}) collective-permute-start(bf16[128,1024]{1,0:T(8,128)(2,1)S(1)} %fusion.7), channel_id=1, source_target_pairs={{0,16},{8,24},{16,0},{24,8},{1,17},{9,25},{17,1},{25,9},{2,18},{10... | collective-permute-start | bytes 786440 | tf_op jit(solution)/shard_map/ppermute | solution.py:86
  273.7 11.1 %collective-permute-start.16 = (bf16[128,1024]{1,0:T(8,128)(2,1)S(1)}, bf16[128,1024]{1,0:T(8,128)(2,1)S(1)}, u32[]{:S(2)}, u32[]{:S(2)}) collective-permute-start(bf16[128,1024]{1,0:T(8,128)(2,1)S(1)} %copy-done.31), channel_id=1, source_target_pairs={{0,1},{1,2},{2,3},{3,0},{4,5},{5,6},{6,7},{7,4},{8,9},{9,10},{10,1... | collective-permute-start | bytes 786440 | tf_op jit(solution)/shard_map/ppermute | solution.py:69
  275.7 19.6 %collective-permute-start.17 = (bf16[128,1024]{1,0:T(8,128)(2,1)S(1)}, bf16[128,1024]{1,0:T(8,128)(2,1)S(1)}, u32[]{:S(2)}, u32[]{:S(2)}) collective-permute-start(bf16[128,1024]{1,0:T(8,128)(2,1)S(1)} %copy-done.30), channel_id=1, source_target_pairs={{0,2},{1,3},{2,0},{3,1},{4,6},{5,7},{6,4},{7,5},{8,10},{9,11},{10,... | collective-permute-start | bytes 786440 | tf_op jit(solution)/shard_map/ppermute | solution.py:69
  276.7 18.6 %collective-permute-start.18 = (bf16[128,1024]{1,0:T(8,128)(2,1)S(1)}, bf16[128,1024]{1,0:T(8,128)(2,1)S(1)}, u32[]{:S(2)}, u32[]{:S(2)}) collective-permute-start(bf16[128,1024]{1,0:T(8,128)(2,1)S(1)} %copy-done.29), channel_id=1, source_target_pairs={{0,3},{1,0},{2,1},{3,2},{4,7},{5,4},{6,5},{7,6},{8,11},{9,8},{10,9... | collective-permute-start | bytes 786440 | tf_op jit(solution)/shard_map/ppermute | solution.py:69
  278.9 16.4 %collective-permute-start.13 = (bf16[2,144,384]{2,1,0:T(8,128)(2,1)S(1)}, bf16[2,144,384]{2,1,0:T(8,128)(2,1)S(1)}, u32[]{:S(2)}, u32[]{:S(2)}) collective-permute-start(bf16[2,144,384]{2,1,0:T(8,128)(2,1)S(1)} %fusion.8), channel_id=1, source_target_pairs={{0,8},{8,0},{16,24},{24,16},{1,9},{9,1},{17,25},{25,17},{2,10},{10... | collective-permute-start | bytes 663560 | tf_op jit(solution)/shard_map/ppermute | solution.py:86
  280.9 14.4 %collective-permute-start.14 = (bf16[2,144,384]{2,1,0:T(8,128)(2,1)S(1)}, bf16[2,144,384]{2,1,0:T(8,128)(2,1)S(1)}, u32[]{:S(2)}, u32[]{:S(2)}) collective-permute-start(bf16[2,144,384]{2,1,0:T(8,128)(2,1)S(1)} %select_convert_fusion.1), channel_id=1, source_target_pairs={{0,16},{8,24},{16,0},{24,8},{1,17},{9,25},{17,1},{25,9},{2,18},{10... | collective-permute-start | bytes 663560 | tf_op jit(solution)/shard_map/ppermute | solution.py:86
  295.5 8.0 %collective-permute-start.20 = (bf16[144,384]{1,0:T(8,128)(2,1)S(1)}, bf16[144,384]{1,0:T(8,128)(2,1)S(1)}, u32[]{:S(2)}, u32[]{:S(2)}) collective-permute-start(bf16[144,384]{1,0:T(8,128)(2,1)S(1)} %fusion.14), channel_id=1, source_target_pairs={{0,8},{8,0},{16,24},{24,16},{1,9},{9,1},{17,25},{25,17},{2,10},{10... | collective-permute-start | bytes 331784 | tf_op jit(solution)/shard_map/ppermute | solution.py:86
  296.6 7.9 %collective-permute-start.19 = (bf16[144,384]{1,0:T(8,128)(2,1)S(1)}, bf16[144,384]{1,0:T(8,128)(2,1)S(1)}, u32[]{:S(2)}, u32[]{:S(2)}) collective-permute-start(bf16[144,384]{1,0:T(8,128)(2,1)S(1)} %fusion.13), channel_id=1, source_target_pairs={{0,16},{8,24},{16,0},{24,8},{1,17},{9,25},{17,1},{25,9},{2,18},{10... | collective-permute-start | bytes 331784 | tf_op jit(solution)/shard_map/ppermute | solution.py:86
  307.6 26.0 %all-to-all-start.6 = ((bf16[4,32,2944]{2,1,0:T(8,128)(2,1)}), bf16[4,32,2944]{2,1,0:T(8,128)(2,1)S(1)}, u32[]{:S(2)}, u32[]{:S(2)}) async-start(bf16[4,32,2944]{2,1,0:T(8,128)(2,1)} %fusion.4), calls=%async_computation.7 | async-start | bytes 1507328 | tf_op jit(solution)/shard_map/all_to_all | solution.py:59
  320.0 5.1 %collective-permute-start.21 = (bf16[2,128,1024]{2,1,0:T(8,128)(2,1)S(1)}, bf16[2,128,1024]{2,1,0:T(8,128)(2,1)S(1)}, u32[]{:S(2)}, u32[]{:S(2)}) collective-permute-start(bf16[2,128,1024]{2,1,0:T(8,128)(2,1)S(1)} %get-tuple-element.213), channel_id=1, source_target_pairs={{0,4},{4,0},{1,5},{5,1},{2,6},{6,2},{3,7},{7,3},{8,12},{12,8},{9,1... | collective-permute-start | bytes 1572872 | tf_op jit(solution)/shard_map/ppermute | solution.py:77
  (35 other events, 146.0 us)
Sparse Core Ops, SparseCore 0:
  9.9 60.0 all-gather.8
  73.9 45.5 all-gather.4
  121.3 52.6 all-gather.6
  176.9 35.1 reduce-scatter.2
  215.3 101.1 reduce-scatter.4

commit v3 on v2

--- a/solution.py
+++ b/solution.py
@@ -989,11 +989,11 @@
     fold.send()
     while out_fold.orders[0]:
         out_fold.send()
-        dattn = out_fold.meet(*dattn)
-    dattn = fold.meet(*dattn)
+        out_fold.meet()
+    fold.meet()
     while fold.orders[0]:
         fold.send()
-        fold.meet()
+        dattn = fold.meet(*dattn)
     out_weight_sum, qkv_sum = (out_fold.pair[0], jnp.concatenate(fold.pair, axis=-1))
     out_total = out_base
     for piece in out_sums:

time: 346 us -> 342 us (0.988)
  waiting for transfers between devices: 114 us -> 108 us
    reduce_scatter x1, waiting for transfers between devices: 1.38 us -> 6.86 us  [shards(): lax.psum_scatter(exp_grads.reshape(-1, width), 'chip', scatter_dimension=...]
    ppermute x6, waiting for transfers between devices: 12.6 us -> 7.83 us  [flip(): return lax.ppermute(values, 'chip', [(i, i ^ bit) for i in chips])]
    all_to_all x7, waiting for transfers between devices: 63.4 us -> 59.5 us  [swap(): return lax.all_to_all(values, axis, split_axis=0, concat_axis=0, tiled=True)]
  transfers between devices with their start and end apart: 34 -> 34, of which waited for: 19 -> 18; matrix products, arithmetic and copies ran while one was open for 10% -> 10% of each run, Pallas kernels for 26% -> 26%
where the time goes in v3:
time: 342 us; the launch traced here: 341 us
  waiting for transfers between devices  108 us (32%)
  Pallas kernels  89.5 us (26%)
  starting transfers between devices  54.6 us (16%)
  local copies, waits for them, and re-layouts  29.3 us (9%)
  blocking collectives  27.7 us (8%)
  other arithmetic  17 us (5%)
  between operations  14.4 us (4%)
    pallas_call x14, Pallas kernels, call(): pl.pallas_call(body, grid=grid, in_specs=in_specs, out_specs=out_specs, o...  89.5 us
    all_to_all x7, waiting for transfers between devices, swap(): return lax.all_to_all(values, axis, split_axis=0, concat_axis=0, tiled=True)  59.5 us
    all_to_all x7, starting transfers between devices, swap(): return lax.all_to_all(values, axis, split_axis=0, concat_axis=0, tiled=True)  33.1 us
    all_gather x2, blocking collectives, gather_small(): lax.all_gather(values[k:k + step], axes, axis=0, tiled=True)  27.7 us
    ppermute x9, waiting for transfers between devices, turn(): lax.ppermute(values, 'expert', [(i, (i + step) % count) for i in range(co...  20.1 us
    ppermute x9, starting transfers between devices, turn(): lax.ppermute(values, 'expert', [(i, (i + step) % count) for i in range(co...  11.4 us
    ppermute x6, starting transfers between devices, flip(): return lax.ppermute(values, 'chip', [(i, i ^ bit) for i in chips])  8.08 us
    ppermute x6, waiting for transfers between devices, flip(): return lax.ppermute(values, 'chip', [(i, i ^ bit) for i in chips])  7.83 us
  transfers between devices with their start and end apart: 34, of which 18 were waited for; matrix products, arithmetic and copies ran while one was open for 10% of the time, Pallas kernels for 26%

profile of v3, /device:TPU:0, one launch (start us, length us, event | category | flops | bytes accessed | tf_op | source)
XLA Modules:
  0.0 340.6 jit_solution(6212341646688117880)
XLA Ops:
  11.7 6.2 %all-to-all-start = ((bf16[4,32,3072]{2,1,0:T(8,128)(2,1)}), bf16[4,32,3072]{2,1,0:T(8,128)(2,1)S(1)}, u32[]{:S(2)}, u32[]{:S(2)}) async-start(bf16[4,32,3072]{2,1,0:T(8,128)(2,1)} %pad_maximum_fusion.1), calls=%async_computation | async-start | bytes 1572864 | tf_op jit(solution)/shard_map/all_to_all | solution.py:59
  19.5 18.8 %all-to-all-done = bf16[4,32,3072]{2,1,0:T(8,128)(2,1)S(1)} async-done(((bf16[4,32,3072]{2,1,0:T(8,128)(2,1)}), bf16[4,32,3072]{2,1,0:T(8,128)(2,1)S(1)}, u32[]{:S(2)}, u32[]{:S(2)}) %all-to-all-start) | async-done | bytes 786464 | tf_op jit(solution)/shard_map/all_to_all | solution.py:59
  40.6 3.6 %all-to-all-start.1 = ((bf16[4,128,1024]{2,1,0:T(8,128)(2,1)}), bf16[4,128,1024]{2,1,0:T(8,128)(2,1)S(1)}, u32[]{:S(2)}, u32[]{:S(2)}) async-start(bf16[4,128,1024]{2,1,0:T(8,128)(2,1)} %broadcast_in_dim.55), calls=%async_computation.1 | async-start | bytes 2097152 | tf_op jit(solution)/shard_map/all_to_all | solution.py:59
  45.4 13.9 %all_gather.16 = bf16[448,768]{1,0:T(8,128)(2,1)S(1)} all-gather(bf16[56,768]{1,0:T(8,128)(2,1)S(1)} %fusion.15), channel_id=1, replica_groups=mesh['chip'=4,'core'=2,'expert'=4] {'chip','core'}, dimensions={0}, use_global_device_ids=true | all-gather | bytes 774144 | tf_op jit(solution)/shard_map/all_gather | solution.py:104
  59.3 13.8 %all_gather.15 = bf16[640,768]{1,0:T(8,128)(2,1)} all-gather(bf16[80,768]{1,0:T(8,128)(2,1)S(1)} %slice.189), channel_id=1, replica_groups=mesh['chip'=4,'core'=2,'expert'=4] {'chip','core'}, dimensions={0}, use_global_device_ids=true | all-gather | bytes 1105920 | tf_op jit(solution)/shard_map/all_gather | solution.py:104
  74.7 4.6 %all-to-all-start.2 = ((bf16[4,128,1024]{2,1,0:T(8,128)(2,1)}), bf16[4,128,1024]{2,1,0:T(8,128)(2,1)S(1)}, u32[]{:S(2)}, u32[]{:S(2)}) async-start(bf16[4,128,1024]{2,1,0:T(8,128)(2,1)} %broadcast_in_dim.54), calls=%async_computation.2 | async-start | bytes 2097152 | tf_op jit(solution)/shard_map/all_to_all | solution.py:59
  79.3 4.5 %shard_map.212 = (bf16[512,768]{1,0:T(8,128)(2,1)}, bf16[512,1024]{1,0:T(8,128)(2,1)}, bf16[1024,768]{1,0:T(8,128)(2,1)}) custom-call(bf16[512,1024]{1,0:T(8,128)(2,1)} %bitcast.162, f32[1,1024]{1,0:T(1,128)} %get-tuple-element.214.gain_ref, bf16[8,80,768]{2,1,0:T(8,128)(2,1)} %bitcast.174, bf16[8,56,768]{2,1,0:T(8,128)(2,1)} %bitcast.176), custom_call_target="tpu_custom_call" | custom-call | tf_op jit(solution)/shard_map/pallas_call | solution.py:155
  83.8 6.1 %shard_map.213 = bf16[4,512,256]{2,1,0:T(8,128)(2,1)} custom-call(s32[1]{0:T(128)} %bitcast.194, bf16[512,768]{1,0:T(8,128)(2,1)} %get-tuple-element.107.q_ref.k_ref.v_ref, bf16[512,768]{1,0:T(8,128)(2,1)} %get-tuple-element.107.q_ref.k_ref.v_ref, bf16[512,768]{1,0:T(8,128)(2,1)} %get-tuple-element.107.q_ref.k_ref.v_ref), custom_call_target="tpu_custom_call" | custom-call | tf_op jit(solution)/shard_map/pallas_call | solution.py:155
  89.9 15.7 %all-to-all-done.2 = bf16[4,128,1024]{2,1,0:T(8,128)(2,1)S(1)} async-done(((bf16[4,128,1024]{2,1,0:T(8,128)(2,1)}), bf16[4,128,1024]{2,1,0:T(8,128)(2,1)S(1)}, u32[]{:S(2)}, u32[]{:S(2)}) %all-to-all-start.2) | async-done | bytes 1048608 | tf_op jit(solution)/shard_map/all_to_all | solution.py:59
  112.5 6.9 %all-gather.5.cloned.1.call-done = bf16[3072,1024]{1,0:T(8,128)(2,1)} async-done(((bf16[384,1024]{1,0:T(8,128)(2,1)}), bf16[3072,1024]{1,0:T(8,128)(2,1)}) %all-gather.5.cloned.1.call-update) | async-done | bytes 6291472 | tf_op jit(solution)/shard_map/all_gather | solution.py:856
  122.6 12.9 %all-to-all-done.3.att_ref = bf16[4,512,256]{2,1,0:T(8,128)(2,1)S(1)} async-done(((bf16[4,512,256]{2,1,0:T(8,128)(2,1)}), bf16[4,512,256]{2,1,0:T(8,128)(2,1)S(1)}, u32[]{:S(2)}, u32[]{:S(2)}) %all-to-all-start.3) | async-done | bytes 1048608 | tf_op jit(solution)/shard_map/all_to_all | solution.py:59
  136.4 5.7 %shard_map.214 = (f32[512,1024]{1,0:T(8,128)}, bf16[512,1024]{1,0:T(8,128)(2,1)}, f32[512,2]{1,0:T(8,128)}) custom-call(bf16[4,512,256]{2,1,0:T(8,128)(2,1)} %copy-done.2, bf16[512,1024]{1,0:T(8,128)(2,1)} %bitcast.163, bf16[1024,1024]{1,0:T(8,128)(2,1)} %bitcast.158, f32[1,1024]{1,0:T(1,128)} %get-tuple-element.213.gain_ref, bf16[16,1024]{1,0:T(8,128)(2,1)} %pad.24.mix_ref), custom_call_target="tpu_custom_call" | custom-call | tf_op jit(solution)/shard_map/pallas_call | solution.py:155
  142.1 13.5 %shard_map.215 = (bf16[128,1024]{1,0:T(8,128)(2,1)}, bf16[128,1024]{1,0:T(8,128)(2,1)}, bf16[128,1024]{1,0:T(8,128)(2,1)}, bf16[128,1024]{1,0:T(8,128)(2,1)}, bf...) custom-call(s32[1]{0:T(128)} %bitcast.ex_ref, ...), custom_call_target="tpu_custom_call" | custom-call | tf_op jit(solution)/shard_map/pallas_call | solution.py:155
  155.7 7.2 %shard_map.216 = (bf16[4,2,128,1024]{3,2,1,0:T(8,128)(2,1)}, bf16[4,2,128,1024]{3,2,1,0:T(8,128)(2,1)}) custom-call(s32[1]{0:T(128)} %bitcast.35.core_ref, bf16[512,1024]{1,0:T(8,128)(2,1)} %get-tuple-element.114.x_ref, bf16[512,1024]{1,0:T(8,128)(2,1)} %get-tuple-element.119.g_ref, bf16[512,1024]{1,0:T(8,128)(2,1)} %get-tuple-element.120.act_ref, ...), custom_call_target="tpu_custom_call" | custom-call | tf_op jit(solution)/shard_map/pallas_call | solution.py:155
  163.4 4.0 %collective-permute-done.2 = bf16[4,2,128,1024]{3,2,1,0:T(8,128)(2,1)S(1)} collective-permute-done((bf16[4,2,128,1024]{3,2,1,0:T(8,128)(2,1)}, bf16[4,2,128,1024]{3,2,1,0:T(8,128)(2,1)S(1)}, u32[]{:S(2)}, u32[]{:S(2)}) %collective-permute-start.2) | collective-permute-done | bytes 2097184 | tf_op jit(solution)/shard_map/ppermute | solution.py:77
  167.4 3.9 %add_convert_fusion = bf16[4,2,128,1024]{3,2,1,0:T(8,128)(2,1)} fusion(bf16[4,2,128,1024]{3,2,1,0:T(8,128)(2,1)S(1)} %collective-permute-done.2, bf16[4,2,128,1024]{3,2,1,0:T(8,128)(2,1)} %get-tuple-element.125), kind=kLoop, calls=%fused_computation | loop fusion | flops 4194304 | bytes 6291456 | tf_op jit(solution)/shard_map/convert_element_type | solution.py:903
  171.3 3.5 %all-to-all-start.4 = ((bf16[4,144,1024]{2,1,0:T(8,128)(2,1)}), bf16[4,144,1024]{2,1,0:T(8,128)(2,1)S(1)}, u32[]{:S(2)}, u32[]{:S(2)}) async-start(bf16[4,144,1024]{2,1,0:T(8,128)(2,1)} %get-tuple-element.117), calls=%async_computation.4 | async-start | bytes 2359296 | tf_op jit(solution)/shard_map/all_to_all | solution.py:59
  175.1 12.4 %shard_map.217 = (f32[2,160,1024]{2,1,0:T(8,128)}, bf16[2,160,1024]{2,1,0:T(8,128)(2,1)}, bf16[320,2048]{1,0:T(8,128)(2,1)}, bf16[320,2048]{1,0:T(8,128)(2,1)}) custom-call(bf16[2,160,1024]{2,1,0:T(8,128)(2,1)} %get-tuple-element.118.own_ref.own_x.own_g, bf16[2,160,1024]{2,1,0:T(8,128)(2,1)} %copy-done.1, bf16[4,512,1024]{2,1,0:T(8,128)(2,1)} %bitcast.168, ...), custom_call_target="tpu_custom_call" | custom-call | tf_op jit(solution)/shard_map/pallas_call | solution.py:155
  187.9 8.7 %shard_map.218 = bf16[4,1024,1024]{2,1,0:T(8,128)(2,1)} custom-call(bf16[2,160,1024]{2,1,0:T(8,128)(2,1)} %get-tuple-element.118.own_ref.own_x.own_g, bf16[2,160,1024]{2,1,0:T(8,128)(2,1)} %copy-done.1, bf16[2,160,1024]{2,1,0:T(8,128)(2,1)} %get-tuple-element.118.own_ref.own_x.own_g, bf16[2,160,1024]{2,1,0:T(8,128)(2,1)} %copy-done.1, ...), custom_call_target="tpu_custom_call" | custom-call | tf_op jit(solution)/shard_map/pallas_call | solution.py:155
  197.6 6.6 %all-to-all-done.4.pay_ref = bf16[4,144,1024]{2,1,0:T(8,128)(2,1)S(1)} async-done(((bf16[4,144,1024]{2,1,0:T(8,128)(2,1)}), bf16[4,144,1024]{2,1,0:T(8,128)(2,1)S(1)}, u32[]{:S(2)}, u32[]{:S(2)}) %all-to-all-start.4) | async-done | bytes 1179680 | tf_op jit(solution)/shard_map/all_to_all | solution.py:59
  216.7 5.6 %collective-permute-done.5.refs_2_ = bf16[2,40,1024]{2,1,0:T(8,128)(2,1)S(1)} collective-permute-done((bf16[2,40,1024]{2,1,0:T(8,128)(2,1)S(1)}, bf16[2,40,1024]{2,1,0:T(8,128)(2,1)S(1)}, u32[]{:S(2)}, u32[]{:S(2)}) %collective-permute-start.5) | collective-permute-done | bytes 163872 | tf_op jit(solution)/shard_map/ppermute | solution.py:69
  223.7 5.4 %shard_map.219 = (f32[128,1024]{1,0:T(8,128)}, bf16[128,1024]{1,0:T(8,128)(2,1)}, bf16[4,128,256]{2,1,0:T(8,128)(2,1)}, f32[8,1024]{1,0:T(8,128)}, f32[128,1024]{1,0:T(8,128)}) custom-call(s32[1]{0:T(128)} %bitcast.ex_ref, bf16[4,144,1024]{2,1,0:T(8,128)(2,1)} %copy-done.3, s32[128,1]{1,0:T(8,128)} %copy.101.slot_ref, ...), custom_call_target="tpu_custom_call" | custom-call | tf_op jit(solution)/shard_map/pallas_call | solution.py:155
  229.1 3.7 %all-to-all-start.5 = ((bf16[4,128,256]{2,1,0:T(8,128)(2,1)}), bf16[4,128,256]{2,1,0:T(8,128)(2,1)S(1)}, u32[]{:S(2)}, u32[]{:S(2)}) async-start(bf16[4,128,256]{2,1,0:T(8,128)(2,1)} %get-tuple-element.143), calls=%async_computation.5 | async-start | bytes 524288 | tf_op jit(solution)/shard_map/all_to_all | solution.py:59
  235.9 5.5 %all-to-all-done.5 = bf16[4,128,256]{2,1,0:T(8,128)(2,1)S(1)} async-done(((bf16[4,128,256]{2,1,0:T(8,128)(2,1)}), bf16[4,128,256]{2,1,0:T(8,128)(2,1)S(1)}, u32[]{:S(2)}, u32[]{:S(2)}) %all-to-all-start.5) | async-done | bytes 262176 | tf_op jit(solution)/shard_map/all_to_all | solution.py:59
  247.6 7.5 %shard_map.221 = (bf16[512,256]{1,0:T(8,128)(2,1)}, bf16[512,256]{1,0:T(8,128)(2,1)}, bf16[512,256]{1,0:T(8,128)(2,1)}) custom-call(s32[1]{0:T(128)} %bitcast.195, bf16[512,768]{1,0:T(8,128)(2,1)} %get-tuple-element.107.q_ref.k_ref.v_ref, bf16[512,768]{1,0:T(8,128)(2,1)} %get-tuple-element.107.q_ref.k_ref.v_ref, ...), custom_call_target="tpu_custom_call" | custom-call | flops 23000000512 | tf_op jit(solution)/shard_map/pallas_call | solution.py:155
  255.1 4.6 %shard_map.222 = (bf16[4,144,768]{2,1,0:T(8,128)(2,1)}, bf16[4,144,768]{2,1,0:T(8,128)(2,1)}) custom-call(s32[1]{0:T(128)} %bitcast.35.core_ref, bf16[512,1024]{1,0:T(8,128)(2,1)} %get-tuple-element.151.x_ref, bf16[1024,768]{1,0:T(8,128)(2,1)} %get-tuple-element.152.w_ref, f32[1,1024]{1,0:T(1,128)} %get-tuple-element.214.gain_ref, ...), custom_call_target="tpu_custom_call" | custom-call | tf_op jit(solution)/shard_map/pallas_call | solution.py:155
  259.6 4.5 %shard_map.223 = (bf16[128,1024]{1,0:T(8,128)(2,1)}, bf16[128,1024]{1,0:T(8,128)(2,1)}, bf16[128,1024]{1,0:T(8,128)(2,1)}, bf16[128,1024]{1,0:T(8,128)(2,1)}) custom-call(s32[1]{0:T(128)} %bitcast.ex_ref, bf16[512,256]{1,0:T(8,128)(2,1)} %get-tuple-element.157.dq_ref, bf16[512,256]{1,0:T(8,128)(2,1)} %get-tuple-element.154.dk_ref, ...), custom_call_target="tpu_custom_call" | custom-call | tf_op jit(solution)/shard_map/pallas_call | solution.py:155
  266.9 4.9 %collective-permute-done.8 = bf16[2,128,1024]{2,1,0:T(8,128)(2,1)S(1)} collective-permute-done((bf16[2,128,1024]{2,1,0:T(8,128)(2,1)S(1)}, bf16[2,128,1024]{2,1,0:T(8,128)(2,1)S(1)}, u32[]{:S(2)}, u32[]{:S(2)}) %collective-permute-start.8) | collective-permute-done | bytes 524320 | tf_op jit(solution)/shard_map/ppermute | solution.py:86
  288.6 9.8 %collective-permute-done.18.refs_2_ = bf16[128,1024]{1,0:T(8,128)(2,1)S(1)} collective-permute-done((bf16[128,1024]{1,0:T(8,128)(2,1)S(1)}, bf16[128,1024]{1,0:T(8,128)(2,1)S(1)}, u32[]{:S(2)}, u32[]{:S(2)}) %collective-permute-start.18) | collective-permute-done | bytes 262176 | tf_op jit(solution)/shard_map/ppermute | solution.py:69
  301.5 7.8 %all-to-all-start.6 = ((bf16[4,32,2944]{2,1,0:T(8,128)(2,1)}), bf16[4,32,2944]{2,1,0:T(8,128)(2,1)S(1)}, u32[]{:S(2)}, u32[]{:S(2)}) async-start(bf16[4,32,2944]{2,1,0:T(8,128)(2,1)} %fusion.4), calls=%async_computation.7 | async-start | bytes 1507328 | tf_op jit(solution)/shard_map/all_to_all | solution.py:59
  309.3 6.9 %reduce-scatter.5.cloned.1.call-done = bf16[1024,1024]{1,0:T(8,128)(2,1)} async-done(((bf16[4096,1024]{1,0:T(8,128)(2,1)}), bf16[1024,1024]{1,0:T(8,128)(2,1)}) %reduce-scatter.5.cloned.1.call-update) | async-done | bytes 2097168 | tf_op jit(solution)/shard_map/reduce_scatter | solution.py:927
  325.5 3.8 %shard_map.225 = (f32[128,4096]{1,0:T(8,128)}, f32[512,1024]{1,0:T(8,128)}) custom-call(s32[1]{0:T(128)} %bitcast.35.core_ref, bf16[2,128,1024]{2,1,0:T(8,128)(2,1)} %get-tuple-element.204.own_ref, bf16[2,128,1024]{2,1,0:T(8,128)(2,1)} %copy-done.12, bf16[512,1024]{1,0:T(8,128)(2,1)} %get-tuple-element.197.down_ref), custom_call_target="tpu_custom_call" | custom-call | tf_op jit(solution)/shard_map/pallas_call | solution.py:155
  (204 shorter events, 83.7 us)
Async XLA Ops:
  7.2 66.5 %all-gather.9.cloned.1.call-start = ((), (), s32[]{:S(2)}) async-start(), calls=%async_computation.13 | async-start | bytes 5242880 | tf_op jit(solution)/shard_map/all_gather | solution.py:805
  9.2 8.7 %collective-permute-start = (bf16[128,2048]{0,1:T(8,128)(2,1)S(1)}, bf16[128,2048]{0,1:T(8,128)(2,1)S(1)}, u32[]{:S(2)}, u32[]{:S(2)}) collective-permute-start(bf16[128,2048]{0,1:T(8,128)(2,1)S(1)} %bitcast.190), channel_id=1, source_target_pairs={{0,4},{4,0},{1,5},{5,1},{2,6},{6,2},{3,7},{7,3},{8,12},{12,8},{9,1... | collective-permute-start | bytes 1572872 | tf_op jit(solution)/shard_map/ppermute | solution.py:77
  11.7 26.6 %all-to-all-start = ((bf16[4,32,3072]{2,1,0:T(8,128)(2,1)}), bf16[4,32,3072]{2,1,0:T(8,128)(2,1)S(1)}, u32[]{:S(2)}, u32[]{:S(2)}) async-start(bf16[4,32,3072]{2,1,0:T(8,128)(2,1)} %pad_maximum_fusion.1), calls=%async_computation | async-start | bytes 1572864 | tf_op jit(solution)/shard_map/all_to_all | solution.py:59
  40.6 33.1 %all-to-all-start.1 = ((bf16[4,128,1024]{2,1,0:T(8,128)(2,1)}), bf16[4,128,1024]{2,1,0:T(8,128)(2,1)S(1)}, u32[]{:S(2)}, u32[]{:S(2)}) async-start(bf16[4,128,1024]{2,1,0:T(8,128)(2,1)} %broadcast_in_dim.55), calls=%async_computation.1 | async-start | bytes 2097152 | tf_op jit(solution)/shard_map/all_to_all | solution.py:59
  44.2 75.3 %all-gather.5.cloned.1.call-start = ((), (), s32[]{:S(2)}) async-start(), calls=%async_computation.9 | async-start | bytes 7077888 | tf_op jit(solution)/shard_map/all_gather | solution.py:856
  73.8 101.4 %all-gather.7.cloned.1.call-start = ((), (), s32[]{:S(2)}) async-start(), calls=%async_computation.10 | async-start | bytes 5242880 | tf_op jit(solution)/shard_map/all_gather | solution.py:869
  74.7 30.9 %all-to-all-start.2 = ((bf16[4,128,1024]{2,1,0:T(8,128)(2,1)}), bf16[4,128,1024]{2,1,0:T(8,128)(2,1)S(1)}, u32[]{:S(2)}, u32[]{:S(2)}) async-start(bf16[4,128,1024]{2,1,0:T(8,128)(2,1)} %broadcast_in_dim.54), calls=%async_computation.2 | async-start | bytes 2097152 | tf_op jit(solution)/shard_map/all_to_all | solution.py:59
  106.6 28.9 %all-to-all-start.3 = ((bf16[4,512,256]{2,1,0:T(8,128)(2,1)}), bf16[4,512,256]{2,1,0:T(8,128)(2,1)S(1)}, u32[]{:S(2)}, u32[]{:S(2)}) async-start(bf16[4,512,256]{2,1,0:T(8,128)(2,1)} %shard_map.213), calls=%async_computation.3 | async-start | bytes 2097152 | tf_op jit(solution)/shard_map/all_to_all | solution.py:59
  110.1 188.5 %reduce-scatter.3.cloned.1.call-start = ((), (), s32[]{:S(2)}) async-start(), calls=%async_computation.11 | async-start | bytes 2621440 | tf_op jit(solution)/shard_map/reduce_scatter | solution.py:905
  155.6 7.3 %collective-permute-start.1 = (bf16[2,160,1024]{2,1,0:T(8,128)(2,1)}, bf16[2,160,1024]{2,1,0:T(8,128)(2,1)S(1)}, u32[]{:S(2)}, u32[]{:S(2)}) collective-permute-start(bf16[2,160,1024]{2,1,0:T(8,128)(2,1)} %get-tuple-element.118.own_ref.own_x.own_g), channel_id=1, source_target_pairs={{0,4},{4,0},{1,5},{5,1},{2,6},{6,2},{3,7},{7,3},{8,12},{12,8},{9,1... | collective-permute-start | bytes 1966088 | tf_op jit(solution)/shard_map/ppermute | solution.py:77
  162.9 4.5 %collective-permute-start.2 = (bf16[4,2,128,1024]{3,2,1,0:T(8,128)(2,1)}, bf16[4,2,128,1024]{3,2,1,0:T(8,128)(2,1)S(1)}, u32[]{:S(2)}, u32[]{:S(2)}) collective-permute-start(bf16[4,2,128,1024]{3,2,1,0:T(8,128)(2,1)} %get-tuple-element.126), channel_id=1, source_target_pairs={{0,4},{4,0},{1,5},{5,1},{2,6},{6,2},{3,7},{7,3},{8,12},{12,8},{9,1... | collective-permute-start | bytes 6291464 | tf_op jit(solution)/shard_map/ppermute | solution.py:77
  171.3 32.9 %all-to-all-start.4 = ((bf16[4,144,1024]{2,1,0:T(8,128)(2,1)}), bf16[4,144,1024]{2,1,0:T(8,128)(2,1)S(1)}, u32[]{:S(2)}, u32[]{:S(2)}) async-start(bf16[4,144,1024]{2,1,0:T(8,128)(2,1)} %get-tuple-element.117), calls=%async_computation.4 | async-start | bytes 2359296 | tf_op jit(solution)/shard_map/all_to_all | solution.py:59
  174.9 141.3 %reduce-scatter.5.cloned.1.call-start = ((), (), s32[]{:S(2)}) async-start(), calls=%async_computation.12 | async-start | bytes 10485760 | tf_op jit(solution)/shard_map/reduce_scatter | solution.py:927
  187.5 9.1 %collective-permute-start.3 = (bf16[2,160,1024]{2,1,0:T(8,128)(2,1)}, bf16[2,160,1024]{2,1,0:T(8,128)(2,1)S(1)}, u32[]{:S(2)}, u32[]{:S(2)}) collective-permute-start(bf16[2,160,1024]{2,1,0:T(8,128)(2,1)} %get-tuple-element.133), channel_id=1, source_target_pairs={{0,4},{4,0},{1,5},{5,1},{2,6},{6,2},{3,7},{7,3},{8,12},{12,8},{9,1... | collective-permute-start | bytes 1966088 | tf_op jit(solution)/shard_map/ppermute | solution.py:77
  207.7 9.0 %collective-permute-start.4 = (bf16[2,40,1024]{2,1,0:T(8,128)(2,1)S(1)}, bf16[2,40,1024]{2,1,0:T(8,128)(2,1)S(1)}, u32[]{:S(2)}, u32[]{:S(2)}) collective-permute-start(bf16[2,40,1024]{2,1,0:T(8,128)(2,1)S(1)} %copy-done.21), channel_id=1, source_target_pairs={{0,1},{1,2},{2,3},{3,0},{4,5},{5,6},{6,7},{7,4},{8,9},{9,10},{10,1... | collective-permute-start | bytes 491528 | tf_op jit(solution)/shard_map/ppermute | solution.py:69
  207.7 14.7 %collective-permute-start.5 = (bf16[2,40,1024]{2,1,0:T(8,128)(2,1)S(1)}, bf16[2,40,1024]{2,1,0:T(8,128)(2,1)S(1)}, u32[]{:S(2)}, u32[]{:S(2)}) collective-permute-start(bf16[2,40,1024]{2,1,0:T(8,128)(2,1)S(1)} %get-tuple-element.140), channel_id=1, source_target_pairs={{0,2},{1,3},{2,0},{3,1},{4,6},{5,7},{6,4},{7,5},{8,10},{9,11},{10,... | collective-permute-start | bytes 491528 | tf_op jit(solution)/shard_map/ppermute | solution.py:69
  209.7 12.7 %collective-permute-start.6 = (bf16[2,40,1024]{2,1,0:T(8,128)(2,1)S(1)}, bf16[2,40,1024]{2,1,0:T(8,128)(2,1)S(1)}, u32[]{:S(2)}, u32[]{:S(2)}) collective-permute-start(bf16[2,40,1024]{2,1,0:T(8,128)(2,1)S(1)} %get-tuple-element.141), channel_id=1, source_target_pairs={{0,3},{1,0},{2,1},{3,2},{4,7},{5,4},{6,5},{7,6},{8,11},{9,8},{10,9... | collective-permute-start | bytes 491528 | tf_op jit(solution)/shard_map/ppermute | solution.py:69
  229.1 12.3 %all-to-all-start.5 = ((bf16[4,128,256]{2,1,0:T(8,128)(2,1)}), bf16[4,128,256]{2,1,0:T(8,128)(2,1)S(1)}, u32[]{:S(2)}, u32[]{:S(2)}) async-start(bf16[4,128,256]{2,1,0:T(8,128)(2,1)} %get-tuple-element.143), calls=%async_computation.5 | async-start | bytes 524288 | tf_op jit(solution)/shard_map/all_to_all | solution.py:59
  241.4 22.8 %collective-permute-start.11 = (bf16[128,1024]{1,0:T(8,128)(2,1)}, bf16[128,1024]{1,0:T(8,128)(2,1)}, u32[]{:S(2)}, u32[]{:S(2)}) collective-permute-start(bf16[128,1024]{1,0:T(8,128)(2,1)} %get-tuple-element.169), channel_id=1, source_target_pairs={{0,3},{1,0},{2,1},{3,2},{4,7},{5,4},{6,5},{7,6},{8,11},{9,8},{10,9... | collective-permute-start | bytes 786440 | tf_op jit(solution)/shard_map/ppermute | solution.py:69
  242.9 24.0 %collective-permute-start.10 = (bf16[128,1024]{1,0:T(8,128)(2,1)}, bf16[128,1024]{1,0:T(8,128)(2,1)}, u32[]{:S(2)}, u32[]{:S(2)}) collective-permute-start(bf16[128,1024]{1,0:T(8,128)(2,1)} %get-tuple-element.167), channel_id=1, source_target_pairs={{0,2},{1,3},{2,0},{3,1},{4,6},{5,7},{6,4},{7,5},{8,10},{9,11},{10,... | collective-permute-start | bytes 786440 | tf_op jit(solution)/shard_map/ppermute | solution.py:69
  243.1 23.9 %collective-permute-start.9 = (bf16[128,1024]{1,0:T(8,128)(2,1)}, bf16[128,1024]{1,0:T(8,128)(2,1)}, u32[]{:S(2)}, u32[]{:S(2)}) collective-permute-start(bf16[128,1024]{1,0:T(8,128)(2,1)} %get-tuple-element.165), channel_id=1, source_target_pairs={{0,1},{1,2},{2,3},{3,0},{4,5},{5,6},{6,7},{7,4},{8,9},{9,10},{10,1... | collective-permute-start | bytes 786440 | tf_op jit(solution)/shard_map/ppermute | solution.py:69
  246.0 25.8 %collective-permute-start.8 = (bf16[2,128,1024]{2,1,0:T(8,128)(2,1)S(1)}, bf16[2,128,1024]{2,1,0:T(8,128)(2,1)S(1)}, u32[]{:S(2)}, u32[]{:S(2)}) collective-permute-start(bf16[2,128,1024]{2,1,0:T(8,128)(2,1)S(1)} %fusion.5), channel_id=1, source_target_pairs={{0,8},{8,0},{16,24},{24,16},{1,9},{9,1},{17,25},{25,17},{2,10},{10... | collective-permute-start | bytes 1572872 | tf_op jit(solution)/shard_map/ppermute | solution.py:86
  272.1 9.2 %collective-permute-start.20 = (bf16[128,1024]{1,0:T(8,128)(2,1)S(1)}, bf16[128,1024]{1,0:T(8,128)(2,1)S(1)}, u32[]{:S(2)}, u32[]{:S(2)}) collective-permute-start(bf16[128,1024]{1,0:T(8,128)(2,1)S(1)} %fusion.7), channel_id=1, source_target_pairs={{0,16},{8,24},{16,0},{24,8},{1,17},{9,25},{17,1},{25,9},{2,18},{10... | collective-permute-start | bytes 786440 | tf_op jit(solution)/shard_map/ppermute | solution.py:86
  274.9 9.9 %collective-permute-start.13 = (bf16[2,144,384]{2,1,0:T(8,128)(2,1)S(1)}, bf16[2,144,384]{2,1,0:T(8,128)(2,1)S(1)}, u32[]{:S(2)}, u32[]{:S(2)}) collective-permute-start(bf16[2,144,384]{2,1,0:T(8,128)(2,1)S(1)} %fusion.8), channel_id=1, source_target_pairs={{0,8},{8,0},{16,24},{24,16},{1,9},{9,1},{17,25},{25,17},{2,10},{10... | collective-permute-start | bytes 663560 | tf_op jit(solution)/shard_map/ppermute | solution.py:86
  276.4 9.2 %collective-permute-start.14 = (bf16[2,144,384]{2,1,0:T(8,128)(2,1)S(1)}, bf16[2,144,384]{2,1,0:T(8,128)(2,1)S(1)}, u32[]{:S(2)}, u32[]{:S(2)}) collective-permute-start(bf16[2,144,384]{2,1,0:T(8,128)(2,1)S(1)} %select_convert_fusion.1), channel_id=1, source_target_pairs={{0,16},{8,24},{16,0},{24,8},{1,17},{9,25},{17,1},{25,9},{2,18},{10... | collective-permute-start | bytes 663560 | tf_op jit(solution)/shard_map/ppermute | solution.py:86
  277.4 11.2 %collective-permute-start.17 = (bf16[128,1024]{1,0:T(8,128)(2,1)S(1)}, bf16[128,1024]{1,0:T(8,128)(2,1)S(1)}, u32[]{:S(2)}, u32[]{:S(2)}) collective-permute-start(bf16[128,1024]{1,0:T(8,128)(2,1)S(1)} %copy-done.31), channel_id=1, source_target_pairs={{0,1},{1,2},{2,3},{3,0},{4,5},{5,6},{6,7},{7,4},{8,9},{9,10},{10,1... | collective-permute-start | bytes 786440 | tf_op jit(solution)/shard_map/ppermute | solution.py:69
  279.2 19.1 %collective-permute-start.18 = (bf16[128,1024]{1,0:T(8,128)(2,1)S(1)}, bf16[128,1024]{1,0:T(8,128)(2,1)S(1)}, u32[]{:S(2)}, u32[]{:S(2)}) collective-permute-start(bf16[128,1024]{1,0:T(8,128)(2,1)S(1)} %copy-done.30), channel_id=1, source_target_pairs={{0,2},{1,3},{2,0},{3,1},{4,6},{5,7},{6,4},{7,5},{8,10},{9,11},{10,... | collective-permute-start | bytes 786440 | tf_op jit(solution)/shard_map/ppermute | solution.py:69
  281.3 17.0 %collective-permute-start.19 = (bf16[128,1024]{1,0:T(8,128)(2,1)S(1)}, bf16[128,1024]{1,0:T(8,128)(2,1)S(1)}, u32[]{:S(2)}, u32[]{:S(2)}) collective-permute-start(bf16[128,1024]{1,0:T(8,128)(2,1)S(1)} %copy-done.29), channel_id=1, source_target_pairs={{0,3},{1,0},{2,1},{3,2},{4,7},{5,4},{6,5},{7,6},{8,11},{9,8},{10,9... | collective-permute-start | bytes 786440 | tf_op jit(solution)/shard_map/ppermute | solution.py:69
  285.8 12.6 %collective-permute-start.16 = (bf16[144,384]{1,0:T(8,128)(2,1)S(1)}, bf16[144,384]{1,0:T(8,128)(2,1)S(1)}, u32[]{:S(2)}, u32[]{:S(2)}) collective-permute-start(bf16[144,384]{1,0:T(8,128)(2,1)S(1)} %fusion.14), channel_id=1, source_target_pairs={{0,8},{8,0},{16,24},{24,16},{1,9},{9,1},{17,25},{25,17},{2,10},{10... | collective-permute-start | bytes 331784 | tf_op jit(solution)/shard_map/ppermute | solution.py:86
  287.4 11.0 %collective-permute-start.15 = (bf16[144,384]{1,0:T(8,128)(2,1)S(1)}, bf16[144,384]{1,0:T(8,128)(2,1)S(1)}, u32[]{:S(2)}, u32[]{:S(2)}) collective-permute-start(bf16[144,384]{1,0:T(8,128)(2,1)S(1)} %fusion.13), channel_id=1, source_target_pairs={{0,16},{8,24},{16,0},{24,8},{1,17},{9,25},{17,1},{25,9},{2,18},{10... | collective-permute-start | bytes 331784 | tf_op jit(solution)/shard_map/ppermute | solution.py:86
  301.5 27.8 %all-to-all-start.6 = ((bf16[4,32,2944]{2,1,0:T(8,128)(2,1)}), bf16[4,32,2944]{2,1,0:T(8,128)(2,1)S(1)}, u32[]{:S(2)}, u32[]{:S(2)}) async-start(bf16[4,32,2944]{2,1,0:T(8,128)(2,1)} %fusion.4), calls=%async_computation.7 | async-start | bytes 1507328 | tf_op jit(solution)/shard_map/all_to_all | solution.py:59
  319.7 5.1 %collective-permute-start.21 = (bf16[2,128,1024]{2,1,0:T(8,128)(2,1)S(1)}, bf16[2,128,1024]{2,1,0:T(8,128)(2,1)S(1)}, u32[]{:S(2)}, u32[]{:S(2)}) collective-permute-start(bf16[2,128,1024]{2,1,0:T(8,128)(2,1)S(1)} %get-tuple-element.203), channel_id=1, source_target_pairs={{0,4},{4,0},{1,5},{5,1},{2,6},{6,2},{3,7},{7,3},{8,12},{12,8},{9,1... | collective-permute-start | bytes 1572872 | tf_op jit(solution)/shard_map/ppermute | solution.py:77
  (35 other events, 148.4 us)
Sparse Core Ops, SparseCore 0:
  9.9 60.0 all-gather.8
  73.9 45.5 all-gather.4
  121.3 52.6 all-gather.6
  176.9 35.1 reduce-scatter.2
  215.3 100.7 reduce-scatter.4

commit v4 on v3

--- a/solution.py
+++ b/solution.py
@@ -959,6 +959,7 @@
     out_sums = turn_all([after(piece, dattended) for piece in out_parts])
     out_core = out_keep.astype(F32) + other_core(out_send).astype(F32)
     out_fold = Fold((out_core,))
+    out_fold.orders = [chip_bits()[::-1]]
     out_fold.send()
 
     dparts = attend_back(qkv, dattended, doc_split, head_cols)

time: 342 us -> 342 us (level)
  transfers between devices with their start and end apart: 34 -> 34, of which waited for: 18 -> 17; matrix products, arithmetic and copies ran while one was open for 10% -> 10% of each run, Pallas kernels for 26% -> 26%
where the time goes in v4:
time: 342 us; the launch traced here: 341 us
  waiting for transfers between devices  108 us (32%)
  Pallas kernels  89.5 us (26%)
  starting transfers between devices  54.6 us (16%)
  local copies, waits for them, and re-layouts  29.3 us (9%)
  blocking collectives  27.7 us (8%)
  other arithmetic  17 us (5%)
  between operations  14.4 us (4%)
    pallas_call x14, Pallas kernels, call(): pl.pallas_call(body, grid=grid, in_specs=in_specs, out_specs=out_specs, o...  89.5 us
    all_to_all x7, waiting for transfers between devices, swap(): return lax.all_to_all(values, axis, split_axis=0, concat_axis=0, tiled=True)  59.5 us
    all_to_all x7, starting transfers between devices, swap(): return lax.all_to_all(values, axis, split_axis=0, concat_axis=0, tiled=True)  33 us
    all_gather x2, blocking collectives, gather_small(): lax.all_gather(values[k:k + step], axes, axis=0, tiled=True)  27.7 us
    ppermute x9, waiting for transfers between devices, turn(): lax.ppermute(values, 'expert', [(i, (i + step) % count) for i in range(co...  20 us
    ppermute x9, starting transfers between devices, turn(): lax.ppermute(values, 'expert', [(i, (i + step) % count) for i in range(co...  11.4 us
    ppermute x6, starting transfers between devices, flip(): return lax.ppermute(values, 'chip', [(i, i ^ bit) for i in chips])  8.1 us
    ppermute x6, waiting for transfers between devices, flip(): return lax.ppermute(values, 'chip', [(i, i ^ bit) for i in chips])  7.83 us
  transfers between devices with their start and end apart: 34, of which 17 were waited for; matrix products, arithmetic and copies ran while one was open for 10% of the time, Pallas kernels for 26%

profile of v4, /device:TPU:0, one launch (start us, length us, event | category | flops | bytes accessed | tf_op | source)
XLA Modules:
  0.0 340.6 jit_solution(18151154451658641330)
XLA Ops:
  11.7 6.2 %all-to-all-start = ((bf16[4,32,3072]{2,1,0:T(8,128)(2,1)}), bf16[4,32,3072]{2,1,0:T(8,128)(2,1)S(1)}, u32[]{:S(2)}, u32[]{:S(2)}) async-start(bf16[4,32,3072]{2,1,0:T(8,128)(2,1)} %pad_maximum_fusion.1), calls=%async_computation | async-start | bytes 1572864 | tf_op jit(solution)/shard_map/all_to_all | solution.py:59
  19.5 18.8 %all-to-all-done = bf16[4,32,3072]{2,1,0:T(8,128)(2,1)S(1)} async-done(((bf16[4,32,3072]{2,1,0:T(8,128)(2,1)}), bf16[4,32,3072]{2,1,0:T(8,128)(2,1)S(1)}, u32[]{:S(2)}, u32[]{:S(2)}) %all-to-all-start) | async-done | bytes 786464 | tf_op jit(solution)/shard_map/all_to_all | solution.py:59
  40.6 3.6 %all-to-all-start.1 = ((bf16[4,128,1024]{2,1,0:T(8,128)(2,1)}), bf16[4,128,1024]{2,1,0:T(8,128)(2,1)S(1)}, u32[]{:S(2)}, u32[]{:S(2)}) async-start(bf16[4,128,1024]{2,1,0:T(8,128)(2,1)} %broadcast_in_dim.55), calls=%async_computation.1 | async-start | bytes 2097152 | tf_op jit(solution)/shard_map/all_to_all | solution.py:59
  45.4 13.9 %all_gather.16 = bf16[448,768]{1,0:T(8,128)(2,1)S(1)} all-gather(bf16[56,768]{1,0:T(8,128)(2,1)S(1)} %fusion.13), channel_id=1, replica_groups=mesh['chip'=4,'core'=2,'expert'=4] {'chip','core'}, dimensions={0}, use_global_device_ids=true | all-gather | bytes 774144 | tf_op jit(solution)/shard_map/all_gather | solution.py:104
  59.3 13.8 %all_gather.15 = bf16[640,768]{1,0:T(8,128)(2,1)} all-gather(bf16[80,768]{1,0:T(8,128)(2,1)S(1)} %slice.191), channel_id=1, replica_groups=mesh['chip'=4,'core'=2,'expert'=4] {'chip','core'}, dimensions={0}, use_global_device_ids=true | all-gather | bytes 1105920 | tf_op jit(solution)/shard_map/all_gather | solution.py:104
  74.7 4.6 %all-to-all-start.2 = ((bf16[4,128,1024]{2,1,0:T(8,128)(2,1)}), bf16[4,128,1024]{2,1,0:T(8,128)(2,1)S(1)}, u32[]{:S(2)}, u32[]{:S(2)}) async-start(bf16[4,128,1024]{2,1,0:T(8,128)(2,1)} %broadcast_in_dim.54), calls=%async_computation.2 | async-start | bytes 2097152 | tf_op jit(solution)/shard_map/all_to_all | solution.py:59
  79.3 4.5 %shard_map.212 = (bf16[512,768]{1,0:T(8,128)(2,1)}, bf16[512,1024]{1,0:T(8,128)(2,1)}, bf16[1024,768]{1,0:T(8,128)(2,1)}) custom-call(bf16[512,1024]{1,0:T(8,128)(2,1)} %bitcast.141, f32[1,1024]{1,0:T(1,128)} %get-tuple-element.214.gain_ref, bf16[8,80,768]{2,1,0:T(8,128)(2,1)} %bitcast.153, bf16[8,56,768]{2,1,0:T(8,128)(2,1)} %bitcast.155), custom_call_target="tpu_custom_call" | custom-call | tf_op jit(solution)/shard_map/pallas_call | solution.py:155
  83.8 6.1 %shard_map.213 = bf16[4,512,256]{2,1,0:T(8,128)(2,1)} custom-call(s32[1]{0:T(128)} %bitcast.173, bf16[512,768]{1,0:T(8,128)(2,1)} %get-tuple-element.107.q_ref.k_ref.v_ref, bf16[512,768]{1,0:T(8,128)(2,1)} %get-tuple-element.107.q_ref.k_ref.v_ref, bf16[512,768]{1,0:T(8,128)(2,1)} %get-tuple-element.107.q_ref.k_ref.v_ref), custom_call_target="tpu_custom_call" | custom-call | tf_op jit(solution)/shard_map/pallas_call | solution.py:155
  89.9 15.7 %all-to-all-done.2 = bf16[4,128,1024]{2,1,0:T(8,128)(2,1)S(1)} async-done(((bf16[4,128,1024]{2,1,0:T(8,128)(2,1)}), bf16[4,128,1024]{2,1,0:T(8,128)(2,1)S(1)}, u32[]{:S(2)}, u32[]{:S(2)}) %all-to-all-start.2) | async-done | bytes 1048608 | tf_op jit(solution)/shard_map/all_to_all | solution.py:59
  112.5 6.9 %all-gather.5.cloned.1.call-done = bf16[3072,1024]{1,0:T(8,128)(2,1)} async-done(((bf16[384,1024]{1,0:T(8,128)(2,1)}), bf16[3072,1024]{1,0:T(8,128)(2,1)}) %all-gather.5.cloned.1.call-update) | async-done | bytes 6291472 | tf_op jit(solution)/shard_map/all_gather | solution.py:856
  122.6 12.9 %all-to-all-done.3.att_ref = bf16[4,512,256]{2,1,0:T(8,128)(2,1)S(1)} async-done(((bf16[4,512,256]{2,1,0:T(8,128)(2,1)}), bf16[4,512,256]{2,1,0:T(8,128)(2,1)S(1)}, u32[]{:S(2)}, u32[]{:S(2)}) %all-to-all-start.3) | async-done | bytes 1048608 | tf_op jit(solution)/shard_map/all_to_all | solution.py:59
  136.4 5.7 %shard_map.214 = (f32[512,1024]{1,0:T(8,128)}, bf16[512,1024]{1,0:T(8,128)(2,1)}, f32[512,2]{1,0:T(8,128)}) custom-call(bf16[4,512,256]{2,1,0:T(8,128)(2,1)} %copy-done.2, bf16[512,1024]{1,0:T(8,128)(2,1)} %bitcast.142, bf16[1024,1024]{1,0:T(8,128)(2,1)} %bitcast.139, f32[1,1024]{1,0:T(1,128)} %get-tuple-element.213.gain_ref, bf16[16,1024]{1,0:T(8,128)(2,1)} %pad.24.mix_ref), custom_call_target="tpu_custom_call" | custom-call | tf_op jit(solution)/shard_map/pallas_call | solution.py:155
  142.1 13.5 %shard_map.215 = (bf16[128,1024]{1,0:T(8,128)(2,1)}, bf16[128,1024]{1,0:T(8,128)(2,1)}, bf16[128,1024]{1,0:T(8,128)(2,1)}, bf16[128,1024]{1,0:T(8,128)(2,1)}, bf...) custom-call(s32[1]{0:T(128)} %bitcast.ex_ref, ...), custom_call_target="tpu_custom_call" | custom-call | tf_op jit(solution)/shard_map/pallas_call | solution.py:155
  155.7 7.2 %shard_map.216 = (bf16[4,2,128,1024]{3,2,1,0:T(8,128)(2,1)}, bf16[4,2,128,1024]{3,2,1,0:T(8,128)(2,1)}) custom-call(s32[1]{0:T(128)} %bitcast.35.core_ref, bf16[512,1024]{1,0:T(8,128)(2,1)} %get-tuple-element.114.x_ref, bf16[512,1024]{1,0:T(8,128)(2,1)} %get-tuple-element.119.g_ref, bf16[512,1024]{1,0:T(8,128)(2,1)} %get-tuple-element.120.act_ref, ...), custom_call_target="tpu_custom_call" | custom-call | tf_op jit(solution)/shard_map/pallas_call | solution.py:155
  163.4 4.0 %collective-permute-done.2 = bf16[4,2,128,1024]{3,2,1,0:T(8,128)(2,1)S(1)} collective-permute-done((bf16[4,2,128,1024]{3,2,1,0:T(8,128)(2,1)}, bf16[4,2,128,1024]{3,2,1,0:T(8,128)(2,1)S(1)}, u32[]{:S(2)}, u32[]{:S(2)}) %collective-permute-start.2) | collective-permute-done | bytes 2097184 | tf_op jit(solution)/shard_map/ppermute | solution.py:77
  167.4 3.9 %add_convert_fusion = bf16[4,2,128,1024]{3,2,1,0:T(8,128)(2,1)} fusion(bf16[4,2,128,1024]{3,2,1,0:T(8,128)(2,1)S(1)} %collective-permute-done.2, bf16[4,2,128,1024]{3,2,1,0:T(8,128)(2,1)} %get-tuple-element.125), kind=kLoop, calls=%fused_computation | loop fusion | flops 4194304 | bytes 6291456 | tf_op jit(solution)/shard_map/convert_element_type | solution.py:903
  171.3 3.5 %all-to-all-start.4 = ((bf16[4,144,1024]{2,1,0:T(8,128)(2,1)}), bf16[4,144,1024]{2,1,0:T(8,128)(2,1)S(1)}, u32[]{:S(2)}, u32[]{:S(2)}) async-start(bf16[4,144,1024]{2,1,0:T(8,128)(2,1)} %get-tuple-element.117), calls=%async_computation.4 | async-start | bytes 2359296 | tf_op jit(solution)/shard_map/all_to_all | solution.py:59
  175.1 12.4 %shard_map.217 = (f32[2,160,1024]{2,1,0:T(8,128)}, bf16[2,160,1024]{2,1,0:T(8,128)(2,1)}, bf16[320,2048]{1,0:T(8,128)(2,1)}, bf16[320,2048]{1,0:T(8,128)(2,1)}) custom-call(bf16[2,160,1024]{2,1,0:T(8,128)(2,1)} %get-tuple-element.118.own_ref.own_x.own_g, bf16[2,160,1024]{2,1,0:T(8,128)(2,1)} %copy-done.1, bf16[4,512,1024]{2,1,0:T(8,128)(2,1)} %bitcast.147, ...), custom_call_target="tpu_custom_call" | custom-call | tf_op jit(solution)/shard_map/pallas_call | solution.py:155
  187.9 8.7 %shard_map.218 = bf16[4,1024,1024]{2,1,0:T(8,128)(2,1)} custom-call(bf16[2,160,1024]{2,1,0:T(8,128)(2,1)} %get-tuple-element.118.own_ref.own_x.own_g, bf16[2,160,1024]{2,1,0:T(8,128)(2,1)} %copy-done.1, bf16[2,160,1024]{2,1,0:T(8,128)(2,1)} %get-tuple-element.118.own_ref.own_x.own_g, bf16[2,160,1024]{2,1,0:T(8,128)(2,1)} %copy-done.1, ...), custom_call_target="tpu_custom_call" | custom-call | tf_op jit(solution)/shard_map/pallas_call | solution.py:155
  197.6 6.6 %all-to-all-done.4.pay_ref = bf16[4,144,1024]{2,1,0:T(8,128)(2,1)S(1)} async-done(((bf16[4,144,1024]{2,1,0:T(8,128)(2,1)}), bf16[4,144,1024]{2,1,0:T(8,128)(2,1)S(1)}, u32[]{:S(2)}, u32[]{:S(2)}) %all-to-all-start.4) | async-done | bytes 1179680 | tf_op jit(solution)/shard_map/all_to_all | solution.py:59
  216.7 5.6 %collective-permute-done.5.refs_2_ = bf16[2,40,1024]{2,1,0:T(8,128)(2,1)S(1)} collective-permute-done((bf16[2,40,1024]{2,1,0:T(8,128)(2,1)S(1)}, bf16[2,40,1024]{2,1,0:T(8,128)(2,1)S(1)}, u32[]{:S(2)}, u32[]{:S(2)}) %collective-permute-start.5) | collective-permute-done | bytes 163872 | tf_op jit(solution)/shard_map/ppermute | solution.py:69
  223.7 5.4 %shard_map.219 = (f32[128,1024]{1,0:T(8,128)}, bf16[128,1024]{1,0:T(8,128)(2,1)}, bf16[4,128,256]{2,1,0:T(8,128)(2,1)}, f32[8,1024]{1,0:T(8,128)}, f32[128,1024]{1,0:T(8,128)}) custom-call(s32[1]{0:T(128)} %bitcast.ex_ref, bf16[4,144,1024]{2,1,0:T(8,128)(2,1)} %copy-done.3, s32[128,1]{1,0:T(8,128)} %copy.81.slot_ref, ...), custom_call_target="tpu_custom_call" | custom-call | tf_op jit(solution)/shard_map/pallas_call | solution.py:155
  229.1 3.7 %all-to-all-start.5 = ((bf16[4,128,256]{2,1,0:T(8,128)(2,1)}), bf16[4,128,256]{2,1,0:T(8,128)(2,1)S(1)}, u32[]{:S(2)}, u32[]{:S(2)}) async-start(bf16[4,128,256]{2,1,0:T(8,128)(2,1)} %get-tuple-element.143), calls=%async_computation.5 | async-start | bytes 524288 | tf_op jit(solution)/shard_map/all_to_all | solution.py:59
  235.9 5.5 %all-to-all-done.5 = bf16[4,128,256]{2,1,0:T(8,128)(2,1)S(1)} async-done(((bf16[4,128,256]{2,1,0:T(8,128)(2,1)}), bf16[4,128,256]{2,1,0:T(8,128)(2,1)S(1)}, u32[]{:S(2)}, u32[]{:S(2)}) %all-to-all-start.5) | async-done | bytes 262176 | tf_op jit(solution)/shard_map/all_to_all | solution.py:59
  247.6 7.5 %shard_map.221 = (bf16[512,256]{1,0:T(8,128)(2,1)}, bf16[512,256]{1,0:T(8,128)(2,1)}, bf16[512,256]{1,0:T(8,128)(2,1)}) custom-call(s32[1]{0:T(128)} %bitcast.174, bf16[512,768]{1,0:T(8,128)(2,1)} %get-tuple-element.107.q_ref.k_ref.v_ref, bf16[512,768]{1,0:T(8,128)(2,1)} %get-tuple-element.107.q_ref.k_ref.v_ref, ...), custom_call_target="tpu_custom_call" | custom-call | flops 23000000512 | tf_op jit(solution)/shard_map/pallas_call | solution.py:155
  255.1 4.6 %shard_map.222 = (bf16[4,144,768]{2,1,0:T(8,128)(2,1)}, bf16[4,144,768]{2,1,0:T(8,128)(2,1)}) custom-call(s32[1]{0:T(128)} %bitcast.35.core_ref, bf16[512,1024]{1,0:T(8,128)(2,1)} %get-tuple-element.151.x_ref, bf16[1024,768]{1,0:T(8,128)(2,1)} %get-tuple-element.152.w_ref, f32[1,1024]{1,0:T(1,128)} %get-tuple-element.214.gain_ref, ...), custom_call_target="tpu_custom_call" | custom-call | tf_op jit(solution)/shard_map/pallas_call | solution.py:155
  259.7 4.5 %shard_map.223 = (bf16[128,1024]{1,0:T(8,128)(2,1)}, bf16[128,1024]{1,0:T(8,128)(2,1)}, bf16[128,1024]{1,0:T(8,128)(2,1)}, bf16[128,1024]{1,0:T(8,128)(2,1)}) custom-call(s32[1]{0:T(128)} %bitcast.ex_ref, bf16[512,256]{1,0:T(8,128)(2,1)} %get-tuple-element.157.dq_ref, bf16[512,256]{1,0:T(8,128)(2,1)} %get-tuple-element.154.dk_ref, ...), custom_call_target="tpu_custom_call" | custom-call | tf_op jit(solution)/shard_map/pallas_call | solution.py:155
  266.9 4.9 %collective-permute-done.8 = bf16[2,128,1024]{2,1,0:T(8,128)(2,1)S(1)} collective-permute-done((bf16[2,128,1024]{2,1,0:T(8,128)(2,1)S(1)}, bf16[2,128,1024]{2,1,0:T(8,128)(2,1)S(1)}, u32[]{:S(2)}, u32[]{:S(2)}) %collective-permute-start.8) | collective-permute-done | bytes 524320 | tf_op jit(solution)/shard_map/ppermute | solution.py:86
  288.6 9.8 %collective-permute-done.18.refs_2_ = bf16[128,1024]{1,0:T(8,128)(2,1)S(1)} collective-permute-done((bf16[128,1024]{1,0:T(8,128)(2,1)S(1)}, bf16[128,1024]{1,0:T(8,128)(2,1)S(1)}, u32[]{:S(2)}, u32[]{:S(2)}) %collective-permute-start.18) | collective-permute-done | bytes 262176 | tf_op jit(solution)/shard_map/ppermute | solution.py:69
  301.5 7.7 %all-to-all-start.6 = ((bf16[4,32,2944]{2,1,0:T(8,128)(2,1)}), bf16[4,32,2944]{2,1,0:T(8,128)(2,1)S(1)}, u32[]{:S(2)}, u32[]{:S(2)}) async-start(bf16[4,32,2944]{2,1,0:T(8,128)(2,1)} %fusion.3), calls=%async_computation.7 | async-start | bytes 1507328 | tf_op jit(solution)/shard_map/all_to_all | solution.py:59
  309.3 6.9 %reduce-scatter.5.cloned.1.call-done = bf16[1024,1024]{1,0:T(8,128)(2,1)} async-done(((bf16[4096,1024]{1,0:T(8,128)(2,1)}), bf16[1024,1024]{1,0:T(8,128)(2,1)}) %reduce-scatter.5.cloned.1.call-update) | async-done | bytes 2097168 | tf_op jit(solution)/shard_map/reduce_scatter | solution.py:927
  325.5 3.8 %shard_map.225 = (f32[128,4096]{1,0:T(8,128)}, f32[512,1024]{1,0:T(8,128)}) custom-call(s32[1]{0:T(128)} %bitcast.35.core_ref, bf16[2,128,1024]{2,1,0:T(8,128)(2,1)} %get-tuple-element.204.own_ref, bf16[2,128,1024]{2,1,0:T(8,128)(2,1)} %copy-done.12, bf16[512,1024]{1,0:T(8,128)(2,1)} %get-tuple-element.197.down_ref), custom_call_target="tpu_custom_call" | custom-call | tf_op jit(solution)/shard_map/pallas_call | solution.py:155
  (204 shorter events, 83.7 us)
Async XLA Ops:
  7.2 66.5 %all-gather.9.cloned.1.call-start = ((), (), s32[]{:S(2)}) async-start(), calls=%async_computation.13 | async-start | bytes 5242880 | tf_op jit(solution)/shard_map/all_gather | solution.py:805
  9.2 8.7 %collective-permute-start = (bf16[128,2048]{0,1:T(8,128)(2,1)S(1)}, bf16[128,2048]{0,1:T(8,128)(2,1)S(1)}, u32[]{:S(2)}, u32[]{:S(2)}) collective-permute-start(bf16[128,2048]{0,1:T(8,128)(2,1)S(1)} %bitcast.169), channel_id=1, source_target_pairs={{0,4},{4,0},{1,5},{5,1},{2,6},{6,2},{3,7},{7,3},{8,12},{12,8},{9,1... | collective-permute-start | bytes 1572872 | tf_op jit(solution)/shard_map/ppermute | solution.py:77
  11.7 26.6 %all-to-all-start = ((bf16[4,32,3072]{2,1,0:T(8,128)(2,1)}), bf16[4,32,3072]{2,1,0:T(8,128)(2,1)S(1)}, u32[]{:S(2)}, u32[]{:S(2)}) async-start(bf16[4,32,3072]{2,1,0:T(8,128)(2,1)} %pad_maximum_fusion.1), calls=%async_computation | async-start | bytes 1572864 | tf_op jit(solution)/shard_map/all_to_all | solution.py:59
  40.6 33.1 %all-to-all-start.1 = ((bf16[4,128,1024]{2,1,0:T(8,128)(2,1)}), bf16[4,128,1024]{2,1,0:T(8,128)(2,1)S(1)}, u32[]{:S(2)}, u32[]{:S(2)}) async-start(bf16[4,128,1024]{2,1,0:T(8,128)(2,1)} %broadcast_in_dim.55), calls=%async_computation.1 | async-start | bytes 2097152 | tf_op jit(solution)/shard_map/all_to_all | solution.py:59
  44.2 75.3 %all-gather.5.cloned.1.call-start = ((), (), s32[]{:S(2)}) async-start(), calls=%async_computation.9 | async-start | bytes 7077888 | tf_op jit(solution)/shard_map/all_gather | solution.py:856
  73.8 101.4 %all-gather.7.cloned.1.call-start = ((), (), s32[]{:S(2)}) async-start(), calls=%async_computation.10 | async-start | bytes 5242880 | tf_op jit(solution)/shard_map/all_gather | solution.py:869
  74.7 30.9 %all-to-all-start.2 = ((bf16[4,128,1024]{2,1,0:T(8,128)(2,1)}), bf16[4,128,1024]{2,1,0:T(8,128)(2,1)S(1)}, u32[]{:S(2)}, u32[]{:S(2)}) async-start(bf16[4,128,1024]{2,1,0:T(8,128)(2,1)} %broadcast_in_dim.54), calls=%async_computation.2 | async-start | bytes 2097152 | tf_op jit(solution)/shard_map/all_to_all | solution.py:59
  106.6 28.9 %all-to-all-start.3 = ((bf16[4,512,256]{2,1,0:T(8,128)(2,1)}), bf16[4,512,256]{2,1,0:T(8,128)(2,1)S(1)}, u32[]{:S(2)}, u32[]{:S(2)}) async-start(bf16[4,512,256]{2,1,0:T(8,128)(2,1)} %shard_map.213), calls=%async_computation.3 | async-start | bytes 2097152 | tf_op jit(solution)/shard_map/all_to_all | solution.py:59
  110.1 188.5 %reduce-scatter.3.cloned.1.call-start = ((), (), s32[]{:S(2)}) async-start(), calls=%async_computation.11 | async-start | bytes 2621440 | tf_op jit(solution)/shard_map/reduce_scatter | solution.py:905
  155.6 7.3 %collective-permute-start.1 = (bf16[2,160,1024]{2,1,0:T(8,128)(2,1)}, bf16[2,160,1024]{2,1,0:T(8,128)(2,1)S(1)}, u32[]{:S(2)}, u32[]{:S(2)}) collective-permute-start(bf16[2,160,1024]{2,1,0:T(8,128)(2,1)} %get-tuple-element.118.own_ref.own_x.own_g), channel_id=1, source_target_pairs={{0,4},{4,0},{1,5},{5,1},{2,6},{6,2},{3,7},{7,3},{8,12},{12,8},{9,1... | collective-permute-start | bytes 1966088 | tf_op jit(solution)/shard_map/ppermute | solution.py:77
  162.9 4.5 %collective-permute-start.2 = (bf16[4,2,128,1024]{3,2,1,0:T(8,128)(2,1)}, bf16[4,2,128,1024]{3,2,1,0:T(8,128)(2,1)S(1)}, u32[]{:S(2)}, u32[]{:S(2)}) collective-permute-start(bf16[4,2,128,1024]{3,2,1,0:T(8,128)(2,1)} %get-tuple-element.126), channel_id=1, source_target_pairs={{0,4},{4,0},{1,5},{5,1},{2,6},{6,2},{3,7},{7,3},{8,12},{12,8},{9,1... | collective-permute-start | bytes 6291464 | tf_op jit(solution)/shard_map/ppermute | solution.py:77
  171.3 32.9 %all-to-all-start.4 = ((bf16[4,144,1024]{2,1,0:T(8,128)(2,1)}), bf16[4,144,1024]{2,1,0:T(8,128)(2,1)S(1)}, u32[]{:S(2)}, u32[]{:S(2)}) async-start(bf16[4,144,1024]{2,1,0:T(8,128)(2,1)} %get-tuple-element.117), calls=%async_computation.4 | async-start | bytes 2359296 | tf_op jit(solution)/shard_map/all_to_all | solution.py:59
  174.9 141.3 %reduce-scatter.5.cloned.1.call-start = ((), (), s32[]{:S(2)}) async-start(), calls=%async_computation.12 | async-start | bytes 10485760 | tf_op jit(solution)/shard_map/reduce_scatter | solution.py:927
  187.5 9.1 %collective-permute-start.3 = (bf16[2,160,1024]{2,1,0:T(8,128)(2,1)}, bf16[2,160,1024]{2,1,0:T(8,128)(2,1)S(1)}, u32[]{:S(2)}, u32[]{:S(2)}) collective-permute-start(bf16[2,160,1024]{2,1,0:T(8,128)(2,1)} %get-tuple-element.133), channel_id=1, source_target_pairs={{0,4},{4,0},{1,5},{5,1},{2,6},{6,2},{3,7},{7,3},{8,12},{12,8},{9,1... | collective-permute-start | bytes 1966088 | tf_op jit(solution)/shard_map/ppermute | solution.py:77
  207.7 9.0 %collective-permute-start.4 = (bf16[2,40,1024]{2,1,0:T(8,128)(2,1)S(1)}, bf16[2,40,1024]{2,1,0:T(8,128)(2,1)S(1)}, u32[]{:S(2)}, u32[]{:S(2)}) collective-permute-start(bf16[2,40,1024]{2,1,0:T(8,128)(2,1)S(1)} %copy-done.21), channel_id=1, source_target_pairs={{0,1},{1,2},{2,3},{3,0},{4,5},{5,6},{6,7},{7,4},{8,9},{9,10},{10,1... | collective-permute-start | bytes 491528 | tf_op jit(solution)/shard_map/ppermute | solution.py:69
  207.7 14.7 %collective-permute-start.5 = (bf16[2,40,1024]{2,1,0:T(8,128)(2,1)S(1)}, bf16[2,40,1024]{2,1,0:T(8,128)(2,1)S(1)}, u32[]{:S(2)}, u32[]{:S(2)}) collective-permute-start(bf16[2,40,1024]{2,1,0:T(8,128)(2,1)S(1)} %get-tuple-element.140), channel_id=1, source_target_pairs={{0,2},{1,3},{2,0},{3,1},{4,6},{5,7},{6,4},{7,5},{8,10},{9,11},{10,... | collective-permute-start | bytes 491528 | tf_op jit(solution)/shard_map/ppermute | solution.py:69
  209.7 12.7 %collective-permute-start.6 = (bf16[2,40,1024]{2,1,0:T(8,128)(2,1)S(1)}, bf16[2,40,1024]{2,1,0:T(8,128)(2,1)S(1)}, u32[]{:S(2)}, u32[]{:S(2)}) collective-permute-start(bf16[2,40,1024]{2,1,0:T(8,128)(2,1)S(1)} %get-tuple-element.141), channel_id=1, source_target_pairs={{0,3},{1,0},{2,1},{3,2},{4,7},{5,4},{6,5},{7,6},{8,11},{9,8},{10,9... | collective-permute-start | bytes 491528 | tf_op jit(solution)/shard_map/ppermute | solution.py:69
  229.1 12.3 %all-to-all-start.5 = ((bf16[4,128,256]{2,1,0:T(8,128)(2,1)}), bf16[4,128,256]{2,1,0:T(8,128)(2,1)S(1)}, u32[]{:S(2)}, u32[]{:S(2)}) async-start(bf16[4,128,256]{2,1,0:T(8,128)(2,1)} %get-tuple-element.143), calls=%async_computation.5 | async-start | bytes 524288 | tf_op jit(solution)/shard_map/all_to_all | solution.py:59
  241.4 22.8 %collective-permute-start.11 = (bf16[128,1024]{1,0:T(8,128)(2,1)}, bf16[128,1024]{1,0:T(8,128)(2,1)}, u32[]{:S(2)}, u32[]{:S(2)}) collective-permute-start(bf16[128,1024]{1,0:T(8,128)(2,1)} %get-tuple-element.169), channel_id=1, source_target_pairs={{0,3},{1,0},{2,1},{3,2},{4,7},{5,4},{6,5},{7,6},{8,11},{9,8},{10,9... | collective-permute-start | bytes 786440 | tf_op jit(solution)/shard_map/ppermute | solution.py:69
  242.9 24.0 %collective-permute-start.10 = (bf16[128,1024]{1,0:T(8,128)(2,1)}, bf16[128,1024]{1,0:T(8,128)(2,1)}, u32[]{:S(2)}, u32[]{:S(2)}) collective-permute-start(bf16[128,1024]{1,0:T(8,128)(2,1)} %get-tuple-element.167), channel_id=1, source_target_pairs={{0,2},{1,3},{2,0},{3,1},{4,6},{5,7},{6,4},{7,5},{8,10},{9,11},{10,... | collective-permute-start | bytes 786440 | tf_op jit(solution)/shard_map/ppermute | solution.py:69
  243.1 23.9 %collective-permute-start.9 = (bf16[128,1024]{1,0:T(8,128)(2,1)}, bf16[128,1024]{1,0:T(8,128)(2,1)}, u32[]{:S(2)}, u32[]{:S(2)}) collective-permute-start(bf16[128,1024]{1,0:T(8,128)(2,1)} %get-tuple-element.165), channel_id=1, source_target_pairs={{0,1},{1,2},{2,3},{3,0},{4,5},{5,6},{6,7},{7,4},{8,9},{9,10},{10,1... | collective-permute-start | bytes 786440 | tf_op jit(solution)/shard_map/ppermute | solution.py:69
  246.0 25.8 %collective-permute-start.8 = (bf16[2,128,1024]{2,1,0:T(8,128)(2,1)S(1)}, bf16[2,128,1024]{2,1,0:T(8,128)(2,1)S(1)}, u32[]{:S(2)}, u32[]{:S(2)}) collective-permute-start(bf16[2,128,1024]{2,1,0:T(8,128)(2,1)S(1)} %select_convert_fusion), channel_id=1, source_target_pairs={{0,16},{8,24},{16,0},{24,8},{1,17},{9,25},{17,1},{25,9},{2,18},{10... | collective-permute-start | bytes 1572872 | tf_op jit(solution)/shard_map/ppermute | solution.py:86
  272.1 9.2 %collective-permute-start.20 = (bf16[128,1024]{1,0:T(8,128)(2,1)S(1)}, bf16[128,1024]{1,0:T(8,128)(2,1)S(1)}, u32[]{:S(2)}, u32[]{:S(2)}) collective-permute-start(bf16[128,1024]{1,0:T(8,128)(2,1)S(1)} %fusion.5), channel_id=1, source_target_pairs={{0,8},{8,0},{16,24},{24,16},{1,9},{9,1},{17,25},{25,17},{2,10},{10... | collective-permute-start | bytes 786440 | tf_op jit(solution)/shard_map/ppermute | solution.py:86
  274.9 10.8 %collective-permute-start.13 = (bf16[2,144,384]{2,1,0:T(8,128)(2,1)S(1)}, bf16[2,144,384]{2,1,0:T(8,128)(2,1)S(1)}, u32[]{:S(2)}, u32[]{:S(2)}) collective-permute-start(bf16[2,144,384]{2,1,0:T(8,128)(2,1)S(1)} %fusion.6), channel_id=1, source_target_pairs={{0,8},{8,0},{16,24},{24,16},{1,9},{9,1},{17,25},{25,17},{2,10},{10... | collective-permute-start | bytes 663560 | tf_op jit(solution)/shard_map/ppermute | solution.py:86
  276.4 9.2 %collective-permute-start.14 = (bf16[2,144,384]{2,1,0:T(8,128)(2,1)S(1)}, bf16[2,144,384]{2,1,0:T(8,128)(2,1)S(1)}, u32[]{:S(2)}, u32[]{:S(2)}) collective-permute-start(bf16[2,144,384]{2,1,0:T(8,128)(2,1)S(1)} %select_convert_fusion.2), channel_id=1, source_target_pairs={{0,16},{8,24},{16,0},{24,8},{1,17},{9,25},{17,1},{25,9},{2,18},{10... | collective-permute-start | bytes 663560 | tf_op jit(solution)/shard_map/ppermute | solution.py:86
  277.4 11.2 %collective-permute-start.17 = (bf16[128,1024]{1,0:T(8,128)(2,1)S(1)}, bf16[128,1024]{1,0:T(8,128)(2,1)S(1)}, u32[]{:S(2)}, u32[]{:S(2)}) collective-permute-start(bf16[128,1024]{1,0:T(8,128)(2,1)S(1)} %copy-done.31), channel_id=1, source_target_pairs={{0,1},{1,2},{2,3},{3,0},{4,5},{5,6},{6,7},{7,4},{8,9},{9,10},{10,1... | collective-permute-start | bytes 786440 | tf_op jit(solution)/shard_map/ppermute | solution.py:69
  279.2 19.1 %collective-permute-start.18 = (bf16[128,1024]{1,0:T(8,128)(2,1)S(1)}, bf16[128,1024]{1,0:T(8,128)(2,1)S(1)}, u32[]{:S(2)}, u32[]{:S(2)}) collective-permute-start(bf16[128,1024]{1,0:T(8,128)(2,1)S(1)} %copy-done.30), channel_id=1, source_target_pairs={{0,2},{1,3},{2,0},{3,1},{4,6},{5,7},{6,4},{7,5},{8,10},{9,11},{10,... | collective-permute-start | bytes 786440 | tf_op jit(solution)/shard_map/ppermute | solution.py:69
  281.3 17.0 %collective-permute-start.19 = (bf16[128,1024]{1,0:T(8,128)(2,1)S(1)}, bf16[128,1024]{1,0:T(8,128)(2,1)S(1)}, u32[]{:S(2)}, u32[]{:S(2)}) collective-permute-start(bf16[128,1024]{1,0:T(8,128)(2,1)S(1)} %copy-done.29), channel_id=1, source_target_pairs={{0,3},{1,0},{2,1},{3,2},{4,7},{5,4},{6,5},{7,6},{8,11},{9,8},{10,9... | collective-permute-start | bytes 786440 | tf_op jit(solution)/shard_map/ppermute | solution.py:69
  285.8 12.6 %collective-permute-start.16 = (bf16[144,384]{1,0:T(8,128)(2,1)S(1)}, bf16[144,384]{1,0:T(8,128)(2,1)S(1)}, u32[]{:S(2)}, u32[]{:S(2)}) collective-permute-start(bf16[144,384]{1,0:T(8,128)(2,1)S(1)} %fusion.12), channel_id=1, source_target_pairs={{0,8},{8,0},{16,24},{24,16},{1,9},{9,1},{17,25},{25,17},{2,10},{10... | collective-permute-start | bytes 331784 | tf_op jit(solution)/shard_map/ppermute | solution.py:86
  287.4 11.0 %collective-permute-start.15 = (bf16[144,384]{1,0:T(8,128)(2,1)S(1)}, bf16[144,384]{1,0:T(8,128)(2,1)S(1)}, u32[]{:S(2)}, u32[]{:S(2)}) collective-permute-start(bf16[144,384]{1,0:T(8,128)(2,1)S(1)} %fusion.11), channel_id=1, source_target_pairs={{0,16},{8,24},{16,0},{24,8},{1,17},{9,25},{17,1},{25,9},{2,18},{10... | collective-permute-start | bytes 331784 | tf_op jit(solution)/shard_map/ppermute | solution.py:86
  301.5 27.8 %all-to-all-start.6 = ((bf16[4,32,2944]{2,1,0:T(8,128)(2,1)}), bf16[4,32,2944]{2,1,0:T(8,128)(2,1)S(1)}, u32[]{:S(2)}, u32[]{:S(2)}) async-start(bf16[4,32,2944]{2,1,0:T(8,128)(2,1)} %fusion.3), calls=%async_computation.7 | async-start | bytes 1507328 | tf_op jit(solution)/shard_map/all_to_all | solution.py:59
  319.7 5.1 %collective-permute-start.21 = (bf16[2,128,1024]{2,1,0:T(8,128)(2,1)S(1)}, bf16[2,128,1024]{2,1,0:T(8,128)(2,1)S(1)}, u32[]{:S(2)}, u32[]{:S(2)}) collective-permute-start(bf16[2,128,1024]{2,1,0:T(8,128)(2,1)S(1)} %get-tuple-element.203), channel_id=1, source_target_pairs={{0,4},{4,0},{1,5},{5,1},{2,6},{6,2},{3,7},{7,3},{8,12},{12,8},{9,1... | collective-permute-start | bytes 1572872 | tf_op jit(solution)/shard_map/ppermute | solution.py:77
  (35 other events, 148.4 us)
Sparse Core Ops, SparseCore 0:
  9.9 60.0 all-gather.8
  73.9 45.5 all-gather.4
  121.3 52.6 all-gather.6
  176.9 35.1 reduce-scatter.2
  215.3 100.7 reduce-scatter.4
